TPU v7x, 128 devices: a whole 4x4x4 slice. The times are simulated.
128 devices in a mesh: img: 16 (over z, x_lo, core), seq: 4 (over y), col: 2 (over x_hi).
Axes of the slice: x: 4 (x_hi: 2, x_lo: 2; x = x_hi * 2 + x_lo), y: 4, z: 4, core: 2. Of those that a mesh axis runs over, the one named last changes fastest.
Arguments:
- images: bfloat16 [16, 112, 56, 512], P('img', 'seq', 'col'), may hold values from -6 to 6
- out_grad: bfloat16 [16, 112, 56, 512], P('img', 'seq', 'col'), may hold values from -6 to 6
- region_ids: int32 [112, 56], P(None, 'col'), may hold values from 0 to 3
- rel_index: int32 [49, 49], replicated, may hold values from 0 to 168
- qkv_weight: float32 [2, 512, 1536], P(None, ('img', 'col')), may hold values from -0.25 to 0.25
- qkv_first: float32 [2, 512, 1536], P(None, ('img', 'col')), may hold values from -160 to 160
- qkv_second: float32 [2, 512, 1536], P(None, ('img', 'col')), may hold values from 64.22528 to 256.90112
- proj_weight: float32 [2, 512, 512], P(None, ('img', 'col')), may hold values from -0.75 to 0.75
- proj_first: float32 [2, 512, 512], P(None, ('img', 'col')), may hold values from -112 to 112
- proj_second: float32 [2, 512, 512], P(None, ('img', 'col')), may hold values from 25.088 to 100.352
- expand_weight: float32 [2, 512, 2048], P(None, ('img', 'col')), may hold values from -0.25 to 0.25
- expand_first: float32 [2, 512, 2048], P(None, ('img', 'col')), may hold values from -80 to 80
- expand_second: float32 [2, 512, 2048], P(None, ('img', 'col')), may hold values from 16.05632 to 64.22528
- contract_weight: float32 [2, 2048, 512], P(None, ('img', 'col')), may hold values from -0.125 to 0.125
- contract_first: float32 [2, 2048, 512], P(None, ('img', 'col')), may hold values from -160 to 160
- contract_second: float32 [2, 2048, 512], P(None, ('img', 'col')), may hold values from 49.17248 to 196.68993
- small_params: float32 [2, 6144], replicated, may hold values from -1 to 1.5, as said below
- small_first: float32 [2, 6144], replicated, may hold values from -160 to 160
- small_second: float32 [2, 6144], replicated, may hold values from 30.1056 to 301.056
- bias_table: float32 [2, 169, 16], replicated, may hold values from -4 to 4
- table_first: float32 [2, 169, 16], replicated, may hold values from -160 to 160
- table_second: float32 [2, 169, 16], replicated, may hold values from 20.0704 to 200.704
Outputs:
- activations: bfloat16 [16, 112, 56, 512], P('img', 'seq', 'col')
- input_grad: float32 [16, 112, 56, 512], P('img', 'seq', 'col')
- qkv_moment: float32 [2, 512, 1536], P(None, ('img', 'col'))
- qkv_variance: float32 [2, 512, 1536], P(None, ('img', 'col'))
- qkv_updated: float32 [2, 512, 1536], P(None, ('img', 'col'))
- proj_moment: float32 [2, 512, 512], P(None, ('img', 'col'))
- proj_variance: float32 [2, 512, 512], P(None, ('img', 'col'))
- proj_updated: float32 [2, 512, 512], P(None, ('img', 'col'))
- expand_moment: float32 [2, 512, 2048], P(None, ('img', 'col'))
- expand_variance: float32 [2, 512, 2048], P(None, ('img', 'col'))
- expand_updated: float32 [2, 512, 2048], P(None, ('img', 'col'))
- contract_moment: float32 [2, 2048, 512], P(None, ('img', 'col'))
- contract_variance: float32 [2, 2048, 512], P(None, ('img', 'col'))
- contract_updated: float32 [2, 2048, 512], P(None, ('img', 'col'))
- small_moment: float32 [2, 6144], replicated
- small_variance: float32 [2, 6144], replicated
- small_updated: float32 [2, 6144], replicated
- table_moment: float32 [2, 169, 16], replicated
- table_variance: float32 [2, 169, 16], replicated
- table_updated: float32 [2, 169, 16], replicated
- bias_gradient: float32 [2, 512], replicated
Inputs may be any that keep to these rules, and one draw needn't show every extreme that they name: `region_ids`: in the shifted layer a query attends only the keys of its window whose cell carries its region id. `rel_index`: row of the bias table used for query position i and key position j of every window. `small_params`: per layer the norms' gains lie near one and the biases take both signs.
All inputs are finite; a program needn't handle non-finite values.
Results may differ from a plain program's by a relative error of at most 0.035.
Values may be sent and summed in bfloat16 or wider, within the bound.
No kernel may reach another device: no remote copies, remote signals or barrier semaphores. Data moves between devices by JAX's collectives and lax.ppermute only.
A program may use at most 256 MiB of HBM per device.

v0:
```python
import jax
import jax.numpy as jnp
from jax import lax
from jax.sharding import PartitionSpec as P

D = 512
HEADS = 16
HEAD_DIM = 32
WIN = 7
SHIFT = 3
LAYERS = 2
STEP = 10
REL = 169


norm_epsilon = 1e-05
masked_score = -1000000000.0
highest = lax.Precision.HIGHEST


def shifted_2(block, axis, distance):
    devices = range(lax.axis_size(axis))
    route = [((i - distance) % len(devices), i) for i in devices]
    return lax.ppermute(block, axis, route)


def laid_out(pieces, dim):
    pieces = jnp.moveaxis(pieces, 0, dim)
    dims = pieces.shape
    return pieces.reshape(*dims[:dim], dims[dim] * dims[dim + 1], *dims[dim + 2 :])


def gather_packed(arrays, axis, dims):
    vector = jnp.concatenate([a.reshape(-1) for a in arrays])
    lines, at, finished = (lax.all_gather(vector, axis), 0, [])
    for a, dim in zip(arrays, dims):
        pieces = lines[:, at : at + a.size].reshape(-1, *a.shape)
        finished.append(laid_out(pieces, dim))
        at += a.size
    return tuple(finished)


def sent_together(arrays, axis, dim, along):
    both = jnp.concatenate(arrays, axis=along)
    whole, at, finished = (lax.psum_scatter(both, axis, scatter_dimension=dim, tiled=True), 0, [])
    for a in arrays:
        finished.append(lax.slice_in_dim(whole, at, at + a.shape[along], axis=along))
        at += a.shape[along]
    return tuple(finished)


def for_sending(x):
    return jax.tree.map(lambda a: a.astype(jnp.bfloat16) if a.dtype == jnp.float32 else a, x)


def copy_for_each(x, axis):
    peers = lax.axis_size(axis)
    return lax.all_to_all(jnp.broadcast_to(x[None], (peers, *x.shape)), axis, 0, 0, tiled=True)


def of_everyone(x, axis):
    return copy_for_each(x, axis).astype(jnp.float32).sum(axis=0)


def layer_norm(values_in, gain_row, bias_row):
    centred = values_in - jnp.mean(values_in, -1, keepdims=True)
    variance = jnp.mean(centred * centred, -1, keepdims=True)
    return centred * lax.rsqrt(variance + norm_epsilon) * gain_row + bias_row


def gelu_exact(values_in):
    return jax.nn.gelu(values_in, approximate=False)


def split_small(vector):
    pieces = [vector[piece_index * D : (piece_index + 1) * D] for piece_index in range(8)]
    return pieces + [vector[8 * D :]]


def qkv_bias_of(query_bias, value_bias):
    head_rows = query_bias.reshape(HEADS, HEAD_DIM)
    return jnp.stack(
        [head_rows, jnp.zeros_like(head_rows), value_bias.reshape(HEADS, HEAD_DIM)], 1
    ).reshape(3 * D)


def to_windows(field):
    image_count, row_count, col_count, group_count, head_dim = field.shape
    grid = field.reshape(
        image_count, row_count // WIN, WIN, col_count // WIN, WIN, group_count, head_dim
    )
    grid = grid.transpose(0, 1, 3, 5, 2, 4, 6)
    return grid.reshape(
        image_count, row_count // WIN, col_count // WIN, group_count, WIN * WIN, head_dim
    )


def from_windows(grid):
    image_count, win_rows, win_cols, group_count = grid.shape[:4]
    head_dim = grid.shape[5]
    field = grid.reshape(image_count, win_rows, win_cols, group_count, WIN, WIN, head_dim)
    field = field.transpose(0, 1, 4, 2, 5, 3, 6)
    return field.reshape(image_count, win_rows * WIN, win_cols * WIN, group_count * head_dim)


def window_allowed(region_part):
    row_count, col_count = region_part.shape
    region_win = region_part.reshape(row_count // WIN, WIN, col_count // WIN, WIN).transpose(
        0, 2, 1, 3
    )
    region_win = region_win.reshape(row_count // WIN, col_count // WIN, WIN * WIN)
    return region_win[:, :, :, None] == region_win[:, :, None, :]


def roll_cells(field, ahead, exact):
    direction = -1 if ahead else 1
    slab = field[:, :SHIFT] if ahead else field[:, -SHIFT:]
    if exact:
        moved = shifted_2(slab.astype(jnp.bfloat16), "seq", direction).astype(slab.dtype)
    else:
        moved = shifted_2(slab, "seq", direction)
    if ahead:
        field = jnp.concatenate([field[:, SHIFT:], moved], 1)
    else:
        field = jnp.concatenate([moved, field[:, :-SHIFT]], 1)
    slab = field[:, :, :SHIFT] if ahead else field[:, :, -SHIFT:]
    if exact:
        moved = shifted_2(slab.astype(jnp.bfloat16), "col", direction).astype(slab.dtype)
    else:
        moved = shifted_2(slab, "col", direction)
    if ahead:
        return jnp.concatenate([field[:, :, SHIFT:], moved], 2)
    return jnp.concatenate([moved, field[:, :, :-SHIFT]], 2)


def head_bias(table_layer, relative_hot):
    return jnp.einsum("ijr,rh->hij", relative_hot, table_layer, precision=highest)


def score_block(queries, key_rows, bias, allowed, scale):
    scores = (
        jnp.einsum("xabhid,xabhjd->xabhij", queries, key_rows, preferred_element_type=jnp.float32)
        * scale
    )
    scores = scores + bias
    if allowed is not None:
        scores = jnp.where(allowed[None, :, :, None], scores, masked_score)
    return scores


def attend(qkv_field, bias, allowed):
    image_count, row_count, col_count, lanes = qkv_field.shape
    group_count = bias.shape[0]
    head_dim = lanes // (3 * group_count)
    grid = to_windows(
        qkv_field.reshape(image_count, row_count, col_count, 3 * group_count, head_dim)
    )
    grid = grid.reshape(grid.shape[:3] + (group_count, 3) + grid.shape[4:])
    queries, key_rows, value_rows = (grid[:, :, :, :, 0], grid[:, :, :, :, 1], grid[:, :, :, :, 2])
    scores = score_block(queries, key_rows, bias, allowed, head_dim ** (-0.5))
    row_max = jnp.max(scores, -1, keepdims=True)
    log_total = row_max + jnp.log(jnp.sum(jnp.exp(scores - row_max), -1, keepdims=True))
    attn_weights = jnp.exp(scores - log_total).astype(jnp.bfloat16)
    context = jnp.einsum(
        "xabhij,xabhjd->xabhid", attn_weights, value_rows, preferred_element_type=jnp.float32
    )
    return (from_windows(context.astype(jnp.bfloat16)), (queries, key_rows, value_rows, log_total))


def attend_back(kept, bias, allowed, grad_field):
    queries, key_rows, value_rows, log_total = kept
    group_count = bias.shape[0]
    head_dim = queries.shape[-1]
    image_count, row_count, col_count = grad_field.shape[:3]
    grad_context = to_windows(
        grad_field.reshape(image_count, row_count, col_count, group_count, head_dim)
    )
    scale = head_dim ** (-0.5)
    scores = score_block(queries, key_rows, bias, allowed, scale)
    attn_float = jnp.exp(scores - log_total)
    attn_weights = attn_float.astype(jnp.bfloat16)
    grad_value = jnp.einsum(
        "xabhij,xabhid->xabhjd", attn_weights, grad_context, preferred_element_type=jnp.float32
    )
    grad_attn = jnp.einsum(
        "xabhid,xabhjd->xabhij", grad_context, value_rows, preferred_element_type=jnp.float32
    )
    grad_scores = attn_float * (grad_attn - jnp.sum(attn_float * grad_attn, -1, keepdims=True))
    grad_scores = grad_scores.astype(jnp.bfloat16)
    grad_query = (
        jnp.einsum(
            "xabhij,xabhjd->xabhid", grad_scores, key_rows, preferred_element_type=jnp.float32
        )
        * scale
    )
    grad_key = (
        jnp.einsum(
            "xabhij,xabhid->xabhjd", grad_scores, queries, preferred_element_type=jnp.float32
        )
        * scale
    )
    grad_bias = jnp.sum(grad_scores.astype(jnp.float32), axis=(0, 1, 2))
    stacked = jnp.stack([grad_query, grad_key, grad_value], 4).astype(jnp.bfloat16)
    stacked = stacked.reshape(stacked.shape[:3] + (3 * group_count,) + stacked.shape[5:])
    return (from_windows(stacked), grad_bias)


def adamw(weight, first, second, grad, rate, decay):
    first = 0.9 * first + 0.1 * grad
    second = 0.999 * second + 0.001 * grad * grad
    first_hat = first / (1.0 - 0.9**STEP)
    second_hat = second / (1.0 - 0.999**STEP)
    return (
        first,
        second,
        weight - rate * (first_hat / (jnp.sqrt(second_hat) + 1e-08) + decay * weight),
    )


def local(
    images,
    out_grad,
    region_ids,
    rel_index,
    qkv_weight,
    qkv_first,
    qkv_second,
    proj_weight,
    proj_first,
    proj_second,
    expand_weight,
    expand_first,
    expand_second,
    contract_weight,
    contract_first,
    contract_second,
    small_params,
    small_first,
    small_second,
    bias_table,
    table_first,
    table_second,
):
    image_count, band_rows, half_cols, channels = images.shape
    band_index = lax.axis_index("seq")
    token_count = image_count * band_rows * half_cols
    field_shape = images.shape
    relative_hot = (
        rel_index[:, :, None] == jnp.arange(REL, dtype=jnp.int32)[None, None, :]
    ).astype(jnp.float32)
    region_part = lax.dynamic_slice_in_dim(region_ids, band_index * band_rows, band_rows, 0)
    allowed = window_allowed(region_part)
    resid = images.astype(jnp.float32)
    kept_layers = []
    for layer_index in range(LAYERS):
        shifted = layer_index % 2 == 1
        weights_full = gather_packed(
            (
                qkv_weight[layer_index].astype(jnp.bfloat16),
                proj_weight[layer_index].astype(jnp.bfloat16),
                expand_weight[layer_index].astype(jnp.bfloat16),
                contract_weight[layer_index].astype(jnp.bfloat16),
            ),
            ("img", "col"),
            (0, 0, 0, 0),
        )
        wide_qkv, wide_proj, wide_expand, wide_contract = weights_full
        (
            gain_one,
            bias_one,
            query_bias,
            value_bias,
            proj_bias,
            gain_two,
            bias_two,
            out_bias,
            hidden_bias,
        ) = split_small(small_params[layer_index])
        bias_heads = head_bias(bias_table[layer_index], relative_hot)
        mask_layer = allowed if shifted else None
        normed = layer_norm(resid, gain_one, bias_one).astype(jnp.bfloat16)
        if shifted:
            normed = roll_cells(normed, True, False)
        projected = jnp.dot(
            normed.reshape(token_count, channels), wide_qkv, preferred_element_type=jnp.float32
        )
        projected = (projected + qkv_bias_of(query_bias, value_bias)).astype(jnp.bfloat16)
        projected = projected.reshape(image_count, band_rows, half_cols, 3 * channels)
        context, kept_attn = attend(projected, bias_heads, mask_layer)
        if shifted:
            context = roll_cells(context, False, False)
        context = context.reshape(token_count, channels)
        branch = jnp.dot(context, wide_proj, preferred_element_type=jnp.float32) + proj_bias
        resid_mid = resid + branch.reshape(field_shape)
        normed_two = (
            layer_norm(resid_mid, gain_two, bias_two)
            .astype(jnp.bfloat16)
            .reshape(token_count, channels)
        )
        hidden_pre = (
            jnp.dot(normed_two, wide_expand, preferred_element_type=jnp.float32) + hidden_bias
        )
        hidden = gelu_exact(hidden_pre).astype(jnp.bfloat16)
        kept_layers.append(
            (
                resid,
                normed,
                kept_attn,
                context,
                resid_mid,
                normed_two,
                hidden_pre,
                hidden,
                weights_full,
                bias_heads,
            )
        )
        branch = jnp.dot(hidden, wide_contract, preferred_element_type=jnp.float32) + out_bias
        resid = resid_mid + branch.reshape(field_shape)
    activations = resid.astype(jnp.bfloat16)
    grad_resid = out_grad.astype(jnp.float32)
    matrix_grads = [None] * LAYERS
    small_grads = [None] * LAYERS
    table_grads = [None] * LAYERS
    for layer_index in reversed(range(LAYERS)):
        shifted = layer_index % 2 == 1
        (
            resid_in,
            normed,
            kept_attn,
            context,
            resid_mid,
            normed_two,
            hidden_pre,
            hidden,
            weights_full,
            bias_heads,
        ) = kept_layers[layer_index]
        wide_qkv, wide_proj, wide_expand, wide_contract = weights_full
        (
            gain_one,
            bias_one,
            query_bias,
            value_bias,
            proj_bias,
            gain_two,
            bias_two,
            out_bias,
            hidden_bias,
        ) = split_small(small_params[layer_index])
        mask_layer = allowed if shifted else None
        grad_branch = grad_resid.reshape(token_count, channels).astype(jnp.bfloat16)
        grad_contract = jnp.einsum(
            "nf,nd->fd", hidden, grad_branch, preferred_element_type=jnp.float32
        )
        grad_out_bias = jnp.sum(grad_branch.astype(jnp.float32), 0)
        grad_hidden = jnp.einsum(
            "nd,fd->nf", grad_branch, wide_contract, preferred_element_type=jnp.float32
        )
        gelu_back = jax.vjp(gelu_exact, hidden_pre)[1]
        grad_pre = gelu_back(grad_hidden)[0].astype(jnp.bfloat16)
        grad_expand = jnp.einsum(
            "nd,nf->df", normed_two, grad_pre, preferred_element_type=jnp.float32
        )
        grad_hidden_bias = jnp.sum(grad_pre.astype(jnp.float32), 0)
        grad_normed_two = jnp.einsum(
            "nf,df->nd", grad_pre, wide_expand, preferred_element_type=jnp.float32
        )
        norm_back = jax.vjp(layer_norm, resid_mid, gain_two, bias_two)[1]
        grad_mid, grad_gain_two, grad_bias_two = norm_back(grad_normed_two.reshape(field_shape))
        grad_mid = grad_resid + grad_mid
        grad_branch = grad_mid.reshape(token_count, channels).astype(jnp.bfloat16)
        grad_proj = jnp.einsum(
            "nc,nd->cd", context, grad_branch, preferred_element_type=jnp.float32
        )
        grad_proj_bias = jnp.sum(grad_branch.astype(jnp.float32), 0)
        grad_context = jnp.einsum(
            "nd,cd->nc", grad_branch, wide_proj, preferred_element_type=jnp.float32
        )
        grad_context = grad_context.astype(jnp.bfloat16).reshape(field_shape)
        if shifted:
            grad_context = roll_cells(grad_context, True, False)
        grad_projected, grad_bias_heads = attend_back(
            kept_attn, bias_heads, mask_layer, grad_context
        )
        grad_projected = grad_projected.reshape(token_count, 3 * channels)
        grad_qkv = jnp.einsum(
            "nc,ne->ce",
            normed.reshape(token_count, channels),
            grad_projected,
            preferred_element_type=jnp.float32,
        )
        grad_qkv_bias = jnp.sum(grad_projected.astype(jnp.float32), 0).reshape(HEADS, 3, HEAD_DIM)
        grad_normed = jnp.einsum(
            "ne,ce->nc", grad_projected, wide_qkv, preferred_element_type=jnp.float32
        )
        grad_normed = grad_normed.reshape(field_shape)
        if shifted:
            grad_normed = roll_cells(grad_normed, False, True)
        norm_back = jax.vjp(layer_norm, resid_in, gain_one, bias_one)[1]
        grad_input, grad_gain_one, grad_bias_one = norm_back(grad_normed)
        grad_resid = grad_mid + grad_input
        table_part = jnp.einsum("ijr,hij->rh", relative_hot, grad_bias_heads, precision=highest)
        table_grads[layer_index] = table_part
        small_grads[layer_index] = jnp.concatenate(
            [
                grad_gain_one,
                grad_bias_one,
                grad_qkv_bias[:, 0].reshape(D),
                grad_qkv_bias[:, 2].reshape(D),
                grad_proj_bias,
                grad_gain_two,
                grad_bias_two,
                grad_out_bias,
                grad_hidden_bias,
            ]
        )
        layer_grads = (grad_qkv, grad_proj, grad_expand, grad_contract)
        matrix_grads[layer_index] = layer_grads
    stacked_grads = tuple(
        (
            jnp.stack([matrix_grads[layer_index][member] for layer_index in range(LAYERS)])
            for member in range(4)
        )
    )
    stacked_grads = (
        *tuple(
            (
                part.astype(jnp.float32)
                for part in sent_together(
                    (
                        stacked_grads[0].astype(jnp.bfloat16),
                        stacked_grads[1].astype(jnp.bfloat16),
                        stacked_grads[2].astype(jnp.bfloat16),
                    ),
                    ("img", "col"),
                    1,
                    2,
                )
            )
        ),
        lax.psum_scatter(
            stacked_grads[3].astype(jnp.bfloat16), ("img", "col"), scatter_dimension=1, tiled=True
        ).astype(jnp.float32),
    )
    stacked_grads = jax.tree.map(
        lambda part: part.astype(jnp.float32),
        jax.tree.map(lambda part: of_everyone(part, "seq"), for_sending(stacked_grads)),
    )
    grad_small, grad_table = lax.psum(
        (jnp.stack(small_grads), jnp.stack(table_grads)), ("img", "seq", "col")
    )
    qkv_new = adamw(qkv_weight, qkv_first, qkv_second, stacked_grads[0], 0.03, 0.05)
    proj_new = adamw(proj_weight, proj_first, proj_second, stacked_grads[1], 0.1, 0.05)
    expand_new = adamw(expand_weight, expand_first, expand_second, stacked_grads[2], 0.03, 0.05)
    contract_new = adamw(
        contract_weight, contract_first, contract_second, stacked_grads[3], 0.03, 0.05
    )
    small_new = adamw(small_params, small_first, small_second, grad_small, 0.3, 0.0)
    table_new = adamw(bias_table, table_first, table_second, grad_table, 0.6, 0.0)
    bias_gradient = grad_small[:, 7 * D : 8 * D]
    return (
        activations,
        grad_resid,
        qkv_new[0],
        qkv_new[1],
        qkv_new[2],
        proj_new[0],
        proj_new[1],
        proj_new[2],
        expand_new[0],
        expand_new[1],
        expand_new[2],
        contract_new[0],
        contract_new[1],
        contract_new[2],
        small_new[0],
        small_new[1],
        small_new[2],
        table_new[0],
        table_new[1],
        table_new[2],
        bias_gradient,
    )


def solution(mesh):
    in_specs = (
        P("img", "seq", "col", None),
        P("img", "seq", "col", None),
        P(None, "col"),
        P(),
        P(None, ("img", "col"), None),
        P(None, ("img", "col"), None),
        P(None, ("img", "col"), None),
        P(None, ("img", "col"), None),
        P(None, ("img", "col"), None),
        P(None, ("img", "col"), None),
        P(None, ("img", "col"), None),
        P(None, ("img", "col"), None),
        P(None, ("img", "col"), None),
        P(None, ("img", "col"), None),
        P(None, ("img", "col"), None),
        P(None, ("img", "col"), None),
        P(),
        P(),
        P(),
        P(),
        P(),
        P(),
    )
    out_specs = (
        P("img", "seq", "col", None),
        P("img", "seq", "col", None),
        P(None, ("img", "col"), None),
        P(None, ("img", "col"), None),
        P(None, ("img", "col"), None),
        P(None, ("img", "col"), None),
        P(None, ("img", "col"), None),
        P(None, ("img", "col"), None),
        P(None, ("img", "col"), None),
        P(None, ("img", "col"), None),
        P(None, ("img", "col"), None),
        P(None, ("img", "col"), None),
        P(None, ("img", "col"), None),
        P(None, ("img", "col"), None),
        P(),
        P(),
        P(),
        P(),
        P(),
        P(),
        P(),
    )
    return jax.shard_map(local, mesh=mesh, in_specs=in_specs, out_specs=out_specs, check_vma=False)
```

profile of v0, /device:TPU:0, one launch (start us, length us, event | category | flops | bytes accessed | tf_op | source)
XLA Modules:
  0.0 1202.6 jit_solution(2769828204476403358)
XLA Ops:
  21.8 82.2 %all-gather.5.cloned.1.call-done = bf16[3145728]{0:T(1024)(128)(2,1)} async-done(((bf16[98304]{0:T(1024)(128)(2,1)}), bf16[3145728]{0:T(1024)(128)(2,1)}) %all-gather.5.cloned.1.call-update) | async-done | bytes 6291472 | tf_op jit(solution)/shard_map/all_gather | solution.py:35
  104.0 7.1 reshape.846
  118.6 11.6 reshape_reshape_reshape.9
  130.2 17.3 %copy.184 = bf16[1,4,4,48,7,7,32]{6,2,5,4,3,1,0:T(4,128)(2,1)S(1)} copy(bf16[1,4,4,48,7,7,32]{6,3,5,2,4,1,0:T(8,128)(2,1)} %bitcast.270) | data formatting | bytes 4816896 | tf_op jit(solution)/shard_map/transpose | solution.py:92
  147.5 4.9 fusion.133
  152.4 6.9 copy.235
  159.3 6.9 copy.234
  166.2 7.1 copy.233
  184.2 5.3 copy.190
  215.7 18.8 %multiply_convert_fusion.3 = (bf16[784,2048]{1,0:T(8,128)(2,1)S(1)}, f32[784,2048]{1,0:T(8,128)}, f32[784,2048]{1,0:T(8,128)}) fusion(f32[2048]{0:T(1024)S(1)} %bitcast.305, bf16[784,512]{1,0:T(8,128)(2,1)S(1)} %reshape.822, bf16[512,2048]{1,0:T(8,128)(2,1)} %reshape_reshape.48), kind=kOutput, calls=%fused_computation.44 | convolution fusion | flops 1750138880 | bytes 18964480 | tf_op jit(solution)/shard_map/dot_general | solution.py:301
  248.1 7.1 reshape.847
  274.5 11.5 reshape_reshape_reshape.10
  286.1 17.3 %copy.196 = bf16[1,4,4,48,7,7,32]{6,2,5,4,3,1,0:T(4,128)(2,1)S(1)} copy(bf16[1,4,4,48,7,7,32]{6,3,5,2,4,1,0:T(8,128)(2,1)} %bitcast.271) | data formatting | bytes 4816896 | tf_op jit(solution)/shard_map/transpose | solution.py:92
  303.4 4.9 fusion.132
  308.3 6.9 copy.238
  315.1 6.9 copy.237
  322.1 6.9 copy.236
  339.1 5.7 copy.202
  349.4 5.5 reshape.830
  395.8 17.5 %multiply_convert_fusion.2 = (bf16[784,2048]{1,0:T(8,128)(2,1)}, f32[784,2048]{1,0:T(8,128)S(1)}, f32[784,2048]{1,0:T(8,128)S(1)}) fusion(f32[2048]{0:T(1024)S(1)} %bitcast.307, bf16[784,512]{1,0:T(8,128)(2,1)S(1)} %reshape.833, bf16[512,2048]{1,0:T(8,128)(2,1)} %reshape_reshape.53), kind=kOutput, calls=%fused_computation.31 | convolution fusion | flops 1750138880 | bytes 18964480 | tf_op jit(solution)/shard_map/dot_general | solution.py:301
  413.3 4.8 convert_reduce_fusion.4
  431.0 5.7 fusion.35
  456.5 5.4 collective-permute-done.5
  469.0 5.4 copy.205
  474.4 5.9 convert_bitcast_fusion.1
  493.9 18.2 %copy.210 = bf16[1,4,4,16,3,49,32]{6,2,5,4,3,1,0:T(4,128)(2,1)} copy(bf16[1,4,4,16,3,49,32]{5,6,3,2,1,4,0:T(8,128)(2,1)} %pad_maximum_fusion) | data formatting | bytes 4816896 | tf_op jit(solution)/shard_map/stack | solution.py:203
  512.1 9.2 copy.211
  521.4 11.7 reshape.838
  533.1 13.6 %reshape_reshape.57 = bf16[784,1536]{1,0:T(8,128)(2,1)} reshape(bf16[1,4,7,4,7,48,32]{6,5,4,3,2,1,0:T(8,128)(2,1)} %copy.211) | data formatting | bytes 4816896 | tf_op jit(solution)/shard_map/reshape;reshape | solution.py:386
  546.7 8.7 convert_reduce_fusion
  568.2 5.4 collective-permute-done.7
  580.5 5.8 fusion.34
  586.3 7.7 convert_reduce_fusion.5
  612.4 5.5 copy.213
  617.9 9.6 multiply_reduce_fusion
  630.0 7.1 convert_reduce_fusion.3
  648.0 18.3 %copy.218 = bf16[1,4,4,16,3,49,32]{6,2,5,4,3,1,0:T(4,128)(2,1)} copy(bf16[1,4,4,16,3,49,32]{5,6,3,2,1,4,0:T(8,128)(2,1)} %pad_maximum_fusion.1) | data formatting | bytes 4816896 | tf_op jit(solution)/shard_map/stack | solution.py:203
  666.3 9.3 copy.219
  675.6 12.2 %reshape_reshape.56 = bf16[784,1536]{1,0:T(8,128)(2,1)S(1)} reshape(bf16[1,4,7,4,7,48,32]{6,5,4,3,2,1,0:T(8,128)(2,1)} %copy.219) | data formatting | bytes 4816896 | tf_op jit(solution)/shard_map/reshape;reshape | solution.py:386
  687.8 5.4 fusion.141
  700.5 8.9 convert_reduce_fusion.1
  723.5 7.5 maximum_maximum_fusion
  736.5 52.7 %reduce-scatter.5.cloned.1.call-done = bf16[2,64,512]{2,1,0:T(8,128)(2,1)} async-done(((bf16[2,2048,512]{2,1,0:T(8,128)(2,1)}), bf16[2,64,512]{2,1,0:T(8,128)(2,1)}) %reduce-scatter.5.cloned.1.call-update) | async-done | bytes 131088 | tf_op jit(solution)/shard_map/reduce_scatter | solution.py:442
  795.3 134.8 %all-reduce.3.cloned.1.call-done = (f32[2,6144]{1,0:T(2,128)}, f32[2,169,16]{1,2,0:T(8,128)}) async-done(((f32[2,6144]{1,0:T(2,128)}, f32[2,169,16]{1,2,0:T(8,128)}), (f32[2,6144]{1,0:T(2,128)}, f32[2,169,16]{1,2,0:T(8,128)})) %all-reduce.3.cloned.1.call-update) | async-done | bytes 70800 | tf_op jit(solution)/shard_map/psum | solution.py:450
  934.4 219.2 %reduce-scatter.3.cloned.1.call-done = bf16[2,16,4096]{2,1,0:T(8,128)(2,1)} async-done(((bf16[2,512,4096]{2,1,0:T(8,128)(2,1)}), bf16[2,16,4096]{2,1,0:T(8,128)(2,1)}) %reduce-scatter.3.cloned.1.call-update) | async-done | bytes 262160 | tf_op jit(solution)/shard_map/reduce_scatter | solution.py:45
  1155.1 9.5 all-to-all-start.1
  1175.6 6.6 all-to-all-done
  1187.5 7.1 all-to-all-done.2
  (543 shorter events, 306.6 us)
Async XLA Ops:
  7.2 14.2 %copy-start = (s32[112,28]{0,1:T(8,128)S(1)}, s32[112,28]{0,1:T(8,128)}, u32[]{:S(2)}) copy-start(s32[112,28]{0,1:T(8,128)} %param.24) | copy-start | bytes 37636
  7.3 96.7 %all-gather.5.cloned.1.call-start = ((), (), s32[]{:S(2)}) async-start(), calls=%async_computation.8 | async-start | bytes 6488064 | tf_op jit(solution)/shard_map/all_gather | solution.py:35
  12.1 236.0 %all-gather.7.cloned.1.call-start = ((), (), s32[]{:S(2)}) async-start(), calls=%async_computation.9 | async-start | bytes 6488064 | tf_op jit(solution)/shard_map/all_gather | solution.py:35
  13.0 776.3 %reduce-scatter.5.cloned.1.call-start = ((), (), s32[]{:S(2)}) async-start(), calls=%async_computation.7 | async-start | bytes 4325376 | tf_op jit(solution)/shard_map/reduce_scatter | solution.py:442
  13.7 202.0 %copy-start.121 = (f32[1,2048]{1,0:T(1,128)}, f32[1,2048]{1,0:T(1,128)S(1)}, u32[]{:S(2)}) copy-start(f32[1,2048]{1,0:T(1,128)S(1)} %get-tuple-element.224) | copy-start | bytes 24580
  14.3 189.4 %copy-start.106 = (f32[1,512]{1,0:T(1,128)}, f32[1,512]{1,0:T(1,128)S(1)}, u32[]{:S(2)}) copy-start(f32[1,512]{1,0:T(1,128)S(1)} %get-tuple-element.217) | copy-start | bytes 6148
  14.3 227.8 %copy-start.100 = (f32[1,512]{1,0:T(1,128)}, f32[1,512]{1,0:T(1,128)S(1)}, u32[]{:S(2)}) copy-start(f32[1,512]{1,0:T(1,128)S(1)} %get-tuple-element.214) | copy-start | bytes 6148
  19.0 85.0 %copy-start.76 = (f32[28,28]{1,0:T(8,128)}, f32[28,28]{1,0:T(8,128)S(1)}, u32[]{:S(2)}) copy-start(f32[28,28]{1,0:T(8,128)S(1)} %fusion.109) | copy-start | bytes 9412
  21.4 159.0 %copy-start.12 = (f32[16,49,49]{1,2,0:T(8,128)}, f32[16,49,49]{1,2,0:T(8,128)S(1)}, u32[]{:S(2)}) copy-start(f32[16,49,49]{1,2,0:T(8,128)S(1)} %copy.187) | copy-start | bytes 460996
  215.7 20.4 %copy-start.41 = (bf16[2048,512]{1,0:T(8,128)(2,1)S(1)}, bf16[2048,512]{1,0:T(8,128)(2,1)}, u32[]{:S(2)}) copy-start(bf16[2048,512]{1,0:T(8,128)(2,1)} %reshape_reshape.49) | copy-start | bytes 6291460
  241.6 150.5 %copy-start.4 = (f32[1,28,28,512]{3,2,1,0:T(8,128)}, f32[1,28,28,512]{3,2,1,0:T(8,128)S(1)}, u32[]{:S(2)}) copy-start(f32[1,28,28,512]{3,2,1,0:T(8,128)S(1)} %get-tuple-element.182) | copy-start | bytes 4816900
  243.1 15.3 %collective-permute-start = (bf16[1,3,28,512]{3,2,1,0:T(8,128)(2,1)}, bf16[1,3,28,512]{3,2,1,0:T(8,128)(2,1)}, u32[]{:S(2)}, u32[]{:S(2)}) collective-permute-start(bf16[1,3,28,512]{3,2,1,0:T(8,128)(2,1)} %slice.330), channel_id=1, source_target_pairs={{2,0},{4,2},{6,4},{0,6},{3,1},{5,3},{7,5},{1,7},{10,8},{12,10},{14... | collective-permute-start | bytes 258056 | tf_op jit(solution)/shard_map/ppermute | solution.py:24
  259.4 7.3 collective-permute-start.1
  355.8 5.8 collective-permute-start.2
  362.4 19.8 %collective-permute-start.3 = (bf16[1,28,3,512]{3,2,1,0:T(4,128)(2,1)}, bf16[1,28,3,512]{3,2,1,0:T(4,128)(2,1)}, u32[]{:S(2)}, u32[]{:S(2)}) collective-permute-start(bf16[1,28,3,512]{3,2,1,0:T(4,128)(2,1)} %pad_maximum_fusion.12), channel_id=1, source_target_pairs={{1,0},{0,1},{3,2},{2,3},{5,4},{4,5},{7,6},{6,7},{9,8},{8,9},{11,10... | collective-permute-start | bytes 258056 | tf_op jit(solution)/shard_map/ppermute | solution.py:24
  395.8 17.5 %copy-start.43 = (bf16[2048,512]{1,0:T(8,128)(2,1)S(1)}, bf16[2048,512]{1,0:T(8,128)(2,1)}, u32[]{:S(2)}) copy-start(bf16[2048,512]{1,0:T(8,128)(2,1)} %reshape_reshape.54) | copy-start | bytes 6291460
  395.8 17.5 %copy-start.57 = (bf16[784,512]{1,0:T(8,128)(2,1)S(1)}, bf16[784,512]{1,0:T(8,128)(2,1)}, u32[]{:S(2)}) copy-start(bf16[784,512]{1,0:T(8,128)(2,1)} %convert_element_type.259) | copy-start | bytes 2408452
  450.9 4.7 collective-permute-start.4
  455.6 6.4 collective-permute-start.5
  559.3 6.9 collective-permute-start.6
  567.2 6.4 collective-permute-start.7
  629.9 300.1 %all-reduce.3.cloned.1.call-start = ((), (), s32[]{:S(2)}) async-start(), calls=%async_computation.10 | async-start | bytes 163840 | tf_op jit(solution)/shard_map/psum | solution.py:450
  700.5 12.0 copy-start.116
  723.5 430.1 %reduce-scatter.3.cloned.1.call-start = ((), (), s32[]{:S(2)}) async-start(), calls=%async_computation.6 | async-start | bytes 8650752 | tf_op jit(solution)/shard_map/reduce_scatter | solution.py:45
  733.6 196.5 %copy-start.88 = (f32[2,6144]{1,0:T(2,128)S(1)}, f32[2,6144]{1,0:T(2,128)}, u32[]{:S(2)}) copy-start(f32[2,6144]{1,0:T(2,128)} %param.38) | copy-start | bytes 147460
  733.6 196.4 %copy-start.104 = (f32[2,6144]{1,0:T(2,128)S(1)}, f32[2,6144]{1,0:T(2,128)}, u32[]{:S(2)}) copy-start(f32[2,6144]{1,0:T(2,128)} %param.40) | copy-start | bytes 147460
  733.6 196.4 %copy-start.105 = (f32[2,6144]{1,0:T(2,128)S(1)}, f32[2,6144]{1,0:T(2,128)}, u32[]{:S(2)}) copy-start(f32[2,6144]{1,0:T(2,128)} %param.39) | copy-start | bytes 147460
  733.6 199.3 %copy-start.109 = (f32[2,169,16]{1,2,0:T(8,128)S(1)}, f32[2,169,16]{1,2,0:T(8,128)}, u32[]{:S(2)}) copy-start(f32[2,169,16]{1,2,0:T(8,128)} %param.41) | copy-start | bytes 64900
  733.7 199.3 %copy-start.110 = (f32[2,169,16]{1,2,0:T(8,128)S(1)}, f32[2,169,16]{1,2,0:T(8,128)}, u32[]{:S(2)}) copy-start(f32[2,169,16]{1,2,0:T(8,128)} %param.43) | copy-start | bytes 64900
  733.7 199.3 %copy-start.111 = (f32[2,169,16]{1,2,0:T(8,128)S(1)}, f32[2,169,16]{1,2,0:T(8,128)}, u32[]{:S(2)}) copy-start(f32[2,169,16]{1,2,0:T(8,128)} %param.42) | copy-start | bytes 64900
  733.7 430.9 %copy-start.51 = (f32[2,64,512]{2,1,0:T(8,128)S(1)}, f32[2,64,512]{2,1,0:T(8,128)}, u32[]{:S(2)}) copy-start(f32[2,64,512]{2,1,0:T(8,128)} %param.35) | copy-start | bytes 786436
  733.7 430.9 %copy-start.82 = (f32[2,64,512]{2,1,0:T(8,128)S(1)}, f32[2,64,512]{2,1,0:T(8,128)}, u32[]{:S(2)}) copy-start(f32[2,64,512]{2,1,0:T(8,128)} %param.37) | copy-start | bytes 786436
  733.7 430.9 %copy-start.83 = (f32[2,64,512]{2,1,0:T(8,128)S(1)}, f32[2,64,512]{2,1,0:T(8,128)}, u32[]{:S(2)}) copy-start(f32[2,64,512]{2,1,0:T(8,128)} %param.36) | copy-start | bytes 786436
  791.0 383.8 %copy-start.86 = (f32[2,16,512]{2,1,0:T(8,128)S(1)}, f32[2,16,512]{2,1,0:T(8,128)}, u32[]{:S(2)}) copy-start(f32[2,16,512]{2,1,0:T(8,128)} %param.29) | copy-start | bytes 196612
  791.0 383.8 %copy-start.98 = (f32[2,16,512]{2,1,0:T(8,128)S(1)}, f32[2,16,512]{2,1,0:T(8,128)}, u32[]{:S(2)}) copy-start(f32[2,16,512]{2,1,0:T(8,128)} %param.31) | copy-start | bytes 196612
  791.0 383.8 %copy-start.99 = (f32[2,16,512]{2,1,0:T(8,128)S(1)}, f32[2,16,512]{2,1,0:T(8,128)}, u32[]{:S(2)}) copy-start(f32[2,16,512]{2,1,0:T(8,128)} %param.30) | copy-start | bytes 196612
  791.0 143.4 %all-to-all-start.3 = ((bf16[4,2,64,512]{3,2,1,0:T(8,128)(2,1)}), bf16[4,2,64,512]{3,2,1,0:T(8,128)(2,1)S(1)}, u32[]{:S(2)}, u32[]{:S(2)}) async-start(bf16[4,2,64,512]{3,2,1,0:T(8,128)(2,1)} %broadcast_in_dim.53), calls=%async_computation.5 | async-start | bytes 1048576 | tf_op jit(solution)/shard_map/all_to_all | solution.py:58
  1153.6 28.5 %slice-start.7 = ((bf16[2,16,4096]{2,1,0:T(8,128)(2,1)}), bf16[2,16,2048]{2,1,0:T(8,128)(2,1)S(1)}, s32[]{:S(2)}) async-start(bf16[2,16,4096]{2,1,0:T(8,128)(2,1)} %reduce-scatter.3.cloned.1.call-done), calls=%async_computation.18 | async-start | bytes 262144 | tf_op jit(solution)/shard_map/slice | solution.py:47
  1155.1 15.5 %all-to-all-start.1 = ((bf16[4,2,16,512]{3,2,1,0:T(8,128)(2,1)}), bf16[4,2,16,512]{3,2,1,0:T(8,128)(2,1)S(1)}, u32[]{:S(2)}, u32[]{:S(2)}) async-start(bf16[4,2,16,512]{3,2,1,0:T(8,128)(2,1)} %broadcast_in_dim.51), calls=%async_computation.2 | async-start | bytes 262144 | tf_op jit(solution)/shard_map/all_to_all | solution.py:58
  1164.6 22.0 %copy-start.62 = (f32[2,16,1536]{2,1,0:T(8,128)S(1)}, f32[2,16,1536]{2,1,0:T(8,128)}, u32[]{:S(2)}) copy-start(f32[2,16,1536]{2,1,0:T(8,128)} %param.26) | copy-start | bytes 589828
  1164.6 22.0 %copy-start.89 = (f32[2,16,1536]{2,1,0:T(8,128)S(1)}, f32[2,16,1536]{2,1,0:T(8,128)}, u32[]{:S(2)}) copy-start(f32[2,16,1536]{2,1,0:T(8,128)} %param.28) | copy-start | bytes 589828
  1164.6 22.0 %copy-start.90 = (f32[2,16,1536]{2,1,0:T(8,128)S(1)}, f32[2,16,1536]{2,1,0:T(8,128)}, u32[]{:S(2)}) copy-start(f32[2,16,1536]{2,1,0:T(8,128)} %param.27) | copy-start | bytes 589828
  1166.5 28.1 %copy-start.52 = (f32[2,16,2048]{2,1,0:T(8,128)S(1)}, f32[2,16,2048]{2,1,0:T(8,128)}, u32[]{:S(2)}) copy-start(f32[2,16,2048]{2,1,0:T(8,128)} %param.32) | copy-start | bytes 786436
  1166.6 28.1 %copy-start.84 = (f32[2,16,2048]{2,1,0:T(8,128)S(1)}, f32[2,16,2048]{2,1,0:T(8,128)}, u32[]{:S(2)}) copy-start(f32[2,16,2048]{2,1,0:T(8,128)} %param.34) | copy-start | bytes 786436
  1166.6 28.1 %copy-start.85 = (f32[2,16,2048]{2,1,0:T(8,128)S(1)}, f32[2,16,2048]{2,1,0:T(8,128)}, u32[]{:S(2)}) copy-start(f32[2,16,2048]{2,1,0:T(8,128)} %param.33) | copy-start | bytes 786436
  1171.3 10.8 all-to-all-start
  1174.9 20.8 %copy-start.1 = (s32[112,28]{0,1:T(8,128)S(1)}, s32[112,28]{0,1:T(8,128)}, u32[]{:S(2)}) copy-start(s32[112,28]{0,1:T(8,128)} %param.24) | copy-start | bytes 37636
  1183.0 11.5 all-to-all-start.2
  (113 other events, 547.0 us)
Sparse Core Ops, SparseCore 0:
  12.2 91.7 all-gather.4
  106.2 91.1 all-gather.6
  630.0 159.1 reduce-scatter.4
  795.3 134.7 all-reduce.2
  932.4 221.1 reduce-scatter.2
where the time goes:
time: 1220 us; the launch traced here: 1200 us
  waiting for transfers between devices  525 us (43%)
  local copies, waits for them, and re-layouts  363 us (30%)
  matrix products  162 us (13%)
  other arithmetic  105 us (9%)
  starting transfers between devices  32 us (3%)
  between operations  16.3 us (1%)
    reduce_scatter x1, waiting for transfers between devices, sent_together(): lax.psum_scatter(both, axis, scatter_dimension=dim, tiled=True)  219 us
    psum x1, waiting for transfers between devices, local(): lax.psum((jnp.stack(small_grads), jnp.stack(table_grads)), ('img', 'seq',...  135 us
    all_gather x2, waiting for transfers between devices, gather_packed(): lines, at, finished = (lax.all_gather(vector, axis), 0, [])  82.2 us
    unnamed x311, local copies, waits for them, and re-layouts  58.4 us
    reduce_scatter x1, waiting for transfers between devices, local(): lax.psum_scatter(stacked_grads[3].astype(jnp.bfloat16), ('img', 'col'), s...  52.7 us
    transpose x3, local copies, waits for them, and re-layouts, to_windows(): grid = grid.transpose(0, 1, 3, 5, 2, 4, 6)  36.8 us
    another operation x2, local copies, waits for them, and re-layouts, attend_back(): jnp.stack([grad_query, grad_key, grad_value], 4).astype(jnp.bfloat16)  36.5 us
    dot_general x2, matrix products, local(): jnp.dot(normed_two, wide_expand, preferred_element_type=jnp.float32)  36.2 us
  transfers between devices with their start and end apart: 17, of which 12 were waited for; matrix products, arithmetic and copies ran while one was open for 25% of the time, Pallas kernels for 0%

commit v1 on v0

v1 whole, which is shorter than its diff:
```python
import functools
import math

import jax
import jax.numpy as jnp
import numpy as np
from jax import lax
from jax.experimental import pallas as pl
from jax.experimental.pallas import tpu as pltpu
from jax.sharding import PartitionSpec as P

D = 512
HEADS = 16
HEAD_DIM = 32
WIN = 7
SHIFT = 3
LAYERS = 2
STEP = 10
REL = 169
SIDE = 28
CELLS = SIDE * SIDE
AREA = WIN * WIN
SLOT = 64
PADDED = 16 * SLOT
PAIRS = 8
GROUPS = 4
SLAB = 96
CORNER = 16
HALO = 2 * SLAB + CORNER
HIDDEN = 4 * D

BF = jnp.bfloat16
F32 = jnp.float32
epsilon = 1e-05
log2e = math.log2(math.e)
masked_score = -1000000000.0 * log2e
padded_score = -1e30
highest = lax.Precision.HIGHEST
VMEM_BYTES = 58 * 2**20


def padded_row(r, c):
    return ((r // WIN) * 4 + c // WIN) * SLOT + (r % WIN) * WIN + c % WIN


def ahead_source(r, c):
    r, c = r + SHIFT, c + SHIFT
    if r < SIDE and c < SIDE:
        return r * SIDE + c
    if c < SIDE:
        return CELLS + (r - SIDE) * SIDE + c
    if r < SIDE:
        return CELLS + SLAB + r * SHIFT + c - SIDE
    return CELLS + 2 * SLAB + (r - SIDE) * SHIFT + c - SIDE


def back_source(r, c):
    if r >= SHIFT and c >= SHIFT:
        return padded_row(r - SHIFT, c - SHIFT)
    if c >= SHIFT:
        return PADDED + r * SIDE + c - SHIFT
    if r >= SHIFT:
        return PADDED + SLAB + (r - SHIFT) * SHIFT + c
    return PADDED + 2 * SLAB + r * SHIFT + c


def placements():
    plain = np.zeros((PADDED, CELLS), np.float32)
    ahead = np.zeros((PADDED, CELLS + HALO), np.float32)
    back = np.zeros((CELLS, PADDED + HALO), np.float32)
    take_first = np.zeros((HALO, CELLS), np.float32)
    take_last = np.zeros((HALO, PADDED), np.float32)
    for r in range(SIDE):
        for c in range(SIDE):
            plain[padded_row(r, c), r * SIDE + c] = 1
            ahead[padded_row(r, c), ahead_source(r, c)] = 1
            back[r * SIDE + c, back_source(r, c)] = 1
    edge = SIDE - SHIFT
    for a in range(SHIFT):
        for b in range(SIDE):
            take_first[a * SIDE + b, a * SIDE + b] = 1
            take_first[SLAB + b * SHIFT + a, b * SIDE + a] = 1
            take_last[a * SIDE + b, padded_row(edge + a, b)] = 1
            take_last[SLAB + b * SHIFT + a, padded_row(b, edge + a)] = 1
        for b in range(SHIFT):
            take_first[2 * SLAB + a * SHIFT + b, a * SIDE + b] = 1
            take_last[2 * SLAB + a * SHIFT + b, padded_row(edge + a, edge + b)] = 1
    return (plain, plain.T.copy(), ahead, back, take_first, take_last)


def column_orders():
    heads = np.zeros((384, 384), np.float32)
    units = np.zeros((512, 512), np.float32)
    for n in range(4):
        for part in range(3):
            for d in range(HEAD_DIM):
                heads[n * 96 + part * 32 + d, part * 128 + n * 32 + d] = 1
    for r in range(8):
        for b in range(4):
            for i in range(16):
                units[r * 64 + b * 16 + i, b * 128 + r * 16 + i] = 1
    return heads, units


def dot(a, b):
    return lax.dot_general(a, b, (((1,), (0,)), ((), ())), preferred_element_type=F32)


def dot_nt(a, b):
    return lax.dot_general(a, b, (((1,), (1,)), ((), ())), preferred_element_type=F32)


def dot_tn(a, b):
    return lax.dot_general(a, b, (((0,), (0,)), ((), ())), preferred_element_type=F32)


def normalized(x):
    centred = x - jnp.mean(x, -1, keepdims=True)
    inverse = lax.rsqrt(jnp.mean(centred * centred, -1, keepdims=True) + epsilon)
    return centred * inverse, inverse


def norm_back(grad, x, gain):
    hat, inverse = normalized(x)
    grad_hat = grad * gain
    grad_x = inverse * (
        grad_hat
        - jnp.mean(grad_hat, -1, keepdims=True)
        - hat * jnp.mean(grad_hat * hat, -1, keepdims=True)
    )
    return grad_x, jnp.sum(grad * hat, 0, keepdims=True), jnp.sum(grad, 0, keepdims=True)


def gelu_both(u):
    a = jnp.abs(u)
    t = 1.0 / (1.0 + (0.3275911 * 0.5**0.5) * a)
    e = jnp.exp2((-0.5 * log2e) * u * u)
    poly = t * (
        0.5 * 0.254829592
        + t * (0.5 * -0.284496736 + t * (0.5 * 1.421413741 + t * (0.5 * -1.453152027 + t * (0.5 * 1.061405429))))
    )
    tail = poly * e
    phi = jnp.where(u >= 0, 1.0 - tail, tail)
    return u * phi, phi + u * e * (1.0 / math.sqrt(2 * math.pi))


def head_rows(pair):
    lane = lax.broadcasted_iota(jnp.int32, pair.shape, 1) % 128 // HEAD_DIM
    zero = jnp.zeros_like(pair)
    return jnp.concatenate([jnp.where(lane == h, pair, zero) for h in range(4)], 0)


def head_fold(rows):
    lane = lax.broadcasted_iota(jnp.int32, (SLOT, 256), 1) % 128 // HEAD_DIM
    out = rows[:SLOT]
    for h in range(1, 4):
        out = jnp.where(lane == h, rows[h * SLOT : (h + 1) * SLOT], out)
    return out


def side_by_side(ref, start, lane):
    return jnp.concatenate(
        [ref[pl.ds(start, SLOT), lane : lane + 128], ref[pl.ds(start + SLOT, SLOT), lane : lane + 128]], 1
    )


def block_diagonal(pair):
    lane = lax.broadcasted_iota(jnp.int32, pair.shape, 1)
    zero = jnp.zeros_like(pair)
    return jnp.concatenate([jnp.where(lane < 128, pair, zero), jnp.where(lane >= 128, pair, zero)], 0)


def store_diagonal(ref, start, lane, rows):
    ref[pl.ds(start, SLOT), lane : lane + 128] = rows[:SLOT, :128].astype(ref.dtype)
    ref[pl.ds(start + SLOT, SLOT), lane : lane + 128] = rows[SLOT:, 128:].astype(ref.dtype)


def call(body, outs, args, scratch=(), pieces=(), place=None, us=1, after=(), blocks=None):
    shapes = [jax.ShapeDtypeStruct(s, d) for s, d in outs]
    lead = [] if place is None else [place]
    anywhere = pl.BlockSpec(memory_space=pl.ANY)
    specs = [anywhere] * len(after)
    specs += [pl.BlockSpec(memory_space=pltpu.SMEM)] * len(lead)
    specs += [anywhere] * len(pieces)
    for i in range(len(args)):
        if blocks and i in blocks:
            shape, index = blocks[i]
            specs.append(pl.BlockSpec(shape, lambda _, at=index: at, memory_space=pltpu.VMEM))
        else:
            specs.append(pl.BlockSpec(memory_space=pltpu.VMEM))

    def whole(*refs):
        body(*refs[len(after) :])

    return pl.pallas_call(
        whole,
        grid=(1,) if blocks else (),
        out_shape=shapes,
        in_specs=specs,
        out_specs=[pl.BlockSpec(memory_space=pltpu.VMEM)] * len(shapes),
        scratch_shapes=list(scratch),
        compiler_params=pltpu.CompilerParams(vmem_limit_bytes=VMEM_BYTES),
        cost_estimate=pl.CostEstimate(flops=us * 10**9, bytes_accessed=us * 10**6, transcendentals=0),
    )(*after, *lead, *pieces, *args)


def owner_of(z, x, core):
    return z * 8 + (x // 2) * 4 + core * 2 + x % 2


def assembly(coords_ref, sets, w_ref, sems):
    z, x, core = coords_ref[0], coords_ref[1], coords_ref[2]
    copies = []
    for pieces, heavy_z, taken, first in sets:
        for k, piece in enumerate(pieces):
            for i in range(4):
                in_z, in_x = (k % 4, i) if heavy_z else (i, k % 4)
                owner = owner_of(lax.rem(z + in_z, 4), lax.bitwise_xor(x, in_x), core if k < 4 else 1 - core)
                source = piece.at[i, pl.ds(taken[0], taken[1])]
                target = w_ref.at[pl.ds(first, taken[1]), owner]
                copies.append(pltpu.make_async_copy(source, target, sems.at[len(copies)]))
    for c in copies:
        c.start()
    return copies


def block(ref, b):
    return ref[b].reshape(D, D)


def block_lanes(ref, b, lanes):
    return ref[b, :, :, lanes].reshape(D, lanes.stop - lanes.start)


def block_rows(ref, b, half):
    return ref[b, half * 16 : half * 16 + 16].reshape(256, D)


def store_grad(place_ref, keep_ref, send_ref, b, half, rows):
    first = place_ref[2] == 0
    rows = rows.astype(BF)
    for zz in range(2):
        for x in range(4):
            base = (zz * 8 + (x // 2) * 4 + x % 2) * 16
            one, two = rows[base : base + 16], rows[base + 32 : base + 48]
            keep_ref[half * 2 + zz, x, b] = jnp.where(first, one, two)
            send_ref[half * 2 + zz, x, b] = jnp.where(first, two, one)


def pack_kernel(qkv_ref, proj_ref, expand_ref, contract_ref, heads_ref, units_ref, one_ref, two_ref):
    for layer in range(LAYERS):
        at = 6 * layer
        one_ref[at + 3] = proj_ref[layer].astype(BF)
        for b in range(4):
            two_ref[at + 2 + b] = contract_ref[layer, 16 * b : 16 * b + 16, :].astype(BF)
        for g in range(GROUPS):
            lanes = slice(128 * g, 128 * g + 128)
            part = dot(qkv_ref[layer, :, 384 * g : 384 * g + 384].astype(BF), heads_ref[...]).astype(BF)
            for s in range(3):
                one_ref[at + s, :, lanes] = part[:, 128 * s : 128 * s + 128]
            part = dot(expand_ref[layer, :, 512 * g : 512 * g + 512].astype(BF), units_ref[...]).astype(BF)
            for b in range(2):
                one_ref[at + 4 + b, :, lanes] = part[:, 128 * b : 128 * b + 128]
                two_ref[at + b, :, lanes] = part[:, 256 + 128 * b : 384 + 128 * b]


def stack_kernel(*refs):
    for k in range(4):
        refs[8][k] = refs[k][6:]
        refs[9][k] = refs[4 + k][6:]


def enter_kernel(x_ref, gain_ref, bias_ref, place_ref, hp_ref):
    hat, _ = normalized(x_ref[...].astype(F32))
    h = (hat * gain_ref[...] + bias_ref[...]).astype(BF)
    hp_ref[...] = dot(place_ref[...], h).astype(BF)


def attend_kernel(shifted, *refs):
    coords_ref, pieces, refs = refs[0], refs[1:9], refs[9:]
    if shifted:
        h_ref, rows_ref, cols_ref, corner_ref, place_ref, bias_ref, table_ref, mask_ref, take_ref = refs[:9]
        w_ref, hp_ref, qkv_ref, attn_ref, ctx_ref, rows_out, cols_out, corner_out, sems = refs[9:]
        copies = assembly(coords_ref, [(pieces, True, (0, 3), 0)], w_ref, sems)
        place = place_ref[...]
        hp = dot(place[:, :CELLS], h_ref[...])
        slabs = jnp.concatenate([rows_ref[...], cols_ref[...], corner_ref[...]], 0)
        hp_ref[...] = (hp + dot(place[:, CELLS:], slabs)).astype(BF)
    else:
        hp_ref, bias_ref, table_ref, place_ref = refs[:4]
        w_ref, qkv_ref, attn_ref, ctx_ref, ctxp_ref, sems = refs[4:]
        copies = assembly(coords_ref, [(pieces, True, (0, 3), 0)], w_ref, sems)
    for c in copies:
        c.wait()
    for s in range(3):
        for half in range(2):
            lanes = slice(half * 256, half * 256 + 256)
            wide = slice(s * D + half * 256, s * D + half * 256 + 256)
            qkv_ref[:, wide] = (dot(hp_ref[...], block_lanes(w_ref, s, lanes)) + bias_ref[:, wide]).astype(BF)
    into = ctx_ref if shifted else ctxp_ref

    def one_pair(p, carry):
        start = pl.multiple_of(p * 128, 128)
        for g in range(GROUPS):
            lane = g * 128
            keys = head_rows(side_by_side(qkv_ref, start, D + lane))
            queries = block_diagonal(side_by_side(qkv_ref, start, lane))
            scores = dot_nt(keys, queries) * (HEAD_DIM**-0.5 * log2e) + table_ref[g * 256 : (g + 1) * 256, :]
            scores = scores.reshape(4, SLOT, 128)
            if shifted:
                scores = jnp.where(mask_ref[p][None] > 0, scores, masked_score)
            scores = jnp.exp2(scores - jnp.max(scores, 1, keepdims=True))
            scores = scores * (1.0 / jnp.sum(scores, 1, keepdims=True))
            attn = scores.reshape(256, 128).astype(BF)
            attn_ref[p, g] = attn
            values = head_rows(side_by_side(qkv_ref, start, 2 * D + lane))
            store_diagonal(into, start, lane, dot_tn(attn, values))
        return carry

    lax.fori_loop(0, PAIRS, one_pair, 0)
    if shifted:
        sent = dot(take_ref[...], ctx_ref[...]).astype(BF)
        rows_out[...] = sent[:SLAB]
        cols_out[...] = sent[SLAB : 2 * SLAB]
        corner_out[...] = sent[2 * SLAB :]
    else:
        ctx_ref[...] = dot(place_ref[...], ctxp_ref[...]).astype(BF)


def forward_kernel(last, *refs):
    coords_ref, ones, twos, refs = refs[0], refs[1:9], refs[9:17], refs[17:]
    w_ref, sems = refs[11] if last else refs[10], refs[-1]
    copies = assembly(coords_ref, [(ones, True, (3, 3), 0), (twos, False, (0, 6), 3)], w_ref, sems)
    if last:
        x_ref, ctxp_ref, rows_ref, cols_ref, corner_ref, place_ref = refs[:6]
        bp_ref, g2_ref, b2_ref, bo_ref, bh_ref = refs[6:11]
        ctx_ref, mid_ref, h2_ref, hidden_ref, slope_ref, out_ref = refs[12:18]
        place = place_ref[...]
        slabs = jnp.concatenate([rows_ref[...], cols_ref[...], corner_ref[...]], 0)
        ctx_ref[...] = (dot(place[:, :PADDED], ctxp_ref[...]) + dot(place[:, PADDED:], slabs)).astype(BF)
    else:
        x_ref, ctx_ref, bp_ref, g2_ref, b2_ref, bo_ref, bh_ref = refs[:7]
        g1_ref, b1_ref, take_ref = refs[7:10]
        mid_ref, h2_ref, hidden_ref, slope_ref, out_ref, h_ref, rows_out, cols_out, corner_out = refs[11:20]
    for c in copies:
        c.wait()
    mid_ref[...] = x_ref[...].astype(F32) + dot(ctx_ref[...], block(w_ref, 0)) + bp_ref[...]
    hat, _ = normalized(mid_ref[...])
    h2_ref[...] = (hat * g2_ref[...] + b2_ref[...]).astype(BF)
    for b in range(4):
        for half in range(2):
            lanes = slice(half * 256, half * 256 + 256)
            wide = slice(b * D + half * 256, b * D + half * 256 + 256)
            pre = dot(h2_ref[...], block_lanes(w_ref, 1 + b, lanes)) + bh_ref[:, wide]
            hidden, slope = gelu_both(pre)
            hidden_ref[:, wide] = hidden.astype(BF)
            slope_ref[:, wide] = slope.astype(BF)
    out = mid_ref[...] + bo_ref[...]
    for b in range(4):
        out = out + dot(hidden_ref[:, b * D : (b + 1) * D], block(w_ref, 5 + b))
    out_ref[...] = out.astype(out_ref.dtype)
    if not last:
        hat, _ = normalized(out)
        h_ref[...] = (hat * g1_ref[...] + b1_ref[...]).astype(BF)
        sent = dot(take_ref[...], h_ref[...]).astype(BF)
        rows_out[...] = sent[:SLAB]
        cols_out[...] = sent[SLAB : 2 * SLAB]
        corner_out[...] = sent[2 * SLAB :]


def hidden_back_pass(gm_ref, slope_ref, w_ref, dpre_ref, dbh_ref):
    for b in range(4):
        for half in range(2):
            wide = slice(b * D + half * 256, b * D + half * 256 + 256)
            dpre = dot_nt(gm_ref[...], block_rows(w_ref, 5 + b, half)) * slope_ref[:, wide].astype(F32)
            dpre = dpre.astype(BF)
            dpre_ref[:, wide] = dpre
            dbh_ref[:, wide] = jnp.sum(dpre.astype(F32), 0, keepdims=True)


def middle_back_pass(dpre_ref, w_ref, mid_ref, g2_ref, dmid_ref, go_ref, small_ref):
    dh2 = dot_nt(dpre_ref[:, :D], block(w_ref, 1))
    for b in range(1, 4):
        dh2 = dh2 + dot_nt(dpre_ref[:, b * D : (b + 1) * D], block(w_ref, 1 + b))
    dx, dg2, db2 = norm_back(dh2, mid_ref[...], g2_ref[...])
    small_ref[1:2, :] = dg2
    small_ref[2:3, :] = db2
    dmid_ref[...] += dx
    go_ref[...] = dmid_ref[...].astype(BF)
    small_ref[0:1, :] = jnp.sum(go_ref[...].astype(F32), 0, keepdims=True)


def back_last_kernel(*refs):
    g_ref, slope_ref, mid_ref, w_ref, g2_ref, take_ref = refs[:6]
    dmid_ref, dpre_ref, go_ref, small_ref, dbh_ref, dctx_ref, rows_out, cols_out, corner_out = refs[6:]
    dmid_ref[...] = g_ref[...].astype(F32)
    small_ref[3:4, :] = jnp.sum(g_ref[...].astype(F32), 0, keepdims=True)
    hidden_back_pass(g_ref, slope_ref, w_ref, dpre_ref, dbh_ref)
    middle_back_pass(dpre_ref, w_ref, mid_ref, g2_ref, dmid_ref, go_ref, small_ref)
    dctx_ref[...] = dot_nt(go_ref[...], block(w_ref, 0)).astype(BF)
    sent = dot(take_ref[...], dctx_ref[...]).astype(BF)
    rows_out[...] = sent[:SLAB]
    cols_out[...] = sent[SLAB : 2 * SLAB]
    corner_out[...] = sent[2 * SLAB :]


def grads_last_kernel(coords_ref, gm_ref, hidden_ref, h2_ref, dpre_ref, ctx_ref, go_ref, keep_ref, send_ref):
    for half in range(2):
        rows = slice(half * 256, half * 256 + 256)
        store_grad(coords_ref, keep_ref, send_ref, 0, half, dot_tn(ctx_ref[:, rows], go_ref[...]))
        for b in range(4):
            wide = slice(b * D + half * 256, b * D + half * 256 + 256)
            grad_e = dot_tn(h2_ref[:, rows], dpre_ref[:, b * D : (b + 1) * D])
            store_grad(coords_ref, keep_ref, send_ref, 1 + b, half, grad_e)
            store_grad(coords_ref, keep_ref, send_ref, 5 + b, half, dot_tn(hidden_ref[:, wide], gm_ref[...]))


def back_first_kernel(*refs):
    coords_ref, dmid1_ref, dhp_ref, rows_ref, cols_ref, corner_ref, back_ref, x1_ref, g1_ref = refs[:9]
    hidden_ref, slope_ref, h2_ref, w_ref = refs[9:13]
    grad_ref, dpre_ref, keep_ref, send_ref, dbo_ref, dbh_ref, above_ref, gm_ref = refs[13:]
    back = back_ref[...]
    slabs = jnp.concatenate([rows_ref[...], cols_ref[...], corner_ref[...]], 0)
    dh = dot(back[:, :PADDED], dhp_ref[...]) + dot(back[:, PADDED:], slabs)
    dx, dg1, db1 = norm_back(dh, x1_ref[...], g1_ref[...])
    above_ref[0:1, :] = dg1
    above_ref[1:2, :] = db1
    grad = dmid1_ref[...] + dx
    grad_ref[...] = grad
    gm_ref[...] = grad.astype(BF)
    dbo_ref[...] = jnp.sum(gm_ref[...].astype(F32), 0, keepdims=True)
    hidden_back_pass(gm_ref, slope_ref, w_ref, dpre_ref, dbh_ref)
    for half in range(2):
        rows = slice(half * 256, half * 256 + 256)
        for b in range(4):
            wide = slice(b * D + half * 256, b * D + half * 256 + 256)
            grad_e = dot_tn(h2_ref[:, rows], dpre_ref[:, b * D : (b + 1) * D])
            store_grad(coords_ref, keep_ref, send_ref, b, half, grad_e)
            store_grad(coords_ref, keep_ref, send_ref, 4 + b, half, dot_tn(hidden_ref[:, wide], gm_ref[...]))


def middle_first_kernel(grad_ref, dpre_ref, mid_ref, ctx_ref, w_ref, g2_ref, place_ref, *outs):
    dmid_ref, dwp_ref, small_ref, dctxp_ref, go_ref = outs
    dmid_ref[...] = grad_ref[...]
    middle_back_pass(dpre_ref, w_ref, mid_ref, g2_ref, dmid_ref, go_ref, small_ref)
    dctx = dot_nt(go_ref[...], block(w_ref, 0)).astype(BF)
    dctxp_ref[...] = dot(place_ref[...], dctx).astype(BF)
    for half in range(2):
        rows = slice(half * 256, half * 256 + 256)
        dwp_ref[rows, :] = dot_tn(ctx_ref[:, rows], go_ref[...]).astype(BF)


def attend_back_pairs(pairs, qkv_ref, attn_ref, dctxp_ref, dqkv_ref, dtable_ref):
    dtable_ref[...] = jnp.zeros_like(dtable_ref)
    scale = HEAD_DIM**-0.5

    def one_pair(p, carry):
        start = pl.multiple_of(p * 128, 128)
        for g in range(GROUPS):
            lane = g * 128
            attn = attn_ref[p, g]
            keys = head_rows(side_by_side(qkv_ref, start, D + lane))
            values = head_rows(side_by_side(qkv_ref, start, 2 * D + lane))
            queries = block_diagonal(side_by_side(qkv_ref, start, lane))
            grads = block_diagonal(side_by_side(dctxp_ref, start, lane))
            probs = attn.astype(F32).reshape(4, SLOT, 128)
            dprobs = dot_nt(values, grads).reshape(4, SLOT, 128)
            dscores = probs * (dprobs - jnp.sum(probs * dprobs, 1, keepdims=True))
            dscores = dscores.reshape(256, 128).astype(BF)
            dtable_ref[g * 256 : (g + 1) * 256, :] += dscores.astype(F32)
            store_diagonal(dqkv_ref, start, lane, dot_tn(dscores, keys) * scale)
            dkeys = (head_fold(dot(dscores, queries)) * scale).astype(BF)
            dqkv_ref[pl.ds(start, SLOT), D + lane : D + lane + 128] = dkeys[:, :128]
            dqkv_ref[pl.ds(start + SLOT, SLOT), D + lane : D + lane + 128] = dkeys[:, 128:]
            dvalues = head_fold(dot(attn, grads)).astype(BF)
            dqkv_ref[pl.ds(start, SLOT), 2 * D + lane : 2 * D + lane + 128] = dvalues[:, :128]
            dqkv_ref[pl.ds(start + SLOT, SLOT), 2 * D + lane : 2 * D + lane + 128] = dvalues[:, 128:]
        return carry

    lax.fori_loop(0, pairs, one_pair, 0)


def table_sum(dtable_ref, hot_ref, out_ref):
    total = jnp.zeros((2 * HEADS, 256), F32)
    for c in range(25):
        keys = [dtable_ref[pl.ds(2 * c + k, HEADS, stride=SLOT), :] for k in range(2)]
        rows = jnp.concatenate(keys, 1)
        high = rows.astype(BF)
        low = (rows - high.astype(F32)).astype(BF)
        total = total + dot(jnp.concatenate([high, low], 0), hot_ref[256 * c : 256 * c + 256, :])
    out_ref[...] = total[:HEADS] + total[HEADS:]


def attend_back_kernel(*refs):
    dctx_ref, rows_ref, cols_ref, corner_ref, place_ref, qkv_ref, attn_ref, w_ref, take_ref, hot_ref = refs[:10]
    dqkv_ref, dbias_ref, table_ref, dhp_ref, rows_out, cols_out, corner_out, dctxp_ref, dtable_ref = refs[10:]
    place = place_ref[...]
    slabs = jnp.concatenate([rows_ref[...], cols_ref[...], corner_ref[...]], 0)
    dctxp_ref[...] = (dot(place[:, :CELLS], dctx_ref[...]) + dot(place[:, CELLS:], slabs)).astype(BF)
    attend_back_pairs(PAIRS, qkv_ref, attn_ref, dctxp_ref, dqkv_ref, dtable_ref)
    table_sum(dtable_ref, hot_ref, table_ref)
    for s in range(3):
        dbias_ref[s : s + 1, :] = jnp.sum(dqkv_ref[:, s * D : (s + 1) * D].astype(F32), 0, keepdims=True)
    dhp = dot_nt(dqkv_ref[:, :D], block(w_ref, 0))
    for s in range(1, 3):
        dhp = dhp + dot_nt(dqkv_ref[:, s * D : (s + 1) * D], block(w_ref, s))
    dhp_ref[...] = dhp.astype(BF)
    sent = dot(take_ref[...], dhp_ref[...]).astype(BF)
    rows_out[...] = sent[:SLAB]
    cols_out[...] = sent[SLAB : 2 * SLAB]
    corner_out[...] = sent[2 * SLAB :]


def grads_heads_kernel(coords_ref, hp_ref, dqkv_ref, keep_ref, send_ref):
    for s in range(3):
        for half in range(2):
            rows = slice(half * 256, half * 256 + 256)
            grad_w = dot_tn(hp_ref[:, rows], dqkv_ref[:, s * D : (s + 1) * D])
            store_grad(coords_ref, keep_ref, send_ref, s, half, grad_w)


def attend_back_half_kernel(dctxp_ref, qkv_ref, attn_ref, dqkv_ref, dtable_ref):
    attend_back_pairs(PAIRS // 2, qkv_ref, attn_ref, dctxp_ref, dqkv_ref, dtable_ref)


def attend_back_end_kernel(*refs):
    coords_ref, dctxp_ref, qkv_ref, attn_ref, one_ref, first_ref, hp_ref, dwp_ref, hot_ref, w_ref, place_ref = refs[:11]
    x_ref, dmid_ref, g1_ref, norm1, dqb1, sums1, dbh1, table1, sums0, dbo0, dbh0 = refs[11:22]
    keep_ref, send_ref, out_ref, sums_ref, two_ref, dtable_ref, dhp_ref = refs[22:]
    attend_back_pairs(PAIRS // 2, qkv_ref, attn_ref, dctxp_ref, two_ref, dtable_ref)
    upper = PADDED // 2
    dqb = []
    for s in range(3):
        wide = slice(s * D, (s + 1) * D)
        dqb.append(
            jnp.sum(one_ref[:, wide].astype(F32), 0, keepdims=True)
            + jnp.sum(two_ref[:, wide].astype(F32), 0, keepdims=True)
        )
        for half in range(2):
            rows = slice(half * 256, half * 256 + 256)
            grad_w = dot_tn(hp_ref[:upper, rows], one_ref[:, wide]) + dot_tn(hp_ref[upper:, rows], two_ref[:, wide])
            store_grad(coords_ref, keep_ref, send_ref, s, half, grad_w)
    for half in range(2):
        store_grad(coords_ref, keep_ref, send_ref, 3, half, dwp_ref[half * 256 : half * 256 + 256, :])
    for half, half_ref in enumerate((one_ref, two_ref)):
        part = dot_nt(half_ref[:, :D], block(w_ref, 0))
        for s in range(1, 3):
            part = part + dot_nt(half_ref[:, s * D : (s + 1) * D], block(w_ref, s))
        dhp_ref[half * upper : half * upper + upper, :] = part.astype(BF)
    dh = dot(place_ref[...], dhp_ref[...])
    dx, dg1, db1 = norm_back(dh, x_ref[...].astype(F32), g1_ref[...])
    out_ref[...] = dmid_ref[...] + dx
    for at, norm, query, value, sums, dbo, dbh in (
        (0, (dg1, db1), dqb[0], dqb[2], sums0, dbo0[...], dbh0),
        (12, (norm1[0:1, :], norm1[1:2, :]), dqb1[0:1, :], dqb1[2:3, :], sums1, sums1[3:4, :], dbh1),
    ):
        rows = [*norm, query, value, sums[0:1, :], sums[1:2, :], sums[2:3, :], dbo]
        rows += [dbh[:, D * b : D * b + D] for b in range(4)]
        for i, row in enumerate(rows):
            sums_ref[at + i : at + i + 1, :] = row
    dtable_ref[...] += first_ref[...]
    table_sum(dtable_ref, hot_ref, sums_ref.at[24:40, 0:256])
    sums_ref[24:40, 256:512] = table1[...]


def add_kernel(*refs):
    out_ref, at = refs[-1], 0
    for i in range(0, len(refs) - 1, 2):
        n = refs[i].shape[2]
        total = refs[i][...].astype(F32) + refs[i + 1][...].astype(F32)
        out_ref[:, :, at : at + n] = total.astype(BF)
        at += n


def sum_split_kernel(coords_ref, parts_ref, *outs):
    for d, out in enumerate(outs):
        target = lax.bitwise_xor(coords_ref[1], d)
        total = parts_ref[0, target].astype(F32)
        for k in range(1, 4):
            total = total + parts_ref[k, target].astype(F32)
        out[...] = total.astype(BF)


def four(refs, b):
    return (refs[0][b].astype(F32) + refs[1][b].astype(F32)) + (refs[2][b].astype(F32) + refs[3][b].astype(F32))


def reorder(values, order):
    high = values.astype(BF)
    rest = values - high.astype(F32)
    low = rest.astype(BF)
    last = (rest - low.astype(F32)).astype(BF)
    return dot_nt(high, order) + dot_nt(low, order) + dot_nt(last, order)


def step_into(at, grad, old, new, rate, decay):
    weight, first, second = (ref[at] for ref in old)
    for ref, value in zip(new, adamw(weight, first, second, grad, rate, decay)):
        ref[at] = value


def update_small_kernel(sums_ref, units_ref, *refs):
    small, table, new_small, new_table, bias_ref = refs[:3], refs[3:6], refs[6:9], refs[9:12], refs[12]
    for layer in range(LAYERS):
        rows = [sums_ref[12 * layer + i : 12 * layer + i + 1, :] for i in range(12)]
        bias_ref[layer : layer + 1, :] = rows[7]
        for g in range(GROUPS):
            part = jnp.concatenate([rows[8 + b][:, 128 * g : 128 * g + 128] for b in range(4)], 1)
            rows.append(reorder(jnp.broadcast_to(part, (8, D)), units_ref[...])[:1])
        for i, grad in enumerate(rows[:8] + rows[12:]):
            at = (slice(layer, layer + 1), slice(D * i, D * i + D))
            step_into(at, grad, small, new_small, 0.3, 0.0)
        grad = sums_ref[24:40, 256 * layer : 256 * layer + 256].T[:REL]
        step_into((layer,), grad, table, new_table, 0.6, 0.0)


def update_kernel(*refs):
    early, late, heads_ref, units_ref, refs = refs[:4], refs[4:8], refs[8], refs[9], refs[10:]
    old = [refs[3 * i : 3 * i + 3] for i in range(4)]
    new = [refs[12 + 3 * i : 15 + 3 * i] for i in range(4)]

    def layer_step(heads, head_at, rest, rest_at):
        step_into((0,), four(rest, rest_at), old[1], new[1], 0.1, 0.05)
        for b in range(4):
            step_into((0, slice(16 * b, 16 * b + 16)), four(rest, rest_at + 5 + b), old[3], new[3], 0.03, 0.05)
        for n, wide, order_ref, i, pieces, at in (
            (3, 384, heads_ref, 0, heads, head_at),
            (4, 512, units_ref, 2, rest, rest_at + 1),
        ):
            grads = [four(pieces, at + b) for b in range(n)]
            for g in range(GROUPS):
                part = jnp.concatenate([v[:, 128 * g : 128 * g + 128] for v in grads], 1)
                lanes = (0, slice(None), slice(wide * g, wide * g + wide))
                step_into(lanes, reorder(part, order_ref[...]), old[i], new[i], 0.03, 0.05)

    @pl.when(pl.program_id(0) == 0)
    def _():
        layer_step(late, 0, late, 3)

    @pl.when(pl.program_id(0) == 1)
    def _():
        layer_step(late, 12, early, 0)


def to_neighbours(slabs, ahead):
    step = -1 if ahead else 1
    along = [(i, (i + step) % 4) for i in range(4)]
    over = [(0, 1), (1, 0)]
    both = [(i * 2 + c, ((i + step) % 4) * 2 + 1 - c) for i in range(4) for c in range(2)]
    rows, cols, corner = slabs
    return (
        lax.ppermute(rows, "seq", along),
        lax.ppermute(cols, "col", over),
        lax.ppermute(corner, ("seq", "col"), both),
    )


def flat(z, x, core):
    return (z * 4 + (x // 2) * 2 + core) * 2 + x % 2


ALONG_X = [[flat(z, x, core) for x in range(4)] for z in range(4) for core in range(2)]
OVER_XZ = [[flat(z, x, core) for z in range(4) for x in range(4)] for core in range(2)]
OTHER_CORE = [(i, i ^ 1) for i in range(16)]


def from_z(distance):
    return [(((z + distance) % 4) * 4 + k, z * 4 + k) for z in range(4) for k in range(4)]


ALONG_Z = [[z * 4 + k for z in range(4)] for k in range(4)]


def along_x(value):
    return lax.all_to_all(value, ("img", "col"), 0, 0, tiled=True, axis_index_groups=ALONG_X)


def along_z(value):
    return lax.all_to_all(value, "img", 0, 0, tiled=True, axis_index_groups=ALONG_Z)


def from_core(value):
    return lax.ppermute(value, "img", OTHER_CORE)


def four_sum(value, axis, pairs):
    one, two, three = (lax.ppermute(value, axis, p) for p in pairs)
    return (value.astype(F32) + one.astype(F32)) + (two.astype(F32) + three.astype(F32))


BY_SEQ = [[(i, i ^ d) for i in range(4)] for d in (1, 2, 3)]
BY_Z = [[(z * 4 + k, (z ^ d) * 4 + k) for z in range(4) for k in range(4)] for d in (1, 2, 3)]
BY_X = [
    [(flat(z, x, c), flat(z, x ^ d, c)) for z in range(4) for x in range(4) for c in range(2)] for d in (1, 2, 3)
]


def both_cores(*pairs):
    arrays = [a for pair in pairs for a in pair]
    specs = [pl.BlockSpec((1, *a.shape[1:]), lambda i: (i, 0, 0, 0, 0)) for a in arrays]
    shape = (4, 4, sum(keep.shape[2] for keep, _ in pairs), 16, D)
    size = math.prod(shape) * 2
    return pl.pallas_call(
        add_kernel,
        grid=(4,),
        out_shape=jax.ShapeDtypeStruct(shape, BF),
        in_specs=specs,
        out_specs=pl.BlockSpec((1, *shape[1:]), lambda i: (i, 0, 0, 0, 0)),
        compiler_params=pltpu.CompilerParams(vmem_limit_bytes=VMEM_BYTES),
        cost_estimate=pl.CostEstimate(flops=size, bytes_accessed=3 * size, transcendentals=0),
    )(*arrays)


def summed(parts):
    return parts.astype(F32).sum(0).astype(BF)


def by_seq(value):
    return [value] + [lax.ppermute(value, "seq", p) for p in BY_SEQ]


def all_sum(value):
    value = value + lax.ppermute(value, "img", OTHER_CORE)
    value = four_sum(value, ("img", "col"), BY_X)
    value = four_sum(value, "img", BY_Z)
    return four_sum(value, "seq", BY_SEQ)


def update(early, late, heads, units, state):
    whole = [pl.BlockSpec(memory_space=pltpu.VMEM)] * 10
    parts = [pl.BlockSpec((1, *a.shape[1:]), lambda layer: (layer, 0, 0)) for a in state]
    return pl.pallas_call(
        update_kernel,
        grid=(LAYERS,),
        out_shape=[jax.ShapeDtypeStruct(a.shape, F32) for a in state],
        in_specs=whole + parts,
        out_specs=parts,
        compiler_params=pltpu.CompilerParams(vmem_limit_bytes=VMEM_BYTES),
        cost_estimate=pl.CostEstimate(flops=20 * 10**9, bytes_accessed=2 * 10**7, transcendentals=0),
    )(*early, *late, heads, units, *state)


def adamw(weight, first, second, grad, rate, decay):
    first = 0.9 * first + 0.1 * grad
    second = 0.999 * second + 0.001 * grad * grad
    first_hat = first / (1.0 - 0.9**STEP)
    second_hat = second / (1.0 - 0.999**STEP)
    return (first, second, weight - rate * (first_hat / (jnp.sqrt(second_hat) + 1e-08) + decay * weight))


def hidden_order(vector):
    return vector.reshape(32, 4, 16).transpose(1, 0, 2).reshape(HIDDEN)


def split_small(vector):
    pieces = [vector[i * D : (i + 1) * D][None] for i in range(8)]
    return pieces + [hidden_order(vector[8 * D :])[None]]


def score_table(table, hot):
    rows = lax.dot_general(table, hot, (((0,), (0,)), ((), ())), precision=highest, preferred_element_type=F32)
    rows = rows.reshape(HEADS, AREA, AREA) * log2e
    rows = jnp.pad(rows, ((0, 0), (0, 0), (0, SLOT - AREA)))
    rows = jnp.pad(rows, ((0, 0), (0, SLOT - AREA), (0, 0)), constant_values=padded_score)
    return jnp.concatenate([rows, rows], 2).reshape(HEADS * SLOT, 128)


def allowed_pairs(region):
    win = region.reshape(4, WIN, 4, WIN).transpose(0, 2, 1, 3).reshape(16, AREA)
    win = jnp.pad(win, ((0, 0), (0, SLOT - AREA)))
    same = win[:, :, None] == win[:, None, :]
    same = same | (jnp.arange(SLOT) >= AREA)[None, :, None]
    same = same.reshape(PAIRS, 2, SLOT, SLOT).transpose(0, 2, 1, 3).reshape(PAIRS, SLOT, 128)
    return same.astype(F32)


def half_blocks(half):
    return {
        0: ((PADDED // 2, D), (half, 0)),
        1: ((PADDED // 2, 3 * D), (half, 0)),
        2: ((PAIRS // 2, GROUPS, 256, 128), (half, 0, 0, 0)),
    }


def local(
    images,
    out_grad,
    region_ids,
    rel_index,
    qkv_weight,
    qkv_first,
    qkv_second,
    proj_weight,
    proj_first,
    proj_second,
    expand_weight,
    expand_first,
    expand_second,
    contract_weight,
    contract_first,
    contract_second,
    small_params,
    small_first,
    small_second,
    bias_table,
    table_first,
    table_second,
):
    plain, plain_back, ahead, back, take_first, take_last = (jnp.asarray(a, BF) for a in placements())
    heads, units = (jnp.asarray(a, BF) for a in column_orders())
    img = lax.axis_index("img")
    x = (img // 2 % 2) * 2 + lax.axis_index("col")
    coords = jnp.stack([img // 4, x, img % 2]).astype(jnp.int32)
    packed = call(
        pack_kernel,
        [((12, 16, D), BF)] * 2,
        (qkv_weight, proj_weight, expand_weight, contract_weight, heads, units),
        us=3,
    )
    by_x = [packed[0]] + [lax.ppermute(packed[0], ("img", "col"), p) for p in BY_X]
    by_z = [packed[1]] + [lax.ppermute(packed[1], "img", from_z(d)) for d in (1, 2, 3)]

    def gathered(by_x, by_z):
        one = [by_x] + [lax.ppermute(by_x, "img", from_z(d)) for d in (1, 2, 3)]
        two = [by_z] + [lax.ppermute(by_z, ("img", "col"), p) for p in BY_X]
        return one + [from_core(v) for v in one], two + [from_core(v) for v in two]

    one0, two0 = gathered(jnp.stack([v[:6] for v in by_x]), jnp.stack([v[:6] for v in by_z]))
    x0 = images.reshape(CELLS, D)
    g_out = out_grad.reshape(CELLS, D)
    by_key = jnp.pad(rel_index.T, ((0, 1), (0, SLOT - AREA)), constant_values=-1)
    by_key = jnp.concatenate([by_key, by_key], 1)
    hot = (by_key.reshape(-1, 1) == jnp.arange(256, dtype=jnp.int32)).astype(BF)
    keys_hot = (jnp.arange(REL, dtype=jnp.int32)[:, None] == rel_index.T.reshape(1, AREA * AREA)).astype(F32)
    tables = [score_table(bias_table[layer], keys_hot) for layer in range(LAYERS)]
    region = lax.dynamic_slice_in_dim(region_ids, lax.axis_index("seq") * SIDE, SIDE, 0)
    mask = allowed_pairs(region)
    small = [split_small(small_params[layer]) for layer in range(LAYERS)]
    zero = jnp.zeros((1, D), F32)
    qkv_bias = [jnp.concatenate([s[2], zero, s[3]], 1) for s in small]

    qkv_shape = ((PADDED, 3 * D), BF)
    attn_shape = ((PAIRS, GROUPS, 256, 128), BF)
    slab_shapes = [((SLAB, D), BF), ((SLAB, D), BF), ((CORNER, D), BF)]
    cells16, cells32 = ((CELLS, D), BF), ((CELLS, D), F32)
    padded16 = ((PADDED, D), BF)
    wide16 = ((CELLS, HIDDEN), BF)

    copies, more_copies = pltpu.SemaphoreType.DMA((32,)), pltpu.SemaphoreType.DMA((64,))
    w_shapes = [((3, 32, 16, D), BF), ((9, 32, 16, D), BF)]
    g1, b1, _, _, bp, g2, b2, bo, bh = small[0]
    (hp0,) = call(enter_kernel, [padded16], (x0, g1, b1, plain), us=4)
    wq0, qkv0, attn0, ctx0 = call(
        functools.partial(attend_kernel, False),
        [w_shapes[0], qkv_shape, attn_shape, cells16],
        (hp0, qkv_bias[0], tables[0], plain_back),
        [pltpu.VMEM((PADDED, D), BF), copies],
        one0,
        coords,
        us=17,
    )
    one1, two1 = gathered(*call(stack_kernel, [((4, 6, 16, D), BF)] * 2, (*by_x, *by_z), after=(ctx0,)))
    wm0, mid0, h20, hidden0, slope0, x1, h1, *slabs = call(
        functools.partial(forward_kernel, False),
        [w_shapes[1], cells32, cells16, wide16, wide16, cells32, cells16, *slab_shapes],
        (x0, ctx0, bp, g2, b2, bo, bh, small[1][0], small[1][1], take_first),
        [more_copies],
        one0 + two0,
        coords,
        us=15,
    )
    g1, b1, _, _, bp, g2, b2, bo, bh = small[1]
    slabs = to_neighbours(slabs, True)
    wq1, hp1, qkv1, attn1, ctxp1, *slabs = call(
        functools.partial(attend_kernel, True),
        [w_shapes[0], padded16, qkv_shape, attn_shape, padded16, *slab_shapes],
        (h1, *slabs, ahead, qkv_bias[1], tables[1], mask, take_last),
        [copies],
        one1,
        coords,
        us=18,
    )
    slabs = to_neighbours(slabs, False)
    wm1, ctx1, mid1, h21, hidden1, slope1, out = call(
        functools.partial(forward_kernel, True),
        [w_shapes[1], cells16, cells32, cells16, wide16, wide16, cells16],
        (x1, ctxp1, *slabs, back, bp, g2, b2, bo, bh),
        [more_copies],
        one1 + two1,
        coords,
        us=15,
    )
    dmid1, dpre1, go1, sums1, dbh1, dctx1, *slabs = call(
        back_last_kernel,
        [cells32, wide16, cells16, ((4, D), F32), ((1, HIDDEN), F32), cells16, *slab_shapes],
        (g_out, slope1, mid1, wm1, g2, take_first),
        us=11,
    )
    slabs = to_neighbours(slabs, True)
    keep, send = call(
        grads_last_kernel,
        [((4, 4, 9, 16, D), BF)] * 2,
        (g_out, hidden1, h21, dpre1, ctx1, go1),
        place=coords,
        us=8,
    )
    part_m1 = both_cores((keep, from_core(send)))
    dqkv1, dqb1, table1, dhp1, *slabs = call(
        attend_back_kernel,
        [qkv_shape, ((3, D), F32), ((HEADS, 256), F32), padded16, *slab_shapes],
        (dctx1, *slabs, ahead, qkv1, attn1, wq1, take_last, hot),
        [pltpu.VMEM((PADDED, D), BF), pltpu.VMEM((HEADS * SLOT, 128), F32)],
        us=20,
        after=(part_m1,),
    )
    slabs = to_neighbours(slabs, False)
    keep, send = call(grads_heads_kernel, [((4, 4, 3, 16, D), BF)] * 2, (hp1, dqkv1), place=coords, us=4)
    pair_q1 = (keep, from_core(send))
    half_m1 = summed(along_z(part_m1))
    grad1, dpre0, keep, send, dbo0, dbh0, norm1 = call(
        back_first_kernel,
        [cells32, wide16, *[((4, 4, 8, 16, D), BF)] * 2, ((1, D), F32), ((1, HIDDEN), F32), ((2, D), F32)],
        (dmid1, dhp1, *slabs, back, x1, small[1][0], hidden0, slope0, h20, wm0),
        [pltpu.VMEM((CELLS, D), BF)],
        place=coords,
        us=16,
        after=(half_m1,),
    )
    grad_m1 = summed(along_x(half_m1))
    dmid0, dwp0, sums0, dctxp0 = call(
        middle_first_kernel,
        [cells32, ((D, D), BF), ((3, D), F32), padded16],
        (grad1, dpre0, mid0, ctx0, wm0, small[0][5], plain),
        [pltpu.VMEM((CELLS, D), BF)],
        us=8,
        after=(grad_m1,),
    )
    part_0 = both_cores((keep, from_core(send)), pair_q1)
    grads_m1 = by_seq(grad_m1)
    half_qkv, table_shape = ((PADDED // 2, 3 * D), BF), ((HEADS * SLOT, 128), F32)
    one, dtable0 = call(
        attend_back_half_kernel,
        [half_qkv, table_shape],
        (dctxp0, qkv0, attn0),
        us=9,
        after=(part_0,),
        blocks=half_blocks(0),
    )
    half_0 = along_z(part_0)
    keep, send, input_grad, sums = call(
        attend_back_end_kernel,
        [*[((4, 4, 4, 16, D), BF)] * 2, cells32, ((40, D), F32)],
        (dctxp0, qkv0, attn0, one, dtable0, hp0, dwp0, hot, wq0, plain_back, x0, dmid0, small[0][0])
        + (norm1, dqb1, sums1, dbh1, table1, sums0, dbo0, dbh0),
        [pltpu.VMEM(*half_qkv), pltpu.VMEM(*table_shape), pltpu.VMEM(*padded16)],
        place=coords,
        us=22,
        blocks=half_blocks(1),
        after=grads_m1,
    )
    part_q0 = both_cores((keep, from_core(send))).reshape(16, 4, 16, D)
    part_q0 = lax.all_to_all(part_q0, ("img", "col"), 0, 0, tiled=True, axis_index_groups=OVER_XZ)
    half_0, *others = call(sum_split_kernel, [((11, 16, D), BF)] * 4, (half_0,), place=coords)
    others = [lax.ppermute(v, ("img", "col"), p) for v, p in zip(others, BY_X)]
    grad_0 = sum((v.astype(F32) for v in others), half_0.astype(F32)).astype(BF)
    late = by_seq(jnp.concatenate([summed(part_q0), grad_0], 0))

    state = (
        (qkv_weight, qkv_first, qkv_second),
        (proj_weight, proj_first, proj_second),
        (expand_weight, expand_first, expand_second),
        (contract_weight, contract_first, contract_second),
    )
    flat_state = [a for three in state for a in three]
    done = update(grads_m1, late, heads, units, flat_state)
    qkv_new, proj_new, expand_new, contract_new = done[:3], done[3:6], done[6:9], done[9:]
    last = call(
        update_small_kernel,
        [((LAYERS, 12 * D), F32)] * 3 + [((LAYERS, REL, HEADS), F32)] * 3 + [((LAYERS, D), F32)],
        (all_sum(sums), units, small_params, small_first, small_second, bias_table, table_first, table_second),
        us=2,
    )
    return (
        out.reshape(images.shape),
        input_grad.reshape(images.shape),
        *qkv_new,
        *proj_new,
        *expand_new,
        *contract_new,
        *last,
    )


def solution(mesh):
    cells = P("img", "seq", "col", None)
    matrix = P(None, ("img", "col"), None)
    in_specs = (cells, cells, P(None, "col"), P(), *([matrix] * 12), *([P()] * 6))
    out_specs = (cells, cells, *([matrix] * 12), *([P()] * 7))
    return jax.shard_map(local, mesh=mesh, in_specs=in_specs, out_specs=out_specs, check_vma=False)
```

time: 1220 us -> 424 us (0.35)
  waiting for transfers between devices: 525 us -> 52 us
  local copies, waits for them, and re-layouts: 363 us -> 32.6 us
  Pallas kernels: 0 us -> 214 us
  matrix products: 162 us -> 1.32 us
  other arithmetic: 105 us -> 12.4 us
  starting transfers between devices: 32 us -> 102 us
  between operations: 16.3 us -> 1.89 us
    reduce_scatter x2 -> x0, waiting for transfers between devices: 272 us -> none  [the longest x1 219 us: sent_together(): lax.psum_scatter(both, axis, scatter_dimension=dim, tiled=True)]
    pallas_call x0 -> x21, Pallas kernels: none -> 214 us  [the longest x17 191 us: call(): pl.pallas_call(whole, grid=(1,) if blocks else (), out_shape=shapes, in_s...]
    dot_general x40 -> x2, matrix products: 162 us -> 1.32 us  [score_table(): lax.dot_general(table, hot, (((0,), (0,)), ((), ())), precision=highest,...]
    another operation x32 -> x10, local copies, waits for them, and re-layouts: 148 us -> 3.23 us  [the longest x2 1.38 us: split_small(): return pieces + [hidden_order(vector[8 * D:])[None]]]
    psum x1 -> x0, waiting for transfers between devices: 135 us -> none  [local(): lax.psum((jnp.stack(small_grads), jnp.stack(table_grads)), ('img', 'seq',...]
    all_gather x2 -> x0, waiting for transfers between devices: 82.2 us -> none  [gather_packed(): lines, at, finished = (lax.all_gather(vector, axis), 0, [])]
    ppermute x8 -> x69, starting transfers between devices: 11.1 us -> 82.2 us  [the longest x9 12.9 us: four_sum(): one, two, three = (lax.ppermute(value, axis, p) for p in pairs)]
    transpose x8 -> x3, local copies, waits for them, and re-layouts: 64.3 us -> 0.02 us  [the longest x2 0.01 us: hidden_order(): return vector.reshape(32, 4, 16).transpose(1, 0, 2).reshape(HIDDEN)]
  transfers between devices with their start and end apart: 17 -> 73, of which waited for: 12 -> 16; matrix products, arithmetic and copies ran while one was open for 25% -> 9% of each run, Pallas kernels for 0% -> 32%
where the time goes in v1:
time: 424 us; the launch traced here: 416 us
  Pallas kernels  214 us (50%)
  starting transfers between devices  102 us (24%)
  waiting for transfers between devices  52 us (12%)
  local copies, waits for them, and re-layouts  32.6 us (8%)
  other arithmetic  12.4 us (3%)
    pallas_call x17, Pallas kernels, call(): pl.pallas_call(whole, grid=(1,) if blocks else (), out_shape=shapes, in_s...  191 us
    ppermute x6, waiting for transfers between devices, gathered(): one = [by_x] + [lax.ppermute(by_x, 'img', from_z(d)) for d in (1, 2, 3)]  22 us
    unnamed x129, local copies, waits for them, and re-layouts  18.3 us
    pallas_call x3, Pallas kernels, both_cores(): pl.pallas_call(add_kernel, grid=(4,), out_shape=jax.ShapeDtypeStruct(shap...  13 us
    ppermute x9, starting transfers between devices, four_sum(): one, two, three = (lax.ppermute(value, axis, p) for p in pairs)  12.9 us
    all_to_all x2, starting transfers between devices, along_z(): lax.all_to_all(value, 'img', 0, 0, tiled=True, axis_index_groups=ALONG_Z)  10.3 us
    ppermute x6, starting transfers between devices, by_seq(): return [value] + [lax.ppermute(value, 'seq', p) for p in BY_SEQ]  9.85 us
    ppermute x6, starting transfers between devices, gathered(): one = [by_x] + [lax.ppermute(by_x, 'img', from_z(d)) for d in (1, 2, 3)]  9.44 us
  transfers between devices with their start and end apart: 73, of which 16 were waited for; matrix products, arithmetic and copies ran while one was open for 9% of the time, Pallas kernels for 32%

profile of v1, /device:TPU:0, one launch (start us, length us, event | category | flops | bytes accessed | tf_op | source)
XLA Modules:
  0.0 415.6 jit_solution(12244956905677593334)
XLA Ops:
  0.7 3.2 shard_map.445
  3.9 2.9 collective-permute-start.2
  10.6 3.6 collective-permute-start.11
  19.1 2.5 collective-permute-start.3
  23.1 2.7 collective-permute-done.10.refs_6_
  30.8 3.5 collective-permute-done.3.refs_2_
  35.3 2.8 collective-permute-start.29
  38.1 2.8 collective-permute-done.5.refs_4_
  44.0 4.3 %shard_map.446.refs_9_.refs_10_ = bf16[1024,512]{1,0:T(8,128)(2,1)} custom-call(bf16[784,512]{1,0:T(8,128)(2,1)} %reshape.136.refs_0_.refs_17_.refs_15_, f32[1,512]{1,0:T(1,128)} %get-tuple-element.266.refs_1_.refs_17_, f32[1,512]{1,0:T(1,128)} %get-tuple-element.265.refs_2_, bf16[1024,784]{1,0:T(8,128)(2,1)} %constant.87.clone.refs_3_.refs_7_), custom_call_target="tpu_custom_call" | custom-call | flops 4000000000 | bytes 4000000 | tf_op jit(solution)/shard_map/pallas_call | solution.py:195
  49.6 18.1 %shard_map.447 = (bf16[3,32,16,512]{3,2,1,0:T(8,128)(2,1)}, bf16[1024,1536]{1,0:T(8,128)(2,1)}, bf16[8,4,256,128]{3,2,1,0:T(8,128)(2,1)}, bf16[784,512]{1,0:T(8,128)(2,1)}) custom-call(s32[3]{0:T(128)} %pad_add_fusion.refs_0_.refs_1_.refs_4_, bf16[4,6,16,512]{3,2,1,0:T(8,128)(2,1)} %copy-done.10, bf16[4,6,16,512]{3,2,1,0:T(8,128)(2,1)} %collective-permute-done.3.refs_2_, ...), custom_call_target="tpu_custom_call" | custom-call | flops 16999999488 | bytes 17000000 | tf_op jit(solution)/shard_map/pallas_call | solution.py:195
  68.9 16.0 %shard_map.449 = (bf16[9,32,16,512]{3,2,1,0:T(8,128)(2,1)}, f32[784,512]{1,0:T(8,128)}, bf16[784,512]{1,0:T(8,128)(2,1)}, bf16[784,2048]{1,0:T(8,128)(2,1)}, bf1...) custom-call(s32[3]{0:T(128)} %pad_add_fusion.refs_0_.refs_1_.refs_4_, ...), custom_call_target="tpu_custom_call" | custom-call | flops 15000000512 | bytes 15000000 | tf_op jit(solution)/shard_map/pallas_call | solution.py:195
  84.9 3.1 collective-permute-start.34
  91.9 2.4 shard_map.448
  94.4 4.7 %collective-permute-start.13 = (bf16[4,6,16,512]{3,2,1,0:T(8,128)(2,1)}, bf16[4,6,16,512]{3,2,1,0:T(8,128)(2,1)S(1)}, u32[]{:S(2)}, u32[]{:S(2)}) collective-permute-start(bf16[4,6,16,512]{3,2,1,0:T(8,128)(2,1)} %get-tuple-element.117.refs_1_), channel_id=1, source_target_pairs={{32,0},{40,8},{48,16},{56,24},{64,32},{72,40},{80,48},{88,56},{96,... | collective-permute-start | bytes 1179656 | tf_op jit(solution)/shard_map/ppermute | solution.py:824
  102.5 13.4 %collective-permute-done.13.refs_2_ = bf16[4,6,16,512]{3,2,1,0:T(8,128)(2,1)S(1)} collective-permute-done((bf16[4,6,16,512]{3,2,1,0:T(8,128)(2,1)}, bf16[4,6,16,512]{3,2,1,0:T(8,128)(2,1)S(1)}, u32[]{:S(2)}, u32[]{:S(2)}) %collective-permute-start.13) | collective-permute-done | bytes 393248 | tf_op jit(solution)/shard_map/ppermute | solution.py:824
  125.8 19.3 %shard_map.450 = (bf16[3,32,16,512]{3,2,1,0:T(8,128)(2,1)}, bf16[1024,512]{1,0:T(8,128)(2,1)}, bf16[1024,1536]{1,0:T(8,128)(2,1)}, bf16[8,4,256,128]{3,2,1,0:T(8...) custom-call(s32[3]{0:T(128)} %pad_add_fusion.refs_0_.refs_1_.refs_4_, ...), custom_call_target="tpu_custom_call" | custom-call | flops 17999998976 | bytes 18000000 | tf_op jit(solution)/shard_map/pallas_call | solution.py:195
  151.8 4.6 %collective-permute-done.39.refs_21_ = bf16[16,512]{1,0:T(8,128)(2,1)S(1)} collective-permute-done((bf16[16,512]{1,0:T(8,128)(2,1)}, bf16[16,512]{1,0:T(8,128)(2,1)S(1)}, u32[]{:S(2)}, u32[]{:S(2)}) %collective-permute-start.39) | collective-permute-done | bytes 16416 | tf_op jit(solution)/shard_map/ppermute | solution.py:654
  157.1 16.1 %shard_map.451 = (bf16[9,32,16,512]{3,2,1,0:T(8,128)(2,1)}, bf16[784,512]{1,0:T(8,128)(2,1)}, f32[784,512]{1,0:T(8,128)}, bf16[784,512]{1,0:T(8,128)(2,1)}, bf16...) custom-call(s32[3]{0:T(128)} %pad_add_fusion.refs_0_.refs_1_.refs_4_, ...), custom_call_target="tpu_custom_call" | custom-call | flops 15000000512 | bytes 15000000 | tf_op jit(solution)/shard_map/pallas_call | solution.py:195
  173.2 10.3 %shard_map.452 = (f32[784,512]{1,0:T(8,128)}, bf16[784,2048]{1,0:T(8,128)(2,1)}, bf16[784,512]{1,0:T(8,128)(2,1)}, f32[4,512]{1,0:T(4,128)}, f32[1,2048]{1,0:T(1...) custom-call(bf16[784,512]{1,0:T(8,128)(2,1)} %reshape.144.refs_0_.re, ...), custom_call_target="tpu_custom_call" | custom-call | flops 11000000512 | bytes 11000000 | tf_op jit(solution)/shard_map/pallas_call | solution.py:195
  183.5 11.1 %shard_map.453 = (bf16[4,4,9,16,512]{4,3,2,1,0:T(8,128)(2,1)}, bf16[4,4,9,16,512]{4,3,2,1,0:T(8,128)(2,1)}) custom-call(s32[3]{0:T(128)} %pad_add_fusion.refs_0_.refs_1_.refs_4_, bf16[784,512]{1,0:T(8,128)(2,1)} %reshape.144.refs_0_.refs_1_, bf16[784,2048]{1,0:T(8,128)(2,1)} %get-tuple-element.129.refs_2_, bf16[784,512]{1,0:T(8,128)(2,1)} %get-tuple-element.130.refs_3_, ...), custom_call_target="tpu_custom_call" | custom-call | flops 8000000000 | bytes 8000000 | tf_op jit(solution)/shard_map/pallas_call | solution.py:195
  198.5 3.9 fusion.refs_10_.refs_12_
  203.9 4.5 %shard_map.454.refs_0_ = bf16[4,4,9,16,512]{4,3,2,1,0:T(8,128)(2,1)} custom-call(bf16[4,4,9,16,512]{4,3,2,1,0:T(8,128)(2,1)} %get-tuple-element.137.refs_0_, bf16[4,4,9,16,512]{4,3,2,1,0:T(8,128)(2,1)} %copy-done.3), custom_call_target="tpu_custom_call" | custom-call | flops 2359296 | bytes 7077888 | tf_op jit(solution)/shard_map/pallas_call | solution.py:703
  208.4 5.5 %all-to-all-start = ((bf16[4,4,9,16,512]{4,3,2,1,0:T(8,128)(2,1)}), bf16[4,4,9,16,512]{4,3,2,1,0:T(8,128)(2,1)S(1)}, u32[]{:S(2)}, u32[]{:S(2)}) async-start(bf16[4,4,9,16,512]{4,3,2,1,0:T(8,128)(2,1)} %shard_map.454.refs_0_), calls=%async_computation | async-start | bytes 4718592 | tf_op jit(solution)/shard_map/all_to_all | solution.py:679
  214.6 22.3 %shard_map.455 = (bf16[1024,1536]{1,0:T(8,128)(2,1)}, f32[3,512]{1,0:T(4,128)}, f32[16,256]{1,0:T(8,128)}, bf16[1024,512]{1,0:T(8,128)(2,1)}, bf16[96,512]{1,0:T...) custom-call(bf16[4,4,9,16,512]{4,3,2,1,0:T(8,128)(2,1)} %shard_map.454.refs_0_, ...), custom_call_target="tpu_custom_call" | custom-call | flops 20000000000 | bytes 20000000 | tf_op jit(solution)/shard_map/pallas_call | solution.py:195
  238.8 2.8 collective-permute-start.48
  244.8 4.7 %collective-permute-done.49.refs_6_ = bf16[16,512]{1,0:T(8,128)(2,1)S(1)} collective-permute-done((bf16[16,512]{1,0:T(8,128)(2,1)}, bf16[16,512]{1,0:T(8,128)(2,1)S(1)}, u32[]{:S(2)}, u32[]{:S(2)}) %collective-permute-start.49) | collective-permute-done | bytes 16416 | tf_op jit(solution)/shard_map/ppermute | solution.py:654
  250.2 16.4 %shard_map.456 = (f32[784,512]{1,0:T(8,128)}, bf16[784,2048]{1,0:T(8,128)(2,1)}, bf16[4,4,8,16,512]{4,3,2,1,0:T(8,128)(2,1)}, bf16[4,4,8,16,512]{4,3,2,1,0:T(8,1...) custom-call(bf16[4,9,16,512]{3,2,1,0:T(8,128)(2,1)} %reduce_sum.36.refs_0_, ...), custom_call_target="tpu_custom_call" | custom-call | flops 16000000000 | bytes 16000000 | tf_op jit(solution)/shard_map/pallas_call | solution.py:195
  266.6 3.5 all-to-all-start.1
  270.1 5.2 %shard_map.458 = (bf16[4,4,3,16,512]{4,3,2,1,0:T(8,128)(2,1)}, bf16[4,4,3,16,512]{4,3,2,1,0:T(8,128)(2,1)}) custom-call(s32[3]{0:T(128)} %pad_add_fusion.refs_0_.refs_1_.refs_4_, bf16[1024,512]{1,0:T(8,128)(2,1)} %get-tuple-element.163.refs_1_, bf16[1024,1536]{1,0:T(8,128)(2,1)} %get-tuple-element.164.refs_2_), custom_call_target="tpu_custom_call" | custom-call | flops 4000000000 | bytes 4000000 | tf_op jit(solution)/shard_map/pallas_call | solution.py:195
  275.7 5.1 %all-to-all-done.1 = bf16[4,9,16,512]{3,2,1,0:T(8,128)(2,1)S(1)} async-done(((bf16[4,9,16,512]{3,2,1,0:T(8,128)(2,1)}), bf16[4,9,16,512]{3,2,1,0:T(8,128)(2,1)S(1)}, u32[]{:S(2)}, u32[]{:S(2)}) %all-to-all-start.1) | async-done | bytes 589856 | tf_op jit(solution)/shard_map/all_to_all | solution.py:675
  283.2 3.3 collective-permute-start.43
  286.5 10.2 %shard_map.457 = (f32[784,512]{1,0:T(8,128)}, bf16[512,512]{1,0:T(8,128)(2,1)}, f32[3,512]{1,0:T(4,128)}, bf16[1024,512]{1,0:T(8,128)(2,1)}) custom-call(bf16[9,16,512]{2,1,0:T(8,128)(2,1)} %reduce_sum.37.refs_0_, f32[784,512]{1,0:T(8,128)} %get-tuple-element.155.refs_1_, bf16[784,2048]{1,0:T(8,128)(2,1)} %get-tuple-element.156.refs_2_, ...), custom_call_target="tpu_custom_call" | custom-call | flops 8000000000 | bytes 8000000 | tf_op jit(solution)/shard_map/pallas_call | solution.py:195
  298.3 4.8 %shard_map.459.refs_0_ = bf16[4,4,11,16,512]{4,3,2,1,0:T(8,128)(2,1)} custom-call(bf16[4,4,8,16,512]{4,3,2,1,0:T(8,128)(2,1)} %get-tuple-element.161.refs_0_, bf16[4,4,8,16,512]{4,3,2,1,0:T(8,128)(2,1)} %copy-done.4, bf16[4,4,3,16,512]{4,3,2,1,0:T(8,128)(2,1)} %get-tuple-element.165.refs_2_, bf16[4,4,3,16,512]{4,3,2,1,0:T(8,128)(2,1)} %copy-done.9), custom_call_target="tpu_custom_call" | custom-call | flops 2883584 | bytes 8650752 | tf_op jit(solution)/shard_map/pallas_call | solution.py:703
  303.1 4.8 %all-to-all-start.3 = ((bf16[4,4,11,16,512]{4,3,2,1,0:T(8,128)(2,1)}), bf16[4,4,11,16,512]{4,3,2,1,0:T(8,128)(2,1)S(1)}, u32[]{:S(2)}, u32[]{:S(2)}) async-start(bf16[4,4,11,16,512]{4,3,2,1,0:T(8,128)(2,1)} %shard_map.459.refs_0_), calls=%async_computation.3 | async-start | bytes 5767168 | tf_op jit(solution)/shard_map/all_to_all | solution.py:679
  307.9 9.2 %shard_map.460 = (bf16[512,1536]{1,0:T(8,128)(2,1)}, f32[1024,128]{1,0:T(8,128)}) custom-call(bf16[4,4,11,16,512]{4,3,2,1,0:T(8,128)(2,1)} %shard_map.459.refs_0_, bf16[1024,512]{1,0:T(8,128)(2,1)} %get-tuple-element.158.refs_1_.refs_5_, bf16[1024,1536]{1,0:T(8,128)(2,1)} %get-tuple-element.159.refs_2_.refs_6_, ...), custom_call_target="tpu_custom_call" | custom-call | flops 8999999488 | bytes 9000000 | tf_op jit(solution)/shard_map/pallas_call | solution.py:195
  317.1 18.9 %shard_map.461 = (bf16[4,4,4,16,512]{4,3,2,1,0:T(8,128)(2,1)}, bf16[4,4,4,16,512]{4,3,2,1,0:T(8,128)(2,1)}, f32[784,512]{1,0:T(8,128)}, f32[40,512]{1,0:T(8,128)}) custom-call(bf16[9,16,512]{2,1,0:T(8,128)(2,1)} %reduce_sum.37.refs_0_, bf16[9,16,512]{2,1,0:T(8,128)(2,1)} %collective-permute-done.41.refs_1_, ...), custom_call_target="tpu_custom_call" | custom-call | flops 22000001024 | bytes 22000000 | tf_op jit(solution)/shard_map/pallas_call | solution.py:195
  336.1 2.9 collective-permute-done.52.refs_1_
  340.0 3.7 shard_map.462
  345.3 5.9 %all-to-all-start.2 = ((bf16[16,4,16,512]{3,2,1,0:T(8,128)(2,1)}), bf16[16,4,16,512]{3,2,1,0:T(8,128)(2,1)S(1)}, u32[]{:S(2)}, u32[]{:S(2)}) async-start(bf16[16,4,16,512]{3,2,1,0:T(8,128)(2,1)} %bitcast.41), calls=%async_computation.2 | async-start | bytes 2097152 | tf_op jit(solution)/shard_map/all_to_all | solution.py:962
  352.6 3.5 collective-permute-start.60
  361.9 3.1 reshape.147
  365.0 4.6 %collective-permute-done.60 = f32[40,512]{1,0:T(8,128)S(1)} collective-permute-done((f32[40,512]{1,0:T(8,128)S(1)}, f32[40,512]{1,0:T(8,128)S(1)}, u32[]{:S(2)}, u32[]{:S(2)}) %collective-permute-start.60) | collective-permute-done | bytes 81952 | tf_op jit(solution)/shard_map/ppermute | solution.py:687
  371.2 2.7 collective-permute-start.64
  374.5 3.0 shard_map.463
  388.6 2.4 collective-permute-start.57
  390.9 2.5 collective-permute-start.58
  394.2 5.5 %shard_map.465 = (f32[2,6144]{1,0:T(2,128)}, f32[2,6144]{1,0:T(2,128)}, f32[2,6144]{1,0:T(2,128)}, f32[2,169,16]{2,1,0:T(8,128)}, f32[2,169,16]{2,1,0:T(8,128)},...) custom-call(f32[40,512]{1,0:T(8,128)} %add_add_fusion.refs_0_, bf16[512,512]{1,0:T(8,128)(2,1)} %constant.94.clone.refs_5_.refs_9_.refs_1_, ...), custom_call_target="tpu_custom_call" | custom-call | flops 2000000000 | bytes 2000000 | tf_op jit(solution)/shard_map/pallas_call | solution.py:195
  406.1 9.3 %shard_map.464 = (f32[2,16,1536]{2,1,0:T(8,128)}, f32[2,16,1536]{2,1,0:T(8,128)}, f32[2,16,1536]{2,1,0:T(8,128)}, f32[2,16,512]{2,1,0:T(8,128)}, f32[2,16,512]{2...) custom-call(bf16[9,16,512]{2,1,0:T(8,128)(2,1)} %reduce_sum.37.refs_, ...), custom_call_target="tpu_custom_call" | custom-call | flops 20000000000 | bytes 20000000 | tf_op jit(solution)/shard_map/pallas_call | solution.py:732
  (307 shorter events, 92.4 us)
Async XLA Ops:
  3.9 14.0 %collective-permute-start.2 = (bf16[12,16,512]{2,1,0:T(8,128)(2,1)}, bf16[12,16,512]{2,1,0:T(8,128)(2,1)S(1)}, u32[]{:S(2)}, u32[]{:S(2)}) collective-permute-start(bf16[12,16,512]{2,1,0:T(8,128)(2,1)} %get-tuple-element.114.refs_1_), channel_id=1, source_target_pairs={{0,17},{8,25},{1,16},{9,24},{16,1},{24,9},{17,0},{25,8},{32,49},{4... | collective-permute-start | bytes 589832 | tf_op jit(solution)/shard_map/ppermute | solution.py:820
  6.8 12.2 %collective-permute-start.1 = (bf16[12,16,512]{2,1,0:T(8,128)(2,1)}, bf16[12,16,512]{2,1,0:T(8,128)(2,1)S(1)}, u32[]{:S(2)}, u32[]{:S(2)}) collective-permute-start(bf16[12,16,512]{2,1,0:T(8,128)(2,1)} %get-tuple-element.114.refs_1_), channel_id=1, source_target_pairs={{0,16},{8,24},{1,17},{9,25},{16,0},{24,8},{17,1},{25,9},{32,48},{4... | collective-permute-start | bytes 589832 | tf_op jit(solution)/shard_map/ppermute | solution.py:820
  7.0 12.0 %collective-permute-start = (bf16[12,16,512]{2,1,0:T(8,128)(2,1)}, bf16[12,16,512]{2,1,0:T(8,128)(2,1)S(1)}, u32[]{:S(2)}, u32[]{:S(2)}) collective-permute-start(bf16[12,16,512]{2,1,0:T(8,128)(2,1)} %get-tuple-element.114.refs_1_), channel_id=1, source_target_pairs={{0,1},{8,9},{1,0},{9,8},{16,17},{24,25},{17,16},{25,24},{32,33},{4... | collective-permute-start | bytes 589832 | tf_op jit(solution)/shard_map/ppermute | solution.py:820
  8.6 13.6 %collective-permute-start.12 = (bf16[12,16,512]{2,1,0:T(8,128)(2,1)}, bf16[12,16,512]{2,1,0:T(8,128)(2,1)S(1)}, u32[]{:S(2)}, u32[]{:S(2)}) collective-permute-start(bf16[12,16,512]{2,1,0:T(8,128)(2,1)} %get-tuple-element.116.refs_5_), channel_id=1, source_target_pairs={{96,0},{104,8},{112,16},{120,24},{0,32},{8,40},{16,48},{24,56},{32... | collective-permute-start | bytes 589832 | tf_op jit(solution)/shard_map/ppermute | solution.py:821
  10.6 12.3 %collective-permute-start.11 = (bf16[12,16,512]{2,1,0:T(8,128)(2,1)}, bf16[12,16,512]{2,1,0:T(8,128)(2,1)S(1)}, u32[]{:S(2)}, u32[]{:S(2)}) collective-permute-start(bf16[12,16,512]{2,1,0:T(8,128)(2,1)} %get-tuple-element.116.refs_5_), channel_id=1, source_target_pairs={{64,0},{72,8},{80,16},{88,24},{96,32},{104,40},{112,48},{120,56},{... | collective-permute-start | bytes 589832 | tf_op jit(solution)/shard_map/ppermute | solution.py:821
  19.1 15.2 %collective-permute-start.3 = (bf16[4,6,16,512]{3,2,1,0:T(8,128)(2,1)S(1)}, bf16[4,6,16,512]{3,2,1,0:T(8,128)(2,1)}, u32[]{:S(2)}, u32[]{:S(2)}) collective-permute-start(bf16[4,6,16,512]{3,2,1,0:T(8,128)(2,1)S(1)} %pad_maximum_fusion.2.refs_1_), channel_id=1, source_target_pairs={{32,0},{40,8},{48,16},{56,24},{64,32},{72,40},{80,48},{88,56},{96,... | collective-permute-start | bytes 1179656 | tf_op jit(solution)/shard_map/ppermute | solution.py:824
  21.7 13.7 %collective-permute-start.4 = (bf16[4,6,16,512]{3,2,1,0:T(8,128)(2,1)S(1)}, bf16[4,6,16,512]{3,2,1,0:T(8,128)(2,1)}, u32[]{:S(2)}, u32[]{:S(2)}) collective-permute-start(bf16[4,6,16,512]{3,2,1,0:T(8,128)(2,1)S(1)} %pad_maximum_fusion.2.refs_1_), channel_id=1, source_target_pairs={{64,0},{72,8},{80,16},{88,24},{96,32},{104,40},{112,48},{120,56},{... | collective-permute-start | bytes 1179656 | tf_op jit(solution)/shard_map/ppermute | solution.py:824
  22.3 18.6 %collective-permute-start.5 = (bf16[4,6,16,512]{3,2,1,0:T(8,128)(2,1)S(1)}, bf16[4,6,16,512]{3,2,1,0:T(8,128)(2,1)}, u32[]{:S(2)}, u32[]{:S(2)}) collective-permute-start(bf16[4,6,16,512]{3,2,1,0:T(8,128)(2,1)S(1)} %pad_maximum_fusion.2.refs_1_), channel_id=1, source_target_pairs={{96,0},{104,8},{112,16},{120,24},{0,32},{8,40},{16,48},{24,56},{32... | collective-permute-start | bytes 1179656 | tf_op jit(solution)/shard_map/ppermute | solution.py:824
  22.9 17.9 %collective-permute-start.6 = (bf16[4,6,16,512]{3,2,1,0:T(8,128)(2,1)S(1)}, bf16[4,6,16,512]{3,2,1,0:T(8,128)(2,1)}, u32[]{:S(2)}, u32[]{:S(2)}) collective-permute-start(bf16[4,6,16,512]{3,2,1,0:T(8,128)(2,1)S(1)} %pad_maximum_fusion.2.refs_1_), channel_id=1, source_target_pairs={{0,8},{8,0},{16,24},{24,16},{32,40},{40,32},{48,56},{56,48},{64,72... | collective-permute-start | bytes 1179656 | tf_op jit(solution)/shard_map/ppermute | solution.py:683
  26.5 14.9 %collective-permute-start.27 = (bf16[4,6,16,512]{3,2,1,0:T(8,128)(2,1)S(1)}, bf16[4,6,16,512]{3,2,1,0:T(8,128)(2,1)}, u32[]{:S(2)}, u32[]{:S(2)}) collective-permute-start(bf16[4,6,16,512]{3,2,1,0:T(8,128)(2,1)S(1)} %pad_maximum_fusion.3.refs_9_), channel_id=1, source_target_pairs={{0,1},{8,9},{1,0},{9,8},{16,17},{24,25},{17,16},{25,24},{32,33},{4... | collective-permute-start | bytes 1179656 | tf_op jit(solution)/shard_map/ppermute | solution.py:825
  34.3 14.0 %collective-permute-start.28 = (bf16[4,6,16,512]{3,2,1,0:T(8,128)(2,1)S(1)}, bf16[4,6,16,512]{3,2,1,0:T(8,128)(2,1)S(1)}, u32[]{:S(2)}, u32[]{:S(2)}) collective-permute-start(bf16[4,6,16,512]{3,2,1,0:T(8,128)(2,1)S(1)} %pad_maximum_fusion.3.refs_9_), channel_id=1, source_target_pairs={{0,16},{8,24},{1,17},{9,25},{16,0},{24,8},{17,1},{25,9},{32,48},{4... | collective-permute-start | bytes 1179656 | tf_op jit(solution)/shard_map/ppermute | solution.py:825
  35.3 13.5 %collective-permute-start.29 = (bf16[4,6,16,512]{3,2,1,0:T(8,128)(2,1)S(1)}, bf16[4,6,16,512]{3,2,1,0:T(8,128)(2,1)}, u32[]{:S(2)}, u32[]{:S(2)}) collective-permute-start(bf16[4,6,16,512]{3,2,1,0:T(8,128)(2,1)S(1)} %pad_maximum_fusion.3.refs_9_), channel_id=1, source_target_pairs={{0,17},{8,25},{1,16},{9,24},{16,1},{24,9},{17,0},{25,8},{32,49},{4... | collective-permute-start | bytes 1179656 | tf_op jit(solution)/shard_map/ppermute | solution.py:825
  48.3 19.4 %collective-permute-start.30 = (bf16[4,6,16,512]{3,2,1,0:T(8,128)(2,1)S(1)}, bf16[4,6,16,512]{3,2,1,0:T(8,128)(2,1)S(1)}, u32[]{:S(2)}, u32[]{:S(2)}) collective-permute-start(bf16[4,6,16,512]{3,2,1,0:T(8,128)(2,1)S(1)} %pad_maximum_fusion.3.refs_9_), channel_id=1, source_target_pairs={{0,8},{8,0},{16,24},{24,16},{32,40},{40,32},{48,56},{56,48},{64,72... | collective-permute-start | bytes 1179656 | tf_op jit(solution)/shard_map/ppermute | solution.py:683
  48.8 18.9 %collective-permute-start.31 = (bf16[4,6,16,512]{3,2,1,0:T(8,128)(2,1)}, bf16[4,6,16,512]{3,2,1,0:T(8,128)(2,1)S(1)}, u32[]{:S(2)}, u32[]{:S(2)}) collective-permute-start(bf16[4,6,16,512]{3,2,1,0:T(8,128)(2,1)} %collective-permute-done.27.refs_10_), channel_id=1, source_target_pairs={{0,8},{8,0},{16,24},{24,16},{32,40},{40,32},{48,56},{56,48},{64,72... | collective-permute-start | bytes 1179656 | tf_op jit(solution)/shard_map/ppermute | solution.py:683
  48.9 18.9 %collective-permute-start.32 = (bf16[4,6,16,512]{3,2,1,0:T(8,128)(2,1)S(1)}, bf16[4,6,16,512]{3,2,1,0:T(8,128)(2,1)S(1)}, u32[]{:S(2)}, u32[]{:S(2)}) collective-permute-start(bf16[4,6,16,512]{3,2,1,0:T(8,128)(2,1)S(1)} %collective-permute-done.28.refs_11_), channel_id=1, source_target_pairs={{0,8},{8,0},{16,24},{24,16},{32,40},{40,32},{48,56},{56,48},{64,72... | collective-permute-start | bytes 1179656 | tf_op jit(solution)/shard_map/ppermute | solution.py:683
  49.3 18.5 %collective-permute-start.33 = (bf16[4,6,16,512]{3,2,1,0:T(8,128)(2,1)}, bf16[4,6,16,512]{3,2,1,0:T(8,128)(2,1)S(1)}, u32[]{:S(2)}, u32[]{:S(2)}) collective-permute-start(bf16[4,6,16,512]{3,2,1,0:T(8,128)(2,1)} %collective-permute-done.29.refs_12_), channel_id=1, source_target_pairs={{0,8},{8,0},{16,24},{24,16},{32,40},{40,32},{48,56},{56,48},{64,72... | collective-permute-start | bytes 1179656 | tf_op jit(solution)/shard_map/ppermute | solution.py:683
  84.9 15.1 %collective-permute-start.34 = (bf16[96,512]{1,0:T(8,128)(2,1)}, bf16[96,512]{1,0:T(8,128)(2,1)S(1)}, u32[]{:S(2)}, u32[]{:S(2)}) collective-permute-start(bf16[96,512]{1,0:T(8,128)(2,1)} %get-tuple-element.121), channel_id=1, source_target_pairs={{0,6},{2,0},{4,2},{6,4},{1,7},{3,1},{5,3},{7,5},{8,14},{10,8},{12,... | collective-permute-start | bytes 294920 | tf_op jit(solution)/shard_map/ppermute | solution.py:652
  88.0 12.0 %collective-permute-start.35 = (bf16[96,512]{1,0:T(8,128)(2,1)}, bf16[96,512]{1,0:T(8,128)(2,1)S(1)}, u32[]{:S(2)}, u32[]{:S(2)}) collective-permute-start(bf16[96,512]{1,0:T(8,128)(2,1)} %get-tuple-element.122), channel_id=1, source_target_pairs={{0,1},{1,0},{2,3},{3,2},{4,5},{5,4},{6,7},{7,6},{8,9},{9,8},{10,11... | collective-permute-start | bytes 294920 | tf_op jit(solution)/shard_map/ppermute | solution.py:653
  94.4 21.6 %collective-permute-start.13 = (bf16[4,6,16,512]{3,2,1,0:T(8,128)(2,1)}, bf16[4,6,16,512]{3,2,1,0:T(8,128)(2,1)S(1)}, u32[]{:S(2)}, u32[]{:S(2)}) collective-permute-start(bf16[4,6,16,512]{3,2,1,0:T(8,128)(2,1)} %get-tuple-element.117.refs_1_), channel_id=1, source_target_pairs={{32,0},{40,8},{48,16},{56,24},{64,32},{72,40},{80,48},{88,56},{96,... | collective-permute-start | bytes 1179656 | tf_op jit(solution)/shard_map/ppermute | solution.py:824
  99.1 16.9 %collective-permute-start.14 = (bf16[4,6,16,512]{3,2,1,0:T(8,128)(2,1)}, bf16[4,6,16,512]{3,2,1,0:T(8,128)(2,1)S(1)}, u32[]{:S(2)}, u32[]{:S(2)}) collective-permute-start(bf16[4,6,16,512]{3,2,1,0:T(8,128)(2,1)} %get-tuple-element.117.refs_1_), channel_id=1, source_target_pairs={{64,0},{72,8},{80,16},{88,24},{96,32},{104,40},{112,48},{120,56},{... | collective-permute-start | bytes 1179656 | tf_op jit(solution)/shard_map/ppermute | solution.py:824
  99.7 19.8 %collective-permute-start.15 = (bf16[4,6,16,512]{3,2,1,0:T(8,128)(2,1)}, bf16[4,6,16,512]{3,2,1,0:T(8,128)(2,1)S(1)}, u32[]{:S(2)}, u32[]{:S(2)}) collective-permute-start(bf16[4,6,16,512]{3,2,1,0:T(8,128)(2,1)} %get-tuple-element.117.refs_1_), channel_id=1, source_target_pairs={{96,0},{104,8},{112,16},{120,24},{0,32},{8,40},{16,48},{24,56},{32... | collective-permute-start | bytes 1179656 | tf_op jit(solution)/shard_map/ppermute | solution.py:824
  100.0 19.5 %collective-permute-start.16 = (bf16[4,6,16,512]{3,2,1,0:T(8,128)(2,1)}, bf16[4,6,16,512]{3,2,1,0:T(8,128)(2,1)}, u32[]{:S(2)}, u32[]{:S(2)}) collective-permute-start(bf16[4,6,16,512]{3,2,1,0:T(8,128)(2,1)} %get-tuple-element.117.refs_1_), channel_id=1, source_target_pairs={{0,8},{8,0},{16,24},{24,16},{32,40},{40,32},{48,56},{56,48},{64,72... | collective-permute-start | bytes 1179656 | tf_op jit(solution)/shard_map/ppermute | solution.py:683
  100.0 20.0 %collective-permute-start.20 = (bf16[4,6,16,512]{3,2,1,0:T(8,128)(2,1)}, bf16[4,6,16,512]{3,2,1,0:T(8,128)(2,1)}, u32[]{:S(2)}, u32[]{:S(2)}) collective-permute-start(bf16[4,6,16,512]{3,2,1,0:T(8,128)(2,1)} %get-tuple-element.118.refs_9_), channel_id=1, source_target_pairs={{0,1},{8,9},{1,0},{9,8},{16,17},{24,25},{17,16},{25,24},{32,33},{4... | collective-permute-start | bytes 1179656 | tf_op jit(solution)/shard_map/ppermute | solution.py:825
  123.8 22.6 %collective-permute-start.23 = (bf16[4,6,16,512]{3,2,1,0:T(8,128)(2,1)S(1)}, bf16[4,6,16,512]{3,2,1,0:T(8,128)(2,1)S(1)}, u32[]{:S(2)}, u32[]{:S(2)}) collective-permute-start(bf16[4,6,16,512]{3,2,1,0:T(8,128)(2,1)S(1)} %copy-done.32), channel_id=1, source_target_pairs={{0,8},{8,0},{16,24},{24,16},{32,40},{40,32},{48,56},{56,48},{64,72... | collective-permute-start | bytes 1179656 | tf_op jit(solution)/shard_map/ppermute | solution.py:683
  125.1 23.4 %collective-permute-start.24 = (bf16[4,6,16,512]{3,2,1,0:T(8,128)(2,1)}, bf16[4,6,16,512]{3,2,1,0:T(8,128)(2,1)S(1)}, u32[]{:S(2)}, u32[]{:S(2)}) collective-permute-start(bf16[4,6,16,512]{3,2,1,0:T(8,128)(2,1)} %collective-permute-done.20.refs_10_), channel_id=1, source_target_pairs={{0,8},{8,0},{16,24},{24,16},{32,40},{40,32},{48,56},{56,48},{64,72... | collective-permute-start | bytes 1179656 | tf_op jit(solution)/shard_map/ppermute | solution.py:683
  125.1 26.7 %collective-permute-start.25 = (bf16[4,6,16,512]{3,2,1,0:T(8,128)(2,1)}, bf16[4,6,16,512]{3,2,1,0:T(8,128)(2,1)}, u32[]{:S(2)}, u32[]{:S(2)}) collective-permute-start(bf16[4,6,16,512]{3,2,1,0:T(8,128)(2,1)} %collective-permute-done.21.refs_11_), channel_id=1, source_target_pairs={{0,8},{8,0},{16,24},{24,16},{32,40},{40,32},{48,56},{56,48},{64,72... | collective-permute-start | bytes 1179656 | tf_op jit(solution)/shard_map/ppermute | solution.py:683
  125.6 26.2 %collective-permute-start.26 = (bf16[4,6,16,512]{3,2,1,0:T(8,128)(2,1)}, bf16[4,6,16,512]{3,2,1,0:T(8,128)(2,1)}, u32[]{:S(2)}, u32[]{:S(2)}) collective-permute-start(bf16[4,6,16,512]{3,2,1,0:T(8,128)(2,1)} %collective-permute-done.22.refs_12_), channel_id=1, source_target_pairs={{0,8},{8,0},{16,24},{24,16},{32,40},{40,32},{48,56},{56,48},{64,72... | collective-permute-start | bytes 1179656 | tf_op jit(solution)/shard_map/ppermute | solution.py:683
  145.1 11.4 %collective-permute-start.37 = (bf16[96,512]{1,0:T(8,128)(2,1)}, bf16[96,512]{1,0:T(8,128)(2,1)S(1)}, u32[]{:S(2)}, u32[]{:S(2)}) collective-permute-start(bf16[96,512]{1,0:T(8,128)(2,1)} %get-tuple-element.125), channel_id=1, source_target_pairs={{0,2},{2,4},{4,6},{6,0},{1,3},{3,5},{5,7},{7,1},{8,10},{10,12},{12... | collective-permute-start | bytes 294920 | tf_op jit(solution)/shard_map/ppermute | solution.py:652
  194.7 19.2 %collective-permute-start.44 = (bf16[96,512]{1,0:T(8,128)(2,1)S(1)}, bf16[96,512]{1,0:T(8,128)(2,1)S(1)}, u32[]{:S(2)}, u32[]{:S(2)}) collective-permute-start(bf16[96,512]{1,0:T(8,128)(2,1)S(1)} %copy-done.51), channel_id=1, source_target_pairs={{0,6},{2,0},{4,2},{6,4},{1,7},{3,1},{5,3},{7,5},{8,14},{10,8},{12,... | collective-permute-start | bytes 294920 | tf_op jit(solution)/shard_map/ppermute | solution.py:652
  195.5 18.5 %collective-permute-start.45 = (bf16[96,512]{1,0:T(8,128)(2,1)S(1)}, bf16[96,512]{1,0:T(8,128)(2,1)S(1)}, u32[]{:S(2)}, u32[]{:S(2)}) collective-permute-start(bf16[96,512]{1,0:T(8,128)(2,1)S(1)} %copy-done.50), channel_id=1, source_target_pairs={{0,1},{1,0},{2,3},{3,2},{4,5},{5,4},{6,7},{7,6},{8,9},{9,8},{10,11... | collective-permute-start | bytes 294920 | tf_op jit(solution)/shard_map/ppermute | solution.py:653
  196.9 17.0 %collective-permute-start.46 = (bf16[16,512]{1,0:T(8,128)(2,1)S(1)}, bf16[16,512]{1,0:T(8,128)(2,1)S(1)}, u32[]{:S(2)}, u32[]{:S(2)}) collective-permute-start(bf16[16,512]{1,0:T(8,128)(2,1)S(1)} %copy-done.58), channel_id=1, source_target_pairs={{0,7},{1,6},{2,1},{3,0},{4,3},{5,2},{6,5},{7,4},{8,15},{9,14},{10,... | collective-permute-start | bytes 49160 | tf_op jit(solution)/shard_map/ppermute | solution.py:654
  208.4 35.0 %all-to-all-start = ((bf16[4,4,9,16,512]{4,3,2,1,0:T(8,128)(2,1)}), bf16[4,4,9,16,512]{4,3,2,1,0:T(8,128)(2,1)S(1)}, u32[]{:S(2)}, u32[]{:S(2)}) async-start(bf16[4,4,9,16,512]{4,3,2,1,0:T(8,128)(2,1)} %shard_map.454.refs_0_), calls=%async_computation | async-start | bytes 4718592 | tf_op jit(solution)/shard_map/all_to_all | solution.py:679
  236.9 12.7 %collective-permute-start.47 = (bf16[96,512]{1,0:T(8,128)(2,1)}, bf16[96,512]{1,0:T(8,128)(2,1)S(1)}, u32[]{:S(2)}, u32[]{:S(2)}) collective-permute-start(bf16[96,512]{1,0:T(8,128)(2,1)} %get-tuple-element.148), channel_id=1, source_target_pairs={{0,2},{2,4},{4,6},{6,0},{1,3},{3,5},{5,7},{7,1},{8,10},{10,12},{12... | collective-permute-start | bytes 294920 | tf_op jit(solution)/shard_map/ppermute | solution.py:652
  266.6 30.2 %collective-permute-start.50 = (bf16[4,4,8,16,512]{4,3,2,1,0:T(8,128)(2,1)}, bf16[4,4,8,16,512]{4,3,2,1,0:T(8,128)(2,1)S(1)}, u32[]{:S(2)}, u32[]{:S(2)}) collective-permute-start(bf16[4,4,8,16,512]{4,3,2,1,0:T(8,128)(2,1)} %get-tuple-element.162), channel_id=1, source_target_pairs={{0,8},{8,0},{16,24},{24,16},{32,40},{40,32},{48,56},{56,48},{64,72... | collective-permute-start | bytes 6291464 | tf_op jit(solution)/shard_map/ppermute | solution.py:683
  266.6 14.3 %all-to-all-start.1 = ((bf16[4,9,16,512]{3,2,1,0:T(8,128)(2,1)}), bf16[4,9,16,512]{3,2,1,0:T(8,128)(2,1)S(1)}, u32[]{:S(2)}, u32[]{:S(2)}) async-start(bf16[4,9,16,512]{3,2,1,0:T(8,128)(2,1)} %reduce_sum.36.refs_0_), calls=%async_computation.1 | async-start | bytes 1179648 | tf_op jit(solution)/shard_map/all_to_all | solution.py:675
  275.3 21.4 %collective-permute-start.51 = (bf16[4,4,3,16,512]{4,3,2,1,0:T(8,128)(2,1)}, bf16[4,4,3,16,512]{4,3,2,1,0:T(8,128)(2,1)S(1)}, u32[]{:S(2)}, u32[]{:S(2)}) collective-permute-start(bf16[4,4,3,16,512]{4,3,2,1,0:T(8,128)(2,1)} %get-tuple-element.166), channel_id=1, source_target_pairs={{0,8},{8,0},{16,24},{24,16},{32,40},{40,32},{48,56},{56,48},{64,72... | collective-permute-start | bytes 2359304 | tf_op jit(solution)/shard_map/ppermute | solution.py:683
  281.6 35.5 %collective-permute-start.41 = (bf16[9,16,512]{2,1,0:T(8,128)(2,1)}, bf16[9,16,512]{2,1,0:T(8,128)(2,1)}, u32[]{:S(2)}, u32[]{:S(2)}) collective-permute-start(bf16[9,16,512]{2,1,0:T(8,128)(2,1)} %reduce_sum.37.refs_0_), channel_id=1, source_target_pairs={{0,2},{2,0},{4,6},{6,4},{1,3},{3,1},{5,7},{7,5},{8,10},{10,8},{12,... | collective-permute-start | bytes 442376 | tf_op jit(solution)/shard_map/ppermute | solution.py:719
  281.7 35.4 %collective-permute-start.42 = (bf16[9,16,512]{2,1,0:T(8,128)(2,1)}, bf16[9,16,512]{2,1,0:T(8,128)(2,1)}, u32[]{:S(2)}, u32[]{:S(2)}) collective-permute-start(bf16[9,16,512]{2,1,0:T(8,128)(2,1)} %reduce_sum.37.refs_0_), channel_id=1, source_target_pairs={{0,4},{2,6},{4,0},{6,2},{1,5},{3,7},{5,1},{7,3},{8,12},{10,14},{12... | collective-permute-start | bytes 442376 | tf_op jit(solution)/shard_map/ppermute | solution.py:719
  283.2 33.9 %collective-permute-start.43 = (bf16[9,16,512]{2,1,0:T(8,128)(2,1)}, bf16[9,16,512]{2,1,0:T(8,128)(2,1)}, u32[]{:S(2)}, u32[]{:S(2)}) collective-permute-start(bf16[9,16,512]{2,1,0:T(8,128)(2,1)} %reduce_sum.37.refs_0_), channel_id=1, source_target_pairs={{0,6},{2,4},{4,2},{6,0},{1,7},{3,5},{5,3},{7,1},{8,14},{10,12},{12... | collective-permute-start | bytes 442376 | tf_op jit(solution)/shard_map/ppermute | solution.py:719
  303.1 40.6 %all-to-all-start.3 = ((bf16[4,4,11,16,512]{4,3,2,1,0:T(8,128)(2,1)}), bf16[4,4,11,16,512]{4,3,2,1,0:T(8,128)(2,1)S(1)}, u32[]{:S(2)}, u32[]{:S(2)}) async-start(bf16[4,4,11,16,512]{4,3,2,1,0:T(8,128)(2,1)} %shard_map.459.refs_0_), calls=%async_computation.3 | async-start | bytes 5767168 | tf_op jit(solution)/shard_map/all_to_all | solution.py:679
  345.3 37.9 %all-to-all-start.2 = ((bf16[16,4,16,512]{3,2,1,0:T(8,128)(2,1)}), bf16[16,4,16,512]{3,2,1,0:T(8,128)(2,1)S(1)}, u32[]{:S(2)}, u32[]{:S(2)}) async-start(bf16[16,4,16,512]{3,2,1,0:T(8,128)(2,1)} %bitcast.41), calls=%async_computation.2 | async-start | bytes 2097152 | tf_op jit(solution)/shard_map/all_to_all | solution.py:962
  352.6 17.1 %collective-permute-start.60 = (f32[40,512]{1,0:T(8,128)S(1)}, f32[40,512]{1,0:T(8,128)S(1)}, u32[]{:S(2)}, u32[]{:S(2)}) collective-permute-start(f32[40,512]{1,0:T(8,128)S(1)} %add.73), channel_id=1, source_target_pairs={{0,1},{8,9},{1,0},{9,8},{16,17},{24,25},{17,16},{25,24},{32,33},{4... | collective-permute-start | bytes 245768 | tf_op jit(solution)/shard_map/ppermute | solution.py:687
  356.1 13.6 %collective-permute-start.61 = (f32[40,512]{1,0:T(8,128)S(1)}, f32[40,512]{1,0:T(8,128)S(1)}, u32[]{:S(2)}, u32[]{:S(2)}) collective-permute-start(f32[40,512]{1,0:T(8,128)S(1)} %add.73), channel_id=1, source_target_pairs={{0,16},{8,24},{1,17},{9,25},{16,0},{24,8},{17,1},{25,9},{32,48},{4... | collective-permute-start | bytes 245768 | tf_op jit(solution)/shard_map/ppermute | solution.py:687
  356.8 12.9 %collective-permute-start.62 = (f32[40,512]{1,0:T(8,128)S(1)}, f32[40,512]{1,0:T(8,128)S(1)}, u32[]{:S(2)}, u32[]{:S(2)}) collective-permute-start(f32[40,512]{1,0:T(8,128)S(1)} %add.73), channel_id=1, source_target_pairs={{0,17},{8,25},{1,16},{9,24},{16,1},{24,9},{17,0},{25,8},{32,49},{4... | collective-permute-start | bytes 245768 | tf_op jit(solution)/shard_map/ppermute | solution.py:687
  381.7 11.8 %collective-permute-start.67 = (f32[40,512]{1,0:T(8,128)S(1)}, f32[40,512]{1,0:T(8,128)S(1)}, u32[]{:S(2)}, u32[]{:S(2)}) collective-permute-start(f32[40,512]{1,0:T(8,128)S(1)} %add_add_fusion.1), channel_id=1, source_target_pairs={{0,4},{2,6},{4,0},{6,2},{1,5},{3,7},{5,1},{7,3},{8,12},{10,14},{12... | collective-permute-start | bytes 245768 | tf_op jit(solution)/shard_map/ppermute | solution.py:687
  388.5 16.1 %collective-permute-start.56 = (bf16[15,16,512]{2,1,0:T(8,128)(2,1)S(1)}, bf16[15,16,512]{2,1,0:T(8,128)(2,1)S(1)}, u32[]{:S(2)}, u32[]{:S(2)}) collective-permute-start(bf16[15,16,512]{2,1,0:T(8,128)(2,1)S(1)} %pad_maximum_fusion.4.refs_4_), channel_id=1, source_target_pairs={{0,2},{2,0},{4,6},{6,4},{1,3},{3,1},{5,7},{7,5},{8,10},{10,8},{12,... | collective-permute-start | bytes 737288 | tf_op jit(solution)/shard_map/ppermute | solution.py:719
  388.6 16.0 %collective-permute-start.57 = (bf16[15,16,512]{2,1,0:T(8,128)(2,1)S(1)}, bf16[15,16,512]{2,1,0:T(8,128)(2,1)S(1)}, u32[]{:S(2)}, u32[]{:S(2)}) collective-permute-start(bf16[15,16,512]{2,1,0:T(8,128)(2,1)S(1)} %pad_maximum_fusion.4.refs_4_), channel_id=1, source_target_pairs={{0,4},{2,6},{4,0},{6,2},{1,5},{3,7},{5,1},{7,3},{8,12},{10,14},{12... | collective-permute-start | bytes 737288 | tf_op jit(solution)/shard_map/ppermute | solution.py:719
  390.9 13.6 %collective-permute-start.58 = (bf16[15,16,512]{2,1,0:T(8,128)(2,1)S(1)}, bf16[15,16,512]{2,1,0:T(8,128)(2,1)S(1)}, u32[]{:S(2)}, u32[]{:S(2)}) collective-permute-start(bf16[15,16,512]{2,1,0:T(8,128)(2,1)S(1)} %pad_maximum_fusion.4.refs_4_), channel_id=1, source_target_pairs={{0,6},{2,4},{4,2},{6,0},{1,7},{3,5},{5,3},{7,1},{8,14},{10,12},{12... | collective-permute-start | bytes 737288 | tf_op jit(solution)/shard_map/ppermute | solution.py:719
  (86 other events, 881.6 us)

commit v2 on v1

v2 whole, which is shorter than its diff:
```python
import functools
import math

import jax
import jax.numpy as jnp
import numpy as np
from jax import lax
from jax.experimental import pallas as pl
from jax.experimental.pallas import tpu as pltpu
from jax.sharding import PartitionSpec as P

D = 512
HEADS = 16
HEAD_DIM = 32
WIN = 7
SHIFT = 3
LAYERS = 2
STEP = 10
REL = 169
SIDE = 28
CELLS = SIDE * SIDE
AREA = WIN * WIN
SLOT = 64
PADDED = 16 * SLOT
PAIRS = 8
GROUPS = 4
SLAB = 96
CORNER = 16
HALO = 2 * SLAB + CORNER
HIDDEN = 4 * D

BF = jnp.bfloat16
F32 = jnp.float32
epsilon = 1e-05
log2e = math.log2(math.e)
masked_score = -1000000000.0 * log2e
padded_score = -1e30
highest = lax.Precision.HIGHEST
VMEM_BYTES = 58 * 2**20


def padded_row(r, c):
    return ((r // WIN) * 4 + c // WIN) * SLOT + (r % WIN) * WIN + c % WIN


def ahead_source(r, c):
    r, c = r + SHIFT, c + SHIFT
    if r < SIDE and c < SIDE:
        return r * SIDE + c
    if c < SIDE:
        return CELLS + (r - SIDE) * SIDE + c
    if r < SIDE:
        return CELLS + SLAB + r * SHIFT + c - SIDE
    return CELLS + 2 * SLAB + (r - SIDE) * SHIFT + c - SIDE


def back_source(r, c):
    if r >= SHIFT and c >= SHIFT:
        return padded_row(r - SHIFT, c - SHIFT)
    if c >= SHIFT:
        return PADDED + r * SIDE + c - SHIFT
    if r >= SHIFT:
        return PADDED + SLAB + (r - SHIFT) * SHIFT + c
    return PADDED + 2 * SLAB + r * SHIFT + c


def placements():
    plain = np.zeros((PADDED, CELLS), np.float32)
    ahead = np.zeros((PADDED, CELLS + HALO), np.float32)
    back = np.zeros((CELLS, PADDED + HALO), np.float32)
    take_first = np.zeros((HALO, CELLS), np.float32)
    take_last = np.zeros((HALO, PADDED), np.float32)
    for r in range(SIDE):
        for c in range(SIDE):
            plain[padded_row(r, c), r * SIDE + c] = 1
            ahead[padded_row(r, c), ahead_source(r, c)] = 1
            back[r * SIDE + c, back_source(r, c)] = 1
    edge = SIDE - SHIFT
    for a in range(SHIFT):
        for b in range(SIDE):
            take_first[a * SIDE + b, a * SIDE + b] = 1
            take_first[SLAB + b * SHIFT + a, b * SIDE + a] = 1
            take_last[a * SIDE + b, padded_row(edge + a, b)] = 1
            take_last[SLAB + b * SHIFT + a, padded_row(b, edge + a)] = 1
        for b in range(SHIFT):
            take_first[2 * SLAB + a * SHIFT + b, a * SIDE + b] = 1
            take_last[2 * SLAB + a * SHIFT + b, padded_row(edge + a, edge + b)] = 1
    return (plain, plain.T.copy(), ahead, back, take_first, take_last)


def column_orders():
    heads = np.zeros((384, 384), np.float32)
    units = np.zeros((512, 512), np.float32)
    for n in range(4):
        for part in range(3):
            for d in range(HEAD_DIM):
                heads[n * 96 + part * 32 + d, part * 128 + n * 32 + d] = 1
    for r in range(8):
        for b in range(4):
            for i in range(16):
                units[r * 64 + b * 16 + i, b * 128 + r * 16 + i] = 1
    return heads, units


def dot(a, b):
    return lax.dot_general(a, b, (((1,), (0,)), ((), ())), preferred_element_type=F32)


def dot_nt(a, b):
    return lax.dot_general(a, b, (((1,), (1,)), ((), ())), preferred_element_type=F32)


def dot_tn(a, b):
    return lax.dot_general(a, b, (((0,), (0,)), ((), ())), preferred_element_type=F32)


def normalized(x):
    centred = x - jnp.mean(x, -1, keepdims=True)
    inverse = lax.rsqrt(jnp.mean(centred * centred, -1, keepdims=True) + epsilon)
    return centred * inverse, inverse


def norm_back(grad, x, gain):
    hat, inverse = normalized(x)
    grad_hat = grad * gain
    grad_x = inverse * (
        grad_hat
        - jnp.mean(grad_hat, -1, keepdims=True)
        - hat * jnp.mean(grad_hat * hat, -1, keepdims=True)
    )
    return grad_x, jnp.sum(grad * hat, 0, keepdims=True), jnp.sum(grad, 0, keepdims=True)


def gelu_both(u):
    a = jnp.abs(u)
    t = 1.0 / (1.0 + (0.3275911 * 0.5**0.5) * a)
    e = jnp.exp2((-0.5 * log2e) * u * u)
    poly = t * (
        0.5 * 0.254829592
        + t * (0.5 * -0.284496736 + t * (0.5 * 1.421413741 + t * (0.5 * -1.453152027 + t * (0.5 * 1.061405429))))
    )
    tail = poly * e
    phi = jnp.where(u >= 0, 1.0 - tail, tail)
    return u * phi, phi + u * e * (1.0 / math.sqrt(2 * math.pi))


def head_rows(pair):
    lane = lax.broadcasted_iota(jnp.int32, pair.shape, 1) % 128 // HEAD_DIM
    zero = jnp.zeros_like(pair)
    return jnp.concatenate([jnp.where(lane == h, pair, zero) for h in range(4)], 0)


def head_fold(rows):
    lane = lax.broadcasted_iota(jnp.int32, (SLOT, 256), 1) % 128 // HEAD_DIM
    out = rows[:SLOT]
    for h in range(1, 4):
        out = jnp.where(lane == h, rows[h * SLOT : (h + 1) * SLOT], out)
    return out


def side_by_side(ref, start, lane):
    return jnp.concatenate(
        [ref[pl.ds(start, SLOT), lane : lane + 128], ref[pl.ds(start + SLOT, SLOT), lane : lane + 128]], 1
    )


def block_diagonal(pair):
    lane = lax.broadcasted_iota(jnp.int32, pair.shape, 1)
    zero = jnp.zeros_like(pair)
    return jnp.concatenate([jnp.where(lane < 128, pair, zero), jnp.where(lane >= 128, pair, zero)], 0)


def store_diagonal(ref, start, lane, rows):
    ref[pl.ds(start, SLOT), lane : lane + 128] = rows[:SLOT, :128].astype(ref.dtype)
    ref[pl.ds(start + SLOT, SLOT), lane : lane + 128] = rows[SLOT:, 128:].astype(ref.dtype)


class Moves:
    def __init__(self, sems):
        self.loads, self.stores, self.started, self.sems = {}, {}, [], sems

    def load(self, pairs, buffer):
        at = len(self.started)
        for source, target in pairs:
            copy = pltpu.make_async_copy(source, target, self.sems.at[len(self.started)])
            copy.start()
            self.started.append(copy)
        self.loads[id(buffer)] = range(at, len(self.started))

    def need(self, *refs, part=None):
        for ref in refs:
            places = self.loads.get(id(ref), ())
            for at in places if part is None else places[part : part + 1]:
                if self.started[at] is not None:
                    self.started[at].wait()
                    self.started[at] = None

    def ship(self, ref, at=()):
        if id(ref) in self.stores:
            copy = pltpu.make_async_copy(
                ref.at[at] if at else ref,
                self.stores[id(ref)].at[at] if at else self.stores[id(ref)],
                self.sems.at[len(self.started)],
            )
            copy.start()
            self.started.append(copy)

    def finish(self):
        for copy in self.started:
            if copy is not None:
                copy.wait()


def columns(b):
    return (slice(None), slice(b * D, (b + 1) * D))


def of_blocks(b):
    return (slice(None), slice(None), b)


def call(body, outs, args, scratch=(), pieces=(), place=None, us=1, after=(), late=None, early=()):
    shapes = [jax.ShapeDtypeStruct(s, d) for s, d in outs]
    late = late or {}
    lead = [] if place is None else [place]
    anywhere, inside = pl.BlockSpec(memory_space=pl.ANY), pl.BlockSpec(memory_space=pltpu.VMEM)
    specs = [anywhere] * len(after) + [pl.BlockSpec(memory_space=pltpu.SMEM)] * len(lead) + [anywhere] * len(pieces)
    specs += [anywhere if i in late else inside for i in range(len(args))]
    buffers = []
    for i, parts in late.items():
        rows = parts[1:] if isinstance(parts, tuple) else args[i].shape[:1]
        buffers.append(pltpu.VMEM((*rows, *args[i].shape[1:]), args[i].dtype))
    buffers += [pltpu.VMEM(*outs[i]) for i in early]
    moving = bool(buffers)
    if moving:
        buffers.append(pltpu.SemaphoreType.DMA((96,)))

    def whole(*refs):
        refs = refs[len(after) :]
        first, n_in = len(lead) + len(pieces), len(lead) + len(pieces) + len(args)
        ins, results = list(refs[:n_in]), list(refs[n_in : n_in + len(outs)])
        rest = refs[n_in + len(outs) :]
        if not moving:
            body(*refs)
            return
        own, buffer = rest[: len(scratch)], rest[len(scratch) :]
        moves = Moves(buffer[-1])
        for (i, parts), target in zip(late.items(), buffer):
            source = ins[first + i]
            if parts is None:
                pairs = [(source, target)]
            elif isinstance(parts, tuple):
                pairs = [(source.at[pl.ds(*parts)], target)]
            else:
                pairs = [(source.at[part], target.at[part]) for part in parts]
            moves.load(pairs, target)
            ins[first + i] = target
        for i, source in zip(early, buffer[len(late) :]):
            moves.stores[id(source)] = results[i]
            results[i] = source
        body(moves, *ins, *results, *own)
        moves.finish()

    return pl.pallas_call(
        whole,
        out_shape=shapes,
        in_specs=specs,
        out_specs=[anywhere if i in early else inside for i in range(len(outs))],
        scratch_shapes=list(scratch) + buffers,
        compiler_params=pltpu.CompilerParams(vmem_limit_bytes=VMEM_BYTES),
        cost_estimate=pl.CostEstimate(flops=us * 3 * 10**9, bytes_accessed=us * 10**6, transcendentals=0),
    )(*after, *lead, *pieces, *args)


def held(arrays, after):
    anywhere = pl.BlockSpec(memory_space=pl.ANY)
    return pl.pallas_call(
        lambda *refs: None,
        out_shape=[jax.ShapeDtypeStruct(a.shape, a.dtype) for a in arrays],
        in_specs=[anywhere] * (len(arrays) + len(after)),
        out_specs=[anywhere] * len(arrays),
        input_output_aliases={i: i for i in range(len(arrays))},
    )(*arrays, *after)


def owner_of(z, x, core):
    return z * 8 + (x % 2) * 4 + core * 2 + x // 2


def assembly(coords_ref, sets, w_ref, sems):
    z, x, core = coords_ref[0], coords_ref[1], coords_ref[2]
    copies = []
    for pieces, far, (low, count), first in sets:
        for k, piece in enumerate(pieces):
            from_core = core if k < len(pieces) // 2 else 1 - core
            for i in range(piece.shape[0]):
                if far == "zx":
                    owner = owner_of(i // 4, i % 4, from_core)
                elif far == "z":
                    owner = owner_of(i // 4, lax.rem(x + i % 4, 4), from_core)
                elif far == "by z":
                    owner = owner_of(lax.rem(z + k % 4, 4), i, from_core)
                else:
                    owner = owner_of(lax.rem(z + i, 4), lax.rem(x + k % 4, 4), from_core)
                source, target = piece.at[i, pl.ds(low, count)], w_ref.at[pl.ds(first, count), owner]
                copies.append(pltpu.make_async_copy(source, target, sems.at[len(copies)]))
    for c in copies:
        c.start()
    return copies


def block(ref, b):
    return ref[b].reshape(D, D)


def block_lanes(ref, b, lanes):
    return ref[b, :, :, lanes].reshape(D, lanes.stop - lanes.start)


def block_rows(ref, b, half):
    return ref[b, half * 16 : half * 16 + 16].reshape(256, D)


def store_grad(place_ref, keep_ref, send_ref, b, half, rows):
    first = place_ref[2] == 0
    rows = rows.astype(BF)
    for zz in range(2):
        for x in range(4):
            base = (zz * 8 + (x % 2) * 4 + x // 2) * 16
            one, two = rows[base : base + 16], rows[base + 32 : base + 48]
            keep_ref[half * 2 + zz, x, b] = jnp.where(first, one, two)
            send_ref[half * 2 + zz, x, b] = jnp.where(first, two, one)


def pack_blocks(layer, qkv_ref, proj_ref, expand_ref, contract_ref, heads_ref, units_ref, store):
    every = slice(None)
    store(3, every, proj_ref[layer].astype(BF))
    for b in range(4):
        store(8 + b, every, contract_ref[layer, 16 * b : 16 * b + 16, :].astype(BF))
    for g in range(GROUPS):
        lanes = slice(128 * g, 128 * g + 128)
        part = dot(qkv_ref[layer, :, 384 * g : 384 * g + 384].astype(BF), heads_ref[...]).astype(BF)
        for s in range(3):
            store(s, lanes, part[:, 128 * s : 128 * s + 128])
        part = dot(expand_ref[layer, :, 512 * g : 512 * g + 512].astype(BF), units_ref[...]).astype(BF)
        for b in range(4):
            store(4 + b, lanes, part[:, 128 * b : 128 * b + 128])


def pack_kernel(*refs):
    one_ref, two_ref = refs[6:]

    def store(b, lanes, value):
        if b < 6:
            for i in range(4):
                one_ref[i, b, :, lanes] = value
        else:
            two_ref[b - 6, :, lanes] = value

    pack_blocks(0, *refs[:6], store)


def pack_next_kernel(*refs):
    spread_ref, rest_ref = refs[6:]

    def store(b, lanes, value):
        if b < 3:
            for i in range(16):
                spread_ref[i, b, :, lanes] = value
        else:
            rest_ref[b - 3, :, lanes] = value

    pack_blocks(1, *refs[:6], store)


def stack_kernel(*refs):
    for k in range(4):
        refs[4][k] = refs[k][...]


def stack_spread_kernel(*refs):
    for k in range(4):
        for x in range(4):
            refs[4][x, k] = refs[k][...]


def enter_kernel(x_ref, gain_ref, bias_ref, place_ref, hp_ref):
    hat, _ = normalized(x_ref[...].astype(F32))
    h = (hat * gain_ref[...] + bias_ref[...]).astype(BF)
    hp_ref[...] = dot(place_ref[...], h).astype(BF)


def attend_pairs(qkv_ref, first, table_ref, mask_ref, attn_ref, into_ref):
    def one_pair(p, carry):
        start = pl.multiple_of(first + p * 128, 128)
        for g in range(GROUPS):
            lane = g * 128
            keys = head_rows(side_by_side(qkv_ref, start, D + lane))
            queries = block_diagonal(side_by_side(qkv_ref, start, lane))
            scores = dot_nt(keys, queries) * (HEAD_DIM**-0.5 * log2e) + table_ref[g * 256 : (g + 1) * 256, :]
            scores = scores.reshape(4, SLOT, 128)
            if mask_ref is not None:
                scores = jnp.where(mask_ref[p][None] > 0, scores, masked_score)
            scores = jnp.exp2(scores - jnp.max(scores, 1, keepdims=True))
            scores = scores * (1.0 / jnp.sum(scores, 1, keepdims=True))
            attn = scores.reshape(256, 128).astype(BF)
            attn_ref[p, g] = attn
            values = head_rows(side_by_side(qkv_ref, start, 2 * D + lane))
            store_diagonal(into_ref, pl.multiple_of(p * 128, 128), lane, dot_tn(attn, values))
        return carry

    lax.fori_loop(0, PAIRS // 2, one_pair, 0)


def attend_kernel(shifted, moves, *refs):
    count = 2 if shifted else 8
    coords_ref, pieces, refs = refs[0], refs[1 : count + 1], refs[count + 1 :]
    if shifted:
        h_ref, rows_ref, cols_ref, corner_ref, place_ref, bias_ref, table_ref, mask_ref, take_ref = refs[:9]
        w_ref, hp_ref, qkv_ref, one_ref, two_ref, ctxp_ref, rows_out, cols_out, corner_out, sems = refs[9:]
        copies = assembly(coords_ref, [(pieces, "zx", (0, 3), 0)], w_ref, sems)
        moves.need(place_ref, h_ref)
        place = place_ref[...]
        hp = dot(place[:, :CELLS], h_ref[...])
        slabs = jnp.concatenate([rows_ref[...], cols_ref[...], corner_ref[...]], 0)
        hp_ref[...] = (hp + dot(place[:, CELLS:], slabs)).astype(BF)
        moves.ship(hp_ref)
    else:
        hp_ref, bias_ref, table_ref, place_ref = refs[:4]
        w_ref, qkv_ref, one_ref, two_ref, ctx_ref, ctxp_ref, sems = refs[4:]
        mask_ref = None
        copies = assembly(coords_ref, [(pieces, "by z", (0, 3), 0)], w_ref, sems)
        moves.need(hp_ref)
    for c in copies:
        c.wait()
    moves.ship(w_ref)
    for s in range(3):
        for half in range(2):
            lanes = slice(half * 256, half * 256 + 256)
            wide = slice(s * D + half * 256, s * D + half * 256 + 256)
            qkv_ref[:, wide] = (dot(hp_ref[...], block_lanes(w_ref, s, lanes)) + bias_ref[:, wide]).astype(BF)
        moves.ship(qkv_ref, columns(s))
    upper = PADDED // 2
    masks = (None, None) if mask_ref is None else (mask_ref.at[:4], mask_ref.at[4:])
    moves.need(table_ref)
    if shifted:
        moves.need(mask_ref)
    attend_pairs(qkv_ref, 0, table_ref, masks[0], one_ref, ctxp_ref.at[:upper])
    moves.ship(one_ref)
    attend_pairs(qkv_ref, upper, table_ref, masks[1], two_ref, ctxp_ref.at[upper:])
    moves.ship(two_ref)
    if shifted:
        moves.ship(ctxp_ref)
        moves.need(take_ref)
        sent = dot(take_ref[...], ctxp_ref[...]).astype(BF)
        rows_out[...] = sent[:SLAB]
        cols_out[...] = sent[SLAB : 2 * SLAB]
        corner_out[...] = sent[2 * SLAB :]
    else:
        moves.need(place_ref)
        ctx_ref[...] = dot(place_ref[...], ctxp_ref[...]).astype(BF)


def feed_forward(moves, x_ref, ctx_ref, w_ref, vectors, mid_ref, h2_ref, hidden_ref, slope_ref):
    bp_ref, g2_ref, b2_ref, bo_ref, bh_ref = vectors
    mid_ref[...] = x_ref[...].astype(F32) + dot(ctx_ref[...], block(w_ref, 0)) + bp_ref[...]
    moves.ship(mid_ref)
    hat, _ = normalized(mid_ref[...])
    h2_ref[...] = (hat * g2_ref[...] + b2_ref[...]).astype(BF)
    moves.ship(h2_ref)
    for b in range(4):
        for half in range(2):
            lanes = slice(half * 256, half * 256 + 256)
            wide = slice(b * D + half * 256, b * D + half * 256 + 256)
            pre = dot(h2_ref[...], block_lanes(w_ref, 1 + b, lanes)) + bh_ref[:, wide]
            hidden, slope = gelu_both(pre)
            hidden_ref[:, wide] = hidden.astype(BF)
            slope_ref[:, wide] = slope.astype(BF)
        moves.ship(hidden_ref, columns(b))
        moves.ship(slope_ref, columns(b))
    out = mid_ref[...] + bo_ref[...]
    for b in range(4):
        out = out + dot(hidden_ref[:, b * D : (b + 1) * D], block(w_ref, 5 + b))
    return out


def forward_kernel(moves, *refs):
    coords_ref, ones, twos, refs = refs[0], refs[1:9], refs[9:17], refs[17:]
    x_ref, ctx_ref, *vectors = refs[:7]
    g1_ref, b1_ref, take_ref, w_ref, *kept = refs[7:15]
    out_ref, h_ref, rows_out, cols_out, corner_out, sems = refs[15:]
    copies = assembly(coords_ref, [(ones, "by z", (3, 3), 0), (twos, "by x", (0, 6), 3)], w_ref, sems)
    moves.need(ctx_ref)
    for c in copies:
        c.wait()
    moves.ship(w_ref)
    moves.need(x_ref)
    out = feed_forward(moves, x_ref, ctx_ref, w_ref, vectors, *kept)
    out_ref[...] = out
    moves.ship(out_ref)
    hat, _ = normalized(out)
    h_ref[...] = (hat * g1_ref[...] + b1_ref[...]).astype(BF)
    moves.ship(h_ref)
    moves.need(take_ref)
    sent = dot(take_ref[...], h_ref[...]).astype(BF)
    rows_out[...] = sent[:SLAB]
    cols_out[...] = sent[SLAB : 2 * SLAB]
    corner_out[...] = sent[2 * SLAB :]


def hidden_back_pass(moves, gm_ref, slope_ref, w_ref, dpre_ref, dbh_ref):
    moves.need(w_ref, part=0)
    for b in range(4):
        moves.need(slope_ref, part=b)
        for half in range(2):
            wide = slice(b * D + half * 256, b * D + half * 256 + 256)
            dpre = dot_nt(gm_ref[...], block_rows(w_ref, 5 + b, half)) * slope_ref[:, wide].astype(F32)
            dpre = dpre.astype(BF)
            dpre_ref[:, wide] = dpre
            dbh_ref[:, wide] = jnp.sum(dpre.astype(F32), 0, keepdims=True)
        moves.ship(dpre_ref, columns(b))


def middle_back_pass(moves, grad_ref, dpre_ref, w_ref, mid_ref, g2_ref, dmid_ref, go_ref, small_ref):
    moves.need(w_ref)
    moves.need(dpre_ref, part=0)
    dh2 = dot_nt(dpre_ref[:, :D], block(w_ref, 1))
    for b in range(1, 4):
        moves.need(dpre_ref, part=b)
        dh2 = dh2 + dot_nt(dpre_ref[:, b * D : (b + 1) * D], block(w_ref, 1 + b))
    moves.need(mid_ref, grad_ref)
    dx, dg2, db2 = norm_back(dh2, mid_ref[...], g2_ref[...])
    small_ref[1:2, :] = dg2
    small_ref[2:3, :] = db2
    dmid_ref[...] = grad_ref[...].astype(F32) + dx
    moves.ship(dmid_ref)
    go_ref[...] = dmid_ref[...].astype(BF)
    moves.ship(go_ref)
    small_ref[0:1, :] = jnp.sum(go_ref[...].astype(F32), 0, keepdims=True)


def turn_kernel(moves, *refs):
    coords_ref, pieces, refs = refs[0], refs[1:3], refs[3:]
    x_ref, ctxp_ref, rows_ref, cols_ref, corner_ref, place_ref, *vectors = refs[:11]
    g_ref, take_ref, out_ref, dmid_ref, small_ref, dbh_ref, dctx_ref, rows_out, cols_out, corner_out = refs[11:21]
    keep_ref, send_ref, w_ref, ctx_ref, mid_ref, h2_ref, hidden_ref, slope_ref, dpre_ref, go_ref, sems = refs[21:]
    copies = assembly(coords_ref, [(pieces, "z", (0, 9), 0)], w_ref, sems)
    moves.need(place_ref, ctxp_ref)
    place = place_ref[...]
    slabs = jnp.concatenate([rows_ref[...], cols_ref[...], corner_ref[...]], 0)
    ctx_ref[...] = (dot(place[:, :PADDED], ctxp_ref[...]) + dot(place[:, PADDED:], slabs)).astype(BF)
    for c in copies:
        c.wait()
    moves.need(x_ref)
    out = feed_forward(moves, x_ref, ctx_ref, w_ref, vectors, mid_ref, h2_ref, hidden_ref, slope_ref)
    out_ref[...] = out.astype(BF)
    moves.ship(out_ref)
    moves.need(g_ref)
    small_ref[3:4, :] = jnp.sum(g_ref[...].astype(F32), 0, keepdims=True)
    hidden_back_pass(moves, g_ref, slope_ref, w_ref, dpre_ref, dbh_ref)
    middle_back_pass(moves, g_ref, dpre_ref, w_ref, mid_ref, vectors[1], dmid_ref, go_ref, small_ref)
    dctx_ref[...] = dot_nt(go_ref[...], block(w_ref, 0)).astype(BF)
    moves.ship(dctx_ref)
    moves.need(take_ref)
    sent = dot(take_ref[...], dctx_ref[...]).astype(BF)
    rows_out[...] = sent[:SLAB]
    cols_out[...] = sent[SLAB : 2 * SLAB]
    corner_out[...] = sent[2 * SLAB :]
    hidden_grads(moves, coords_ref, 1, g_ref, hidden_ref, h2_ref, dpre_ref, keep_ref, send_ref)
    for half in range(2):
        rows = slice(half * 256, half * 256 + 256)
        store_grad(coords_ref, keep_ref, send_ref, 0, half, dot_tn(ctx_ref[:, rows], go_ref[...]))
    moves.ship(keep_ref, of_blocks(0))
    moves.ship(send_ref, of_blocks(0))


def hidden_grads(moves, coords_ref, first, gm_ref, hidden_ref, h2_ref, dpre_ref, keep_ref, send_ref):
    for b in range(4):
        moves.need(hidden_ref, part=b)
        for half in range(2):
            wide = slice(b * D + half * 256, b * D + half * 256 + 256)
            grad_c = dot_tn(hidden_ref[:, wide], gm_ref[...])
            store_grad(coords_ref, keep_ref, send_ref, first + 4 + b, half, grad_c)
        moves.ship(keep_ref, of_blocks(first + 4 + b))
        moves.ship(send_ref, of_blocks(first + 4 + b))
    moves.need(h2_ref, dpre_ref)
    for b in range(4):
        for half in range(2):
            rows = slice(half * 256, half * 256 + 256)
            grad_e = dot_tn(h2_ref[:, rows], dpre_ref[:, b * D : (b + 1) * D])
            store_grad(coords_ref, keep_ref, send_ref, first + b, half, grad_e)
        moves.ship(keep_ref, of_blocks(first + b))
        moves.ship(send_ref, of_blocks(first + b))


def back_first_kernel(moves, *refs):
    coords_ref, dmid1_ref, dhp_ref, rows_ref, cols_ref, corner_ref, back_ref, x1_ref, g1_ref = refs[:9]
    hidden_ref, slope_ref, h2_ref, w_ref = refs[9:13]
    grad_ref, dpre_ref, keep_ref, send_ref, dbo_ref, dbh_ref, above_ref, gm_ref = refs[13:]
    moves.need(back_ref, dhp_ref)
    back = back_ref[...]
    slabs = jnp.concatenate([rows_ref[...], cols_ref[...], corner_ref[...]], 0)
    dh = dot(back[:, :PADDED], dhp_ref[...]) + dot(back[:, PADDED:], slabs)
    moves.need(x1_ref)
    dx, dg1, db1 = norm_back(dh, x1_ref[...], g1_ref[...])
    above_ref[0:1, :] = dg1
    above_ref[1:2, :] = db1
    moves.need(dmid1_ref)
    grad = dmid1_ref[...] + dx
    grad_ref[...] = grad
    moves.ship(grad_ref)
    gm_ref[...] = grad.astype(BF)
    dbo_ref[...] = jnp.sum(gm_ref[...].astype(F32), 0, keepdims=True)
    hidden_back_pass(moves, gm_ref, slope_ref, w_ref, dpre_ref, dbh_ref)
    hidden_grads(moves, coords_ref, 0, gm_ref, hidden_ref, h2_ref, dpre_ref, keep_ref, send_ref)


def middle_first_kernel(moves, grad_ref, dpre_ref, mid_ref, ctx_ref, w_ref, g2_ref, place_ref, *outs):
    dmid_ref, dwp_ref, small_ref, dctxp_ref, go_ref = outs
    middle_back_pass(moves, grad_ref, dpre_ref, w_ref, mid_ref, g2_ref, dmid_ref, go_ref, small_ref)
    moves.need(ctx_ref)
    for half in range(2):
        rows = slice(half * 256, half * 256 + 256)
        dwp_ref[rows, :] = dot_tn(ctx_ref[:, rows], go_ref[...]).astype(BF)
    moves.ship(dwp_ref)
    dctx = dot_nt(go_ref[...], block(w_ref, 0)).astype(BF)
    moves.need(place_ref)
    dctxp_ref[...] = dot(place_ref[...], dctx).astype(BF)


def attend_back_pairs(first, qkv_ref, attn_ref, dctxp_ref, dqkv_ref, dtable_ref):
    if first == 0:
        dtable_ref[...] = jnp.zeros_like(dtable_ref)
    scale = HEAD_DIM**-0.5

    def one_pair(p, carry):
        start = pl.multiple_of(first + p * 128, 128)
        for g in range(GROUPS):
            lane = g * 128
            attn = attn_ref[p, g]
            keys = head_rows(side_by_side(qkv_ref, start, D + lane))
            values = head_rows(side_by_side(qkv_ref, start, 2 * D + lane))
            queries = block_diagonal(side_by_side(qkv_ref, start, lane))
            grads = block_diagonal(side_by_side(dctxp_ref, start, lane))
            probs = attn.astype(F32).reshape(4, SLOT, 128)
            dprobs = dot_nt(values, grads).reshape(4, SLOT, 128)
            dscores = probs * (dprobs - jnp.sum(probs * dprobs, 1, keepdims=True))
            dscores = dscores.reshape(256, 128).astype(BF)
            dtable_ref[g * 256 : (g + 1) * 256, :] += dscores.astype(F32)
            store_diagonal(dqkv_ref, start, lane, dot_tn(dscores, keys) * scale)
            dkeys = (head_fold(dot(dscores, queries)) * scale).astype(BF)
            dqkv_ref[pl.ds(start, SLOT), D + lane : D + lane + 128] = dkeys[:, :128]
            dqkv_ref[pl.ds(start + SLOT, SLOT), D + lane : D + lane + 128] = dkeys[:, 128:]
            dvalues = head_fold(dot(attn, grads)).astype(BF)
            dqkv_ref[pl.ds(start, SLOT), 2 * D + lane : 2 * D + lane + 128] = dvalues[:, :128]
            dqkv_ref[pl.ds(start + SLOT, SLOT), 2 * D + lane : 2 * D + lane + 128] = dvalues[:, 128:]
        return carry

    lax.fori_loop(0, PAIRS // 2, one_pair, 0)


def table_sum(dtable_ref, by_key_ref, out_ref):
    total = jnp.zeros((2 * HEADS, 256), F32)
    row = lax.broadcasted_iota(jnp.int32, (256, 256), 0)
    for c in range(25):
        hot = jnp.where(row == by_key_ref[c : c + 1, :], 1.0, 0.0).astype(BF)
        keys = [dtable_ref[pl.ds(2 * c + k, HEADS, stride=SLOT), :] for k in range(2)]
        rows = jnp.concatenate(keys, 1)
        high = rows.astype(BF)
        low = (rows - high.astype(F32)).astype(BF)
        total = total + dot_nt(jnp.concatenate([high, low], 0), hot)
    out_ref[...] = total[:HEADS] + total[HEADS:]


def attend_back_kernel(moves, *refs):
    dctx_ref, rows_ref, cols_ref, corner_ref, place_ref, qkv_ref, one_ref, two_ref, w_ref, take_ref, key_ref = refs[:11]
    dqkv_ref, dbias_ref, table_ref, dhp_ref, rows_out, cols_out, corner_out, dctxp_ref, dtable_ref = refs[11:]
    moves.need(place_ref, dctx_ref)
    place = place_ref[...]
    slabs = jnp.concatenate([rows_ref[...], cols_ref[...], corner_ref[...]], 0)
    dctxp_ref[...] = (dot(place[:, :CELLS], dctx_ref[...]) + dot(place[:, CELLS:], slabs)).astype(BF)
    moves.need(qkv_ref, one_ref)
    attend_back_pairs(0, qkv_ref, one_ref, dctxp_ref, dqkv_ref, dtable_ref)
    moves.need(two_ref)
    attend_back_pairs(PADDED // 2, qkv_ref, two_ref, dctxp_ref, dqkv_ref, dtable_ref)
    moves.ship(dqkv_ref)
    moves.need(w_ref)
    table_sum(dtable_ref, key_ref, table_ref)
    for s in range(3):
        dbias_ref[s : s + 1, :] = jnp.sum(dqkv_ref[:, s * D : (s + 1) * D].astype(F32), 0, keepdims=True)
    dhp = dot_nt(dqkv_ref[:, :D], block(w_ref, 0))
    for s in range(1, 3):
        dhp = dhp + dot_nt(dqkv_ref[:, s * D : (s + 1) * D], block(w_ref, s))
    dhp_ref[...] = dhp.astype(BF)
    moves.ship(dhp_ref)
    moves.need(take_ref)
    sent = dot(take_ref[...], dhp_ref[...]).astype(BF)
    rows_out[...] = sent[:SLAB]
    cols_out[...] = sent[SLAB : 2 * SLAB]
    corner_out[...] = sent[2 * SLAB :]


def grads_heads_kernel(moves, coords_ref, hp_ref, dqkv_ref, keep_ref, send_ref):
    moves.need(hp_ref)
    for s in range(3):
        moves.need(dqkv_ref, part=s)
        for half in range(2):
            rows = slice(half * 256, half * 256 + 256)
            grad_w = dot_tn(hp_ref[:, rows], dqkv_ref[:, s * D : (s + 1) * D])
            store_grad(coords_ref, keep_ref, send_ref, s, half, grad_w)
        moves.ship(keep_ref, of_blocks(s))
        moves.ship(send_ref, of_blocks(s))


def attend_back_end_kernel(moves, *refs):
    coords_ref, dctxp_ref, qkv_ref, one_ref, two_ref, hp_ref, dwp_ref, key_ref, w_ref, place_ref = refs[:10]
    x_ref, dmid_ref, g1_ref, norm1, dqb1, sums1, dbh1, table1, sums0, dbo0, dbh0 = refs[10:21]
    keep_ref, send_ref, out_ref, sums_ref, dqkv_ref, dtable_ref, dhp_ref = refs[21:]
    moves.need(dctxp_ref, qkv_ref, one_ref)
    attend_back_pairs(0, qkv_ref, one_ref, dctxp_ref, dqkv_ref, dtable_ref)
    moves.need(two_ref)
    attend_back_pairs(PADDED // 2, qkv_ref, two_ref, dctxp_ref, dqkv_ref, dtable_ref)
    moves.need(hp_ref)
    dqb = []
    for s in range(3):
        wide = slice(s * D, (s + 1) * D)
        dqb.append(jnp.sum(dqkv_ref[:, wide].astype(F32), 0, keepdims=True))
        for half in range(2):
            rows = slice(half * 256, half * 256 + 256)
            grad_w = dot_tn(hp_ref[:, rows], dqkv_ref[:, wide])
            store_grad(coords_ref, keep_ref, send_ref, s, half, grad_w)
    moves.need(dwp_ref)
    for half in range(2):
        store_grad(coords_ref, keep_ref, send_ref, 3, half, dwp_ref[half * 256 : half * 256 + 256, :])
    moves.ship(keep_ref)
    moves.ship(send_ref)
    moves.need(w_ref)
    dhp = dot_nt(dqkv_ref[:, :D], block(w_ref, 0))
    for s in range(1, 3):
        dhp = dhp + dot_nt(dqkv_ref[:, s * D : (s + 1) * D], block(w_ref, s))
    dhp_ref[...] = dhp.astype(BF)
    moves.need(place_ref, x_ref, dmid_ref)
    dh = dot(place_ref[...], dhp_ref[...])
    dx, dg1, db1 = norm_back(dh, x_ref[...].astype(F32), g1_ref[...])
    out_ref[...] = dmid_ref[...] + dx
    moves.ship(out_ref)
    for at, norm, query, value, sums, dbo, dbh in (
        (0, (dg1, db1), dqb[0], dqb[2], sums0, dbo0[...], dbh0),
        (12, (norm1[0:1, :], norm1[1:2, :]), dqb1[0:1, :], dqb1[2:3, :], sums1, sums1[3:4, :], dbh1),
    ):
        rows = [*norm, query, value, sums[0:1, :], sums[1:2, :], sums[2:3, :], dbo]
        rows += [dbh[:, D * b : D * b + D] for b in range(4)]
        for i, row in enumerate(rows):
            sums_ref[at + i : at + i + 1, :] = row
    table_sum(dtable_ref, key_ref, sums_ref.at[24:40, 0:256])
    sums_ref[24:40, 256:512] = table1[...]


def add_kernel(*refs):
    out_ref, at = refs[-1], 0
    for i in range(0, len(refs) - 1, 2):
        n = refs[i].shape[2]
        total = refs[i][...].astype(F32) + refs[i + 1][...].astype(F32)
        out_ref[:, :, at : at + n] = total.astype(BF)
        at += n


def sum_split_kernel(coords_ref, parts_ref, *outs):
    for d, out in enumerate(outs):
        target = lax.rem(coords_ref[1] + d, 4)
        total = parts_ref[0, target].astype(F32)
        for k in range(1, 4):
            total = total + parts_ref[k, target].astype(F32)
        out[...] = total.astype(BF)


def to_xz_kernel(coords_ref, keep_ref, other_ref, parts_ref, sums_ref, more_ref, near_ref, *outs):
    smalls = jnp.concatenate([sums_ref[...] + more_ref[...], jnp.zeros((8, D), F32)], 0)
    high = smalls.astype(BF).astype(F32)
    low = smalls - high
    for z in range(4):
        for x in range(4):
            total = keep_ref[z, x].astype(F32) + other_ref[z, x].astype(F32)
            near_ref[4 * z + x, 0:4] = total.astype(BF)
            at = 3 * (4 * z + x)
            rows = [high[at : at + 3], low[at : at + 3], jnp.zeros((10, D), F32)]
            near_ref[4 * z + x, 4] = jnp.concatenate(rows, 0).astype(BF)
    for d, out in enumerate(outs):
        target = lax.rem(coords_ref[1] + d, 4)
        total = parts_ref[0, target].astype(F32)
        for k in range(1, 4):
            total = total + parts_ref[k, target].astype(F32)
        out[...] = total.astype(BF)


def to_seq_kernel(near_ref, *refs):
    pieces, late_ref, small_ref = refs[:4], refs[4], refs[5]
    total = near_ref[0].astype(F32)
    for i in range(1, 16):
        total = total + near_ref[i].astype(F32)
    late_ref[0:4] = total[0:4].astype(BF)
    rows = total[4, 0:3] + total[4, 3:6]
    rows = [rows[r : r + 1, 128 * q : 128 * q + 128] for r in range(3) for q in range(4)]
    rows = jnp.concatenate(rows + [jnp.zeros((4, 128), F32)], 0)
    for i in range(64):
        small_ref[i] = rows
    total = pieces[0][...].astype(F32)
    for piece in pieces[1:]:
        total = total + piece[...].astype(F32)
    late_ref[4:15] = total.astype(BF)


def four(refs, b):
    return (refs[0][b].astype(F32) + refs[1][b].astype(F32)) + (refs[2][b].astype(F32) + refs[3][b].astype(F32))


def reorder(values, order):
    n = values.shape[0]
    high = values.astype(BF)
    rest = values - high.astype(F32)
    low = rest.astype(BF)
    last = (rest - low.astype(F32)).astype(BF)
    rows = dot_nt(jnp.concatenate([high, low, last], 0), order)
    return rows[:n] + rows[n : 2 * n] + rows[2 * n :]


def step_into(at, grad, old, new, rate, decay):
    weight, first, second = (ref[at] for ref in old)
    for ref, value in zip(new, adamw(weight, first, second, grad, rate, decay)):
        ref[at] = value


def update_small_kernel(*refs):
    smalls_ref, units_ref, small, table = refs[0], refs[1], refs[2:5], refs[5:8]
    new_small, new_table, bias_ref, sums_ref = refs[8:11], refs[11:14], refs[14], refs[15]
    for i in range(16):
        part = (smalls_ref[4 * i] + smalls_ref[4 * i + 1]) + (smalls_ref[4 * i + 2] + smalls_ref[4 * i + 3])
        for k in range(12):
            sums_ref[3 * i + k // 4 : 3 * i + k // 4 + 1, k % 4 * 128 : k % 4 * 128 + 128] = part[k : k + 1]
    for layer in range(LAYERS):
        rows = [sums_ref[12 * layer + i : 12 * layer + i + 1, :] for i in range(12)]
        bias_ref[layer : layer + 1, :] = rows[7]
        parts = [
            jnp.concatenate([rows[8 + b][:, 128 * g : 128 * g + 128] for b in range(4)], 1) for g in range(GROUPS)
        ]
        units = reorder(jnp.concatenate(parts + [jnp.zeros((12, D), F32)], 0), units_ref[...])
        for i, grad in enumerate(rows[:8] + [units[g : g + 1] for g in range(GROUPS)]):
            at = (slice(layer, layer + 1), slice(D * i, D * i + D))
            step_into(at, grad, small, new_small, 0.3, 0.0)
        step_into((layer,), sums_ref[24:40, 256 * layer : 256 * layer + REL], table, new_table, 0.6, 0.0)


def update_kernel(*refs):
    early, late, heads_ref, units_ref, refs = refs[:4], refs[4:8], refs[8], refs[9], refs[10:]
    old = [refs[3 * i : 3 * i + 3] for i in range(4)]
    new = [refs[12 + 3 * i : 15 + 3 * i] for i in range(4)]

    def layer_step(heads, head_at, rest, rest_at):
        step_into((0,), four(rest, rest_at), old[1], new[1], 0.1, 0.05)
        for b in range(4):
            step_into((0, slice(16 * b, 16 * b + 16)), four(rest, rest_at + 5 + b), old[3], new[3], 0.03, 0.05)
        for n, wide, order_ref, i, pieces, at in (
            (3, 384, heads_ref, 0, heads, head_at),
            (4, 512, units_ref, 2, rest, rest_at + 1),
        ):
            grads = [four(pieces, at + b) for b in range(n)]
            for g in range(GROUPS):
                part = jnp.concatenate([v[:, 128 * g : 128 * g + 128] for v in grads], 1)
                lanes = (0, slice(None), slice(wide * g, wide * g + wide))
                step_into(lanes, reorder(part, order_ref[...]), old[i], new[i], 0.03, 0.05)

    @pl.when(pl.program_id(0) == 0)
    def _():
        layer_step(late, 0, late, 3)

    @pl.when(pl.program_id(0) == 1)
    def _():
        layer_step(late, 12, early, 0)


def to_neighbours(slabs, ahead):
    step = -1 if ahead else 1
    along = [(i, (i + step) % 4) for i in range(4)]
    over = [(0, 1), (1, 0)]
    both = [(i * 2 + c, ((i + step) % 4) * 2 + 1 - c) for i in range(4) for c in range(2)]
    rows, cols, corner = slabs
    return (
        lax.ppermute(rows, "seq", along),
        lax.ppermute(cols, "col", over),
        lax.ppermute(corner, ("seq", "col"), both),
    )


def flat(z, x, core):
    return (z * 4 + (x % 2) * 2 + core) * 2 + x // 2


ALONG_X = [[flat(z, x, core) for x in range(4)] for z in range(4) for core in range(2)]
OVER_XZ = [[flat(z, x, core) for z in range(4) for x in range(4)] for core in range(2)]
OVER_CHIPS = [[i * 4 + y for i in group for y in range(4)] for group in OVER_XZ]
OTHER_CORE = [(i, i ^ 1) for i in range(16)]


def from_z(distance):
    return [(((z + distance) % 4) * 4 + k, z * 4 + k) for z in range(4) for k in range(4)]


def from_x(distance):
    return [(flat(z, (x + distance) % 4, c), flat(z, x, c)) for z in range(4) for x in range(4) for c in range(2)]


ALONG_Z = [[z * 4 + k for z in range(4)] for k in range(4)]


def scattered_z(value):
    return lax.all_to_all(value, "img", 0, 0, tiled=True, axis_index_groups=ALONG_Z)


def from_core(value):
    return lax.ppermute(value, "img", OTHER_CORE)


BY_SEQ = [[(i, i ^ d) for i in range(4)] for d in (1, 2, 3)]
BY_Z = [[(z * 4 + k, (z ^ d) * 4 + k) for z in range(4) for k in range(4)] for d in (1, 2, 3)]
def both_cores(*pairs):
    arrays = [a for pair in pairs for a in pair]
    specs = [pl.BlockSpec((1, *a.shape[1:]), lambda i: (i, 0, 0, 0, 0)) for a in arrays]
    shape = (4, 4, sum(keep.shape[2] for keep, _ in pairs), 16, D)
    size = math.prod(shape) * 2
    return pl.pallas_call(
        add_kernel,
        grid=(4,),
        out_shape=jax.ShapeDtypeStruct(shape, BF),
        in_specs=specs,
        out_specs=pl.BlockSpec((1, *shape[1:]), lambda i: (i, 0, 0, 0, 0)),
        compiler_params=pltpu.CompilerParams(vmem_limit_bytes=VMEM_BYTES),
        cost_estimate=pl.CostEstimate(flops=size, bytes_accessed=3 * size, transcendentals=0),
    )(*arrays)


def by_seq(value):
    return [value] + [lax.ppermute(value, "seq", p) for p in BY_SEQ]


def update(early, late, heads, units, state):
    whole = [pl.BlockSpec(memory_space=pltpu.VMEM)] * 10
    parts = [pl.BlockSpec((1, *a.shape[1:]), lambda layer: (layer, 0, 0)) for a in state]
    return pl.pallas_call(
        update_kernel,
        grid=(LAYERS,),
        out_shape=[jax.ShapeDtypeStruct(a.shape, F32) for a in state],
        in_specs=whole + parts,
        out_specs=parts,
        compiler_params=pltpu.CompilerParams(vmem_limit_bytes=VMEM_BYTES),
        cost_estimate=pl.CostEstimate(flops=8 * 10**9, bytes_accessed=8 * 10**6, transcendentals=0),
    )(*early, *late, heads, units, *state)


def adamw(weight, first, second, grad, rate, decay):
    first = 0.9 * first + 0.1 * grad
    second = 0.999 * second + 0.001 * grad * grad
    first_hat = first / (1.0 - 0.9**STEP)
    second_hat = second / (1.0 - 0.999**STEP)
    return (first, second, weight - rate * (first_hat / (jnp.sqrt(second_hat) + 1e-08) + decay * weight))


def hidden_order(vector):
    return vector.reshape(32, 4, 16).transpose(1, 0, 2).reshape(HIDDEN)


def split_small(vector):
    pieces = [vector[i * D : (i + 1) * D][None] for i in range(8)]
    return pieces + [hidden_order(vector[8 * D :])[None]]


def score_table(table, hot):
    rows = lax.dot_general(table, hot, (((0,), (0,)), ((), ())), precision=highest, preferred_element_type=F32)
    rows = rows.reshape(HEADS, AREA, AREA) * log2e
    rows = jnp.pad(rows, ((0, 0), (0, 0), (0, SLOT - AREA)))
    rows = jnp.pad(rows, ((0, 0), (0, SLOT - AREA), (0, 0)), constant_values=padded_score)
    return jnp.concatenate([rows, rows], 2).reshape(HEADS * SLOT, 128)


def allowed_pairs(region):
    win = region.reshape(4, WIN, 4, WIN).transpose(0, 2, 1, 3).reshape(16, AREA)
    win = jnp.pad(win, ((0, 0), (0, SLOT - AREA)))
    same = win[:, :, None] == win[:, None, :]
    same = same | (jnp.arange(SLOT) >= AREA)[None, :, None]
    same = same.reshape(PAIRS, 2, SLOT, SLOT).transpose(0, 2, 1, 3).reshape(PAIRS, SLOT, 128)
    return same.astype(F32)


def local(
    images,
    out_grad,
    region_ids,
    rel_index,
    qkv_weight,
    qkv_first,
    qkv_second,
    proj_weight,
    proj_first,
    proj_second,
    expand_weight,
    expand_first,
    expand_second,
    contract_weight,
    contract_first,
    contract_second,
    small_params,
    small_first,
    small_second,
    bias_table,
    table_first,
    table_second,
):
    plain, plain_back, ahead, back, take_first, take_last = (jnp.asarray(a, BF) for a in placements())
    heads, units = (jnp.asarray(a, BF) for a in column_orders())
    img = lax.axis_index("img")
    x = lax.axis_index("col") * 2 + img // 2 % 2
    coords = jnp.stack([img // 4, x, img % 2]).astype(jnp.int32)
    matrices = (qkv_weight, proj_weight, expand_weight, contract_weight, heads, units)
    one, two = call(pack_kernel, [((4, 6, 16, D), BF), ((6, 16, D), BF)], matrices, us=3)

    def along_z(value):
        return [value] + [lax.ppermute(value, "img", from_z(d)) for d in (1, 2, 3)]

    def along_x(value):
        return [value] + [lax.ppermute(value, ("img", "col"), from_x(d)) for d in (1, 2, 3)]

    one0 = lax.all_to_all(one, ("img", "col"), 0, 0, tiled=True, axis_index_groups=ALONG_X)
    two0 = along_z(two)
    x0 = images.reshape(CELLS, D)
    g_out = out_grad.reshape(CELLS, D)
    by_key = jnp.pad(rel_index.T, ((0, 1), (0, SLOT - AREA)), constant_values=-1)
    by_key = jnp.concatenate([by_key, by_key], 1).reshape(25, 256)
    keys_hot = (jnp.arange(REL, dtype=jnp.int32)[:, None] == rel_index.T.reshape(1, AREA * AREA)).astype(F32)
    tables = [score_table(bias_table[layer], keys_hot) for layer in range(LAYERS)]
    region = lax.dynamic_slice_in_dim(region_ids, lax.axis_index("seq") * SIDE, SIDE, 0)
    mask = allowed_pairs(region)
    small = [split_small(small_params[layer]) for layer in range(LAYERS)]
    zero = jnp.zeros((1, D), F32)
    qkv_bias = [jnp.concatenate([s[2], zero, s[3]], 1) for s in small]

    by_columns = [columns(b) for b in range(4)]
    qkv_shape = ((PADDED, 3 * D), BF)
    attn_shape = ((PAIRS // 2, GROUPS, 256, 128), BF)
    slab_shapes = [((SLAB, D), BF), ((SLAB, D), BF), ((CORNER, D), BF)]
    cells16, cells32 = ((CELLS, D), BF), ((CELLS, D), F32)
    padded16 = ((PADDED, D), BF)
    wide16 = ((CELLS, HIDDEN), BF)

    copies = pltpu.SemaphoreType.DMA((32,))
    w_shapes = [((3, 32, 16, D), BF), ((9, 32, 16, D), BF)]
    g1, b1, _, _, bp, g2, b2, bo, bh = small[0]
    (hp0,) = call(enter_kernel, [padded16], (x0, g1, b1, plain), us=4)
    (two0,) = call(stack_kernel, [((4, 6, 16, D), BF)], two0, after=(hp0,))
    one0, two0 = along_z(one0), along_x(two0)
    one0 = one0 + [from_core(v) for v in one0]
    two0 = two0 + [from_core(v) for v in two0]
    half16 = ((PADDED // 2, D), BF)
    wq0, qkv0, attn0, attn0b, ctx0 = call(
        functools.partial(attend_kernel, False),
        [w_shapes[0], qkv_shape, attn_shape, attn_shape, cells16],
        (hp0, qkv_bias[0], tables[0], plain_back),
        [pltpu.VMEM(*padded16), copies],
        one0,
        coords,
        us=18,
        late=dict.fromkeys((0, 2, 3)),
        early=(0, 1, 2, 3),
    )
    spread, rest = call(
        pack_next_kernel, [((16, 3, 16, D), BF), ((9, 16, D), BF)], matrices, us=3, after=(ctx0,)
    )
    lines = lax.all_to_all(spread, ("img", "col"), 0, 0, tiled=True, axis_index_groups=OVER_XZ)
    one1 = [lines, from_core(lines)]
    wm0, mid0, h20, hidden0, slope0, x1, h1, *slabs = call(
        forward_kernel,
        [w_shapes[1], cells32, cells16, wide16, wide16, cells32, cells16, *slab_shapes],
        (x0, ctx0, bp, g2, b2, bo, bh, small[1][0], small[1][1], take_first),
        [pltpu.SemaphoreType.DMA((64,))],
        one0 + two0,
        coords,
        us=15,
        after=(spread, rest),
        late=dict.fromkeys((1, 0, 9)),
        early=(0, 1, 2, 3, 4, 5, 6),
    )
    (lines,) = call(stack_spread_kernel, [((4, 4, 9, 16, D), BF)], along_x(rest), us=2, after=(h1,))
    two1 = scattered_z(lines).reshape(16, 9, 16, D)
    g1, b1, _, _, bp, g2, b2, bo, bh = small[1]
    slabs = to_neighbours(slabs, True)
    wq1, hp1, qkv1, attn1, attn1b, ctxp1, *slabs = call(
        functools.partial(attend_kernel, True),
        [w_shapes[0], padded16, qkv_shape, attn_shape, attn_shape, padded16, *slab_shapes],
        (h1, *slabs, ahead, qkv_bias[1], tables[1], mask, take_last),
        [copies],
        one1,
        coords,
        us=18,
        after=(by_key,),
        late=dict.fromkeys((4, 0, 6, 7, 8)),
        early=(0, 1, 2, 3, 4, 5),
    )
    (two1,) = held((two1,), (hp1,))
    two1 = [two1, from_core(two1)]
    slabs = to_neighbours(slabs, False)
    out, dmid1, sums1, dbh1, dctx1, *slabs, keep, send = call(
        turn_kernel,
        [cells16, cells32, ((4, D), F32), ((1, HIDDEN), F32), cells16, *slab_shapes, *[((4, 4, 9, 16, D), BF)] * 2],
        (x1, ctxp1, *slabs, back, bp, g2, b2, bo, bh, g_out, take_first),
        [pltpu.VMEM(*a) for a in (w_shapes[1], cells16, cells32, cells16, wide16, wide16, wide16, cells16)] + [copies],
        two1,
        coords,
        us=34,
        late=dict.fromkeys((5, 1, 0, 11, 12)),
        early=(0, 1, 4, 8, 9),
    )
    slabs = to_neighbours(slabs, True)
    part_m1 = both_cores((keep, from_core(send)))
    dqkv1, dqb1, table1, dhp1, *slabs = call(
        attend_back_kernel,
        [qkv_shape, ((3, D), F32), ((HEADS, 256), F32), padded16, *slab_shapes],
        (dctx1, *slabs, ahead, qkv1, attn1, attn1b, wq1, take_last, by_key),
        [pltpu.VMEM((PADDED, D), BF), pltpu.VMEM((HEADS * SLOT, 128), F32)],
        us=20,
        after=(part_m1,),
        late=dict.fromkeys((4, 0, 5, 6, 7, 8, 9)),
        early=(0, 3),
    )
    slabs = to_neighbours(slabs, False)
    keep, send = call(
        grads_heads_kernel,
        [((4, 4, 3, 16, D), BF)] * 2,
        (hp1, dqkv1),
        place=coords,
        us=4,
        late={0: None, 1: by_columns[:3]},
        early=(0, 1),
    )
    pair_q1 = (keep, from_core(send))
    half_m1, *sent = call(sum_split_kernel, [((9, 16, D), BF)] * 4, (scattered_z(part_m1),), place=coords, us=2)
    grad1, dpre0, keep, send, dbo0, dbh0, norm1 = call(
        back_first_kernel,
        [cells32, wide16, *[((4, 4, 8, 16, D), BF)] * 2, ((1, D), F32), ((1, HIDDEN), F32), ((2, D), F32)],
        (dmid1, dhp1, *slabs, back, x1, small[1][0], hidden0, slope0, h20, wm0),
        [pltpu.VMEM((CELLS, D), BF)],
        place=coords,
        us=16,
        after=(half_m1, pair_q1[0]),
        late={5: None, 1: None, 6: None, 0: None, 11: [slice(5, 9)], 9: by_columns, 8: by_columns, 10: None},
        early=(0, 1, 2, 3),
    )
    got = [lax.ppermute(v, ("img", "col"), from_x(4 - d)) for d, v in zip((1, 2, 3), sent)]
    grad_m1 = sum((v.astype(F32) for v in got), half_m1.astype(F32)).astype(BF)
    dmid0, dwp0, sums0, dctxp0 = call(
        middle_first_kernel,
        [cells32, ((D, D), BF), ((3, D), F32), padded16],
        (grad1, dpre0, mid0, ctx0, wm0, small[0][5], plain),
        [pltpu.VMEM((CELLS, D), BF)],
        us=8,
        after=(grad_m1,),
        late={4: (0, 5), 1: by_columns, 2: None, 0: None, 3: None, 6: None},
        early=(0, 1),
    )
    part_0 = both_cores((keep, from_core(send)), pair_q1)
    grads_m1 = by_seq(grad_m1)
    half_0 = scattered_z(part_0)
    *keep_send, input_grad, sums = call(
        attend_back_end_kernel,
        [*[((4, 4, 4, 16, D), BF)] * 2, cells32, ((40, D), F32)],
        (dctxp0, qkv0, attn0, attn0b, hp0, dwp0, by_key, wq0, plain_back, x0, dmid0, small[0][0])
        + (norm1, dqb1, sums1, dbh1, table1, sums0, dbo0, dbh0),
        [pltpu.VMEM(*qkv_shape), pltpu.VMEM((HEADS * SLOT, 128), F32), pltpu.VMEM(*padded16)],
        place=coords,
        us=26,
        late=dict.fromkeys((0, 1, 2, 3, 4, 5, 7, 8, 9, 10)),
        early=(0, 1, 2),
        after=(part_0, *grads_m1),
    )
    other, more = from_core(keep_send[1]), from_core(sums)
    near, mine, *sent = call(
        to_xz_kernel,
        [((16, 5, 16, D), BF)] + [((11, 16, D), BF)] * 4,
        (keep_send[0], other, half_0, sums, more),
        place=coords,
        us=5,
    )
    near = lax.all_to_all(near, ("img", "col"), 0, 0, tiled=True, axis_index_groups=OVER_XZ)
    pieces = [mine] + [lax.ppermute(v, ("img", "col"), from_x(4 - d)) for d, v in zip((1, 2, 3), sent)]
    late, smalls = call(to_seq_kernel, [((15, 16, D), BF), ((64, 16, 128), F32)], (near, *pieces), us=3)
    late = by_seq(late)
    smalls = lax.all_to_all(smalls, ("img", "col", "seq"), 0, 0, tiled=True, axis_index_groups=OVER_CHIPS)

    state = (
        (qkv_weight, qkv_first, qkv_second),
        (proj_weight, proj_first, proj_second),
        (expand_weight, expand_first, expand_second),
        (contract_weight, contract_first, contract_second),
    )
    flat_state = [a for three in state for a in three]
    swap = functools.partial(jnp.transpose, axes=(0, 2, 1))
    small = (small_params, small_first, small_second, swap(bias_table), swap(table_first), swap(table_second))
    done = update(grads_m1, late, heads, units, flat_state)
    last = call(
        update_small_kernel,
        [(a.shape, F32) for a in small] + [((LAYERS, D), F32)],
        (smalls, units, *small),
        [pltpu.VMEM((48, D), F32)],
        us=3,
    )
    return (
        out.reshape(images.shape),
        input_grad.reshape(images.shape),
        *done,
        *last[:3],
        *(swap(a) for a in last[3:6]),
        last[6],
    )


def solution(mesh):
    cells = P("img", "seq", "col", None)
    matrix = P(None, ("img", "col"), None)
    in_specs = (cells, cells, P(None, "col"), P(), *([matrix] * 12), *([P()] * 6))
    out_specs = (cells, cells, *([matrix] * 12), *([P()] * 7))
    return jax.shard_map(local, mesh=mesh, in_specs=in_specs, out_specs=out_specs, check_vma=False)
```

time: 424 us -> 404 us (0.953)
  Pallas kernels: 214 us -> 202 us
  waiting for transfers between devices: 52 us -> 60.8 us
  other arithmetic: 12.4 us -> 4.44 us
  starting transfers between devices: 102 us -> 97.6 us
    all_to_all x4 -> x7, waiting for transfers between devices: 5.11 us -> 20.7 us  [the longest x3 13.7 us: scattered_z(): lax.all_to_all(value, 'img', 0, 0, tiled=True, axis_index_groups=ALONG_Z)]
    ppermute x31 -> x18, starting transfers between devices: 46.2 us -> 33.7 us  [the longest x6 12.2 us: along_x(): lax.ppermute(value, ('img', 'col'), from_x(d))]
    all_to_all x4 -> x7, starting transfers between devices: 19.6 us -> 31.9 us  [the longest x3 12.2 us: scattered_z(): lax.all_to_all(value, 'img', 0, 0, tiled=True, axis_index_groups=ALONG_Z)]
    ppermute x4, waiting for transfers between devices: 9.35 us -> 3.14 us  [to_neighbours(): lax.ppermute(corner, ('seq', 'col'), both)]
    convert_element_type x2 -> x1, other arithmetic: 4.98 us -> 0.09 us  [local(): grad_m1 = sum((v.astype(F32) for v in got), half_m1.astype(F32)).astype(BF)]
    pallas_call x17 -> x19, Pallas kernels: 191 us -> 187 us  [the longest x18 187 us: call(): pl.pallas_call(whole, out_shape=shapes, in_specs=specs, out_specs=[anywhe...]
    pallas_call x3 -> x2, Pallas kernels: 13 us -> 9.41 us  [both_cores(): pl.pallas_call(add_kernel, grid=(4,), out_shape=jax.ShapeDtypeStruct(shap...]
    ppermute x31 -> x18, waiting for transfers between devices: 34.6 us -> 33.5 us  [the longest x6 18.3 us: local(): lax.ppermute(v, ('img', 'col'), from_x(4 - d))]
  transfers between devices with their start and end apart: 73 -> 58, of which waited for: 16 -> 13; matrix products, arithmetic and copies ran while one was open for 9% -> 4% of each run, Pallas kernels for 32% -> 41%
where the time goes in v2:
time: 404 us; the launch traced here: 396 us
  Pallas kernels  202 us (50%)
  starting transfers between devices  97.6 us (24%)
  waiting for transfers between devices  60.8 us (15%)
  local copies, waits for them, and re-layouts  28.5 us (7%)
  other arithmetic  4.44 us (1%)
    pallas_call x18, Pallas kernels, call(): pl.pallas_call(whole, out_shape=shapes, in_specs=specs, out_specs=[anywhe...  187 us
    ppermute x6, waiting for transfers between devices, local(): lax.ppermute(v, ('img', 'col'), from_x(4 - d))  18.3 us
    unnamed x129, local copies, waits for them, and re-layouts  17.2 us
    ppermute x6, waiting for transfers between devices, along_z(): return [value] + [lax.ppermute(value, 'img', from_z(d)) for d in (1, 2, 3)]  15.1 us
    all_to_all x3, waiting for transfers between devices, scattered_z(): lax.all_to_all(value, 'img', 0, 0, tiled=True, axis_index_groups=ALONG_Z)  13.7 us
    all_to_all x3, starting transfers between devices, scattered_z(): lax.all_to_all(value, 'img', 0, 0, tiled=True, axis_index_groups=ALONG_Z)  12.2 us
    ppermute x6, starting transfers between devices, along_x(): lax.ppermute(value, ('img', 'col'), from_x(d))  12.2 us
    ppermute x6, starting transfers between devices, local(): lax.ppermute(v, ('img', 'col'), from_x(4 - d))  11.7 us
  transfers between devices with their start and end apart: 58, of which 13 were waited for; matrix products, arithmetic and copies ran while one was open for 4% of the time, Pallas kernels for 41%

profile of v2, /device:TPU:0, one launch (start us, length us, event | category | flops | bytes accessed | tf_op | source)
XLA Modules:
  0.0 396.4 jit_solution(16302753077748821868)
XLA Ops:
  0.7 2.8 shard_map.445
  5.5 3.6 collective-permute-start.8
  9.1 4.3 %all-to-all-start = ((bf16[4,6,16,512]{3,2,1,0:T(8,128)(2,1)}), bf16[4,6,16,512]{3,2,1,0:T(8,128)(2,1)S(1)}, u32[]{:S(2)}, u32[]{:S(2)}) async-start(bf16[4,6,16,512]{3,2,1,0:T(8,128)(2,1)} %get-tuple-element.113), calls=%async_computation | async-start | bytes 786432 | tf_op jit(solution)/shard_map/all_to_all | solution.py:1031
  16.2 4.3 %shard_map.446.refs_9_.refs_0_.refs_10_ = bf16[1024,512]{1,0:T(8,128)(2,1)} custom-call(bf16[784,512]{1,0:T(8,128)(2,1)} %reshape.137.refs_0_.refs_19_.refs_15_, f32[1,512]{1,0:T(1,128)} %get-tuple-element.285.refs_1_.refs_17_, f32[1,512]{1,0:T(1,128)} %get-tuple-element.284.refs_2_, bf16[1024,784]{1,0:T(8,128)(2,1)} %constant.82.clone.refs_3_.refs_7_), custom_call_target="tpu_custom_call" | custom-call | flops 12000000000 | bytes 4000000 | tf_op jit(solution)/shard_map/pallas_call | solution.py:264
  21.2 2.5 collective-permute-start.1
  27.2 13.6 %collective-permute-done.2.refs_4_.refs_6_ = bf16[4,6,16,512]{3,2,1,0:T(8,128)(2,1)S(1)} collective-permute-done((bf16[4,6,16,512]{3,2,1,0:T(8,128)(2,1)S(1)}, bf16[4,6,16,512]{3,2,1,0:T(8,128)(2,1)S(1)}, u32[]{:S(2)}, u32[]{:S(2)}) %collective-permute-start.2) | collective-permute-done | bytes 393248 | tf_op jit(solution)/shard_map/ppermute | solution.py:1026
  47.8 2.7 collective-permute-start.11
  53.1 18.3 %shard_map.447 = (bf16[3,32,16,512]{3,2,1,0:T(8,128)(2,1)}, bf16[1024,1536]{1,0:T(8,128)(2,1)}, bf16[4,4,256,128]{3,2,1,0:T(8,128)(2,1)}, bf16[4,4,256,128]{3,2,1,0:T(8,128)(2,1)}, bf16[784,512]{1,0:T(8,128)(2,1)}) custom-call(s32[3]{0:T(128)} %pad_add_fusion.1.refs_0_.refs_2_.refs_1_.refs_5_, bf16[4,6,16,512]{3,2,1,0:T(8,128)(2,1)} %copy-done.15, ...), custom_call_target="tpu_custom_call" | custom-call | flops 54000001024 | bytes 18000000 | tf_op jit(solution)/shard_map/pallas_call | solution.py:264
  71.4 2.9 shard_map.448
  74.3 3.9 all-to-all-start.2
  86.5 2.7 collective-permute-start.18
  92.7 16.4 %shard_map.450 = (bf16[9,32,16,512]{3,2,1,0:T(8,128)(2,1)}, f32[784,512]{1,0:T(8,128)}, bf16[784,512]{1,0:T(8,128)(2,1)}, bf16[784,2048]{1,0:T(8,128)(2,1)}, bf1...) custom-call(bf16[16,3,16,512]{3,2,1,0:T(8,128)(2,1)} %get-tuple-elem, ...), custom_call_target="tpu_custom_call" | custom-call | flops 44999999488 | bytes 15000000 | tf_op jit(solution)/shard_map/pallas_call | solution.py:264
  109.1 3.2 collective-permute-start.23
  113.0 2.9 collective-permute-start.22
  116.6 2.7 shard_map.451
  119.3 3.6 all-to-all-start.1
  123.6 20.6 %shard_map.452 = (bf16[3,32,16,512]{3,2,1,0:T(8,128)(2,1)}, bf16[1024,512]{1,0:T(8,128)(2,1)}, bf16[1024,1536]{1,0:T(8,128)(2,1)}, bf16[4,4,256,128]{3,2,1,0:T(8...) custom-call(s32[25,256]{1,0:T(8,128)} %reshape.141.refs_0_.refs_11_., ...), custom_call_target="tpu_custom_call" | custom-call | flops 54000001024 | bytes 18000000 | tf_op jit(solution)/shard_map/pallas_call | solution.py:264
  144.2 7.9 %all-to-all-done.1 = bf16[4,4,9,16,512]{4,3,2,1,0:T(8,128)(2,1)S(1)} async-done(((bf16[4,4,9,16,512]{4,3,2,1,0:T(8,128)(2,1)}), bf16[4,4,9,16,512]{4,3,2,1,0:T(8,128)(2,1)S(1)}, u32[]{:S(2)}, u32[]{:S(2)}) %all-to-all-start.1) | async-done | bytes 2359328 | tf_op jit(solution)/shard_map/all_to_all | solution.py:916
  156.3 2.5 collective-permute-start.27
  160.6 3.1 collective-permute-done.27.refs_7_
  164.4 25.9 %shard_map.454 = (bf16[784,512]{1,0:T(8,128)(2,1)}, f32[784,512]{1,0:T(8,128)}, f32[4,512]{1,0:T(4,128)}, f32[1,2048]{1,0:T(1,128)}, bf16[784,512]{1,0:T(8,128)(...) custom-call(s32[3]{0:T(128)} %pad_add_fusion.1.refs_0_.refs_2_.refs_, ...), custom_call_target="tpu_custom_call" | custom-call | flops 102000001024 | bytes 34000000 | tf_op jit(solution)/shard_map/pallas_call | solution.py:264
  191.3 2.9 collective-permute-start.30
  196.7 4.6 %shard_map.455.refs_0_ = bf16[4,4,9,16,512]{4,3,2,1,0:T(8,128)(2,1)} custom-call(bf16[4,4,9,16,512]{4,3,2,1,0:T(8,128)(2,1)} %get-tuple-element.129.refs_0_, bf16[4,4,9,16,512]{4,3,2,1,0:T(8,128)(2,1)} %copy-done.4), custom_call_target="tpu_custom_call" | custom-call | flops 2359296 | bytes 7077888 | tf_op jit(solution)/shard_map/pallas_call | solution.py:930
  201.3 3.6 all-to-all-start.3
  205.6 22.0 %shard_map.457 = (bf16[1024,1536]{1,0:T(8,128)(2,1)}, f32[3,512]{1,0:T(4,128)}, f32[16,256]{1,0:T(8,128)}, bf16[1024,512]{1,0:T(8,128)(2,1)}, bf16[96,512]{1,0:T...) custom-call(bf16[4,4,9,16,512]{4,3,2,1,0:T(8,128)(2,1)} %shard_map.455.refs_0_, ...), custom_call_target="tpu_custom_call" | custom-call | flops 60000002048 | bytes 20000000 | tf_op jit(solution)/shard_map/pallas_call | solution.py:264
  227.6 3.5 collective-permute-start.34
  233.0 6.1 %shard_map.458 = (bf16[4,4,3,16,512]{4,3,2,1,0:T(8,128)(2,1)}, bf16[4,4,3,16,512]{4,3,2,1,0:T(8,128)(2,1)}) custom-call(s32[3]{0:T(128)} %pad_add_fusion.1.refs_0_.refs_2_.refs_1_.refs_5_, bf16[1024,512]{1,0:T(8,128)(2,1)} %get-tuple-element.122.refs_1_, bf16[1024,1536]{1,0:T(8,128)(2,1)} %get-tuple-element.140.refs_2_), custom_call_target="tpu_custom_call" | custom-call | flops 12000000000 | bytes 4000000 | tf_op jit(solution)/shard_map/pallas_call | solution.py:264
  240.6 2.7 shard_map.456
  243.9 3.4 collective-permute-start.38
  249.7 15.7 %shard_map.459 = (f32[784,512]{1,0:T(8,128)}, bf16[784,2048]{1,0:T(8,128)(2,1)}, bf16[4,4,8,16,512]{4,3,2,1,0:T(8,128)(2,1)}, bf16[4,4,8,16,512]{4,3,2,1,0:T(8,1...) custom-call(bf16[9,16,512]{2,1,0:T(8,128)(2,1)} %get-tuple-element.131.refs_0_, ...), custom_call_target="tpu_custom_call" | custom-call | flops 48000000000 | bytes 16000000 | tf_op jit(solution)/shard_map/pallas_call | solution.py:264
  265.6 2.0 collective-permute-start.42
  269.7 10.4 %shard_map.461 = (f32[784,512]{1,0:T(8,128)}, bf16[512,512]{1,0:T(8,128)(2,1)}, f32[3,512]{1,0:T(4,128)}, bf16[1024,512]{1,0:T(8,128)(2,1)}) custom-call(bf16[9,16,512]{2,1,0:T(8,128)(2,1)} %copy-done.16, f32[784,512]{1,0:T(8,128)} %get-tuple-element.157.refs_1_, bf16[784,2048]{1,0:T(8,128)(2,1)} %get-tuple-element.158.refs_2_, ...), custom_call_target="tpu_custom_call" | custom-call | flops 24000000000 | bytes 8000000 | tf_op jit(solution)/shard_map/pallas_call | solution.py:264
  281.8 4.8 %shard_map.460.refs_0_ = bf16[4,4,11,16,512]{4,3,2,1,0:T(8,128)(2,1)} custom-call(bf16[4,4,8,16,512]{4,3,2,1,0:T(8,128)(2,1)} %get-tuple-element.151.refs_0_, bf16[4,4,8,16,512]{4,3,2,1,0:T(8,128)(2,1)} %copy-done.6, bf16[4,4,3,16,512]{4,3,2,1,0:T(8,128)(2,1)} %get-tuple-element.141.refs_1_.refs_2_, bf16[4,4,3,16,512]{4,3,2,1,0:T(8,128)(2,1)} %copy-done.12), custom_call_target="tpu_custom_call" | custom-call | flops 2883584 | bytes 8650752 | tf_op jit(solution)/shard_map/pallas_call | solution.py:930
  286.6 5.0 %all-to-all-start.4 = ((bf16[4,4,11,16,512]{4,3,2,1,0:T(8,128)(2,1)}), bf16[4,4,11,16,512]{4,3,2,1,0:T(8,128)(2,1)S(1)}, u32[]{:S(2)}, u32[]{:S(2)}) async-start(bf16[4,4,11,16,512]{4,3,2,1,0:T(8,128)(2,1)} %shard_map.460.refs_0_), calls=%async_computation.4 | async-start | bytes 5767168 | tf_op jit(solution)/shard_map/all_to_all | solution.py:916
  292.2 24.8 %shard_map.462 = (bf16[4,4,4,16,512]{4,3,2,1,0:T(8,128)(2,1)}, bf16[4,4,4,16,512]{4,3,2,1,0:T(8,128)(2,1)}, f32[784,512]{1,0:T(8,128)}, f32[40,512]{1,0:T(8,128)}) custom-call(bf16[4,4,11,16,512]{4,3,2,1,0:T(8,128)(2,1)} %shard_map.460.refs_0_, bf16[9,16,512]{2,1,0:T(8,128)(2,1)} %copy-done.16, bf16[9,16,512]{2,1,0:T(8,128)(2,1)} %collective-permute-done.40.refs_2_.refs_1_, ...), custom_call_target="tpu_custom_call" | custom-call | flops 77999996928 | bytes 26000000 | tf_op jit(solution)/shard_map/pallas_call | solution.py:264
  317.6 2.1 collective-permute-done.44.refs_5_
  320.2 5.9 %all-to-all-done.4.refs_3_ = bf16[4,4,11,16,512]{4,3,2,1,0:T(8,128)(2,1)S(1)} async-done(((bf16[4,4,11,16,512]{4,3,2,1,0:T(8,128)(2,1)}), bf16[4,4,11,16,512]{4,3,2,1,0:T(8,128)(2,1)S(1)}, u32[]{:S(2)}, u32[]{:S(2)}) %all-to-all-start.4) | async-done | bytes 2883616 | tf_op jit(solution)/shard_map/all_to_all | solution.py:916
  327.7 4.1 %shard_map.463 = (bf16[16,5,16,512]{3,2,1,0:T(8,128)(2,1)}, bf16[11,16,512]{2,1,0:T(8,128)(2,1)}, bf16[11,16,512]{2,1,0:T(8,128)(2,1)}, bf16[11,16,512]{2,1,0:T(8,128)(2,1)}, bf16[11,16,512]{2,1,0:T(8,128)(2,1)}) custom-call(s32[3]{0:T(128)} %pad_add_fusion.1.refs_0_.refs_2_.refs_1_.refs_5_, bf16[4,4,4,16,512]{4,3,2,1,0:T(8,128)(2,1)} %get-tuple-element.176.refs_1_, ...), custom_call_target="tpu_custom_call" | custom-call | flops 15000000512 | bytes 5000000 | tf_op jit(solution)/shard_map/pallas_call | solution.py:264
  331.9 3.8 all-to-all-start.5
  337.6 2.7 collective-permute-start.46
  341.7 16.0 %collective-permute-done.45.refs_2_ = bf16[11,16,512]{2,1,0:T(8,128)(2,1)S(1)} collective-permute-done((bf16[11,16,512]{2,1,0:T(8,128)(2,1)S(1)}, bf16[11,16,512]{2,1,0:T(8,128)(2,1)S(1)}, u32[]{:S(2)}, u32[]{:S(2)}) %collective-permute-start.45) | collective-permute-done | bytes 180256 | tf_op jit(solution)/shard_map/ppermute | solution.py:1191
  357.8 2.3 collective-permute-done.46.refs_3_
  361.3 2.7 shard_map.464
  369.4 3.1 reshape.149
  372.4 7.7 %all-to-all-start.6 = ((f32[64,16,128]{2,1,0:T(8,128)}), f32[64,16,128]{2,1,0:T(8,128)S(1)}, u32[]{:S(2)}, u32[]{:S(2)}) async-start(f32[64,16,128]{2,1,0:T(8,128)} %get-tuple-element.197), calls=%async_computation.6 | async-start | bytes 1048576 | tf_op jit(solution)/shard_map/all_to_all | solution.py:1194
  381.6 5.8 %shard_map.465 = (f32[2,16,1536]{2,1,0:T(8,128)}, f32[2,16,1536]{2,1,0:T(8,128)}, f32[2,16,1536]{2,1,0:T(8,128)}, f32[2,16,512]{2,1,0:T(8,128)}, f32[2,16,512]{2...) custom-call(bf16[9,16,512]{2,1,0:T(8,128)(2,1)} %copy-done.16, ...), custom_call_target="tpu_custom_call" | custom-call | flops 8000000000 | bytes 8000000 | tf_op jit(solution)/shard_map/pallas_call | solution.py:948
  387.5 5.3 %all-to-all-done.6.refs_0_ = f32[64,16,128]{2,1,0:T(8,128)S(1)} async-done(((f32[64,16,128]{2,1,0:T(8,128)}), f32[64,16,128]{2,1,0:T(8,128)S(1)}, u32[]{:S(2)}, u32[]{:S(2)}) %all-to-all-start.6) | async-done | bytes 524320 | tf_op jit(solution)/shard_map/all_to_all | solution.py:1194
  393.6 2.4 shard_map.466
  (260 shorter events, 68.8 us)
Async XLA Ops:
  3.5 22.7 %collective-permute-start.9 = (bf16[6,16,512]{2,1,0:T(8,128)(2,1)}, bf16[6,16,512]{2,1,0:T(8,128)(2,1)S(1)}, u32[]{:S(2)}, u32[]{:S(2)}) collective-permute-start(bf16[6,16,512]{2,1,0:T(8,128)(2,1)} %get-tuple-element.117.refs_1_), channel_id=1, source_target_pairs={{96,0},{104,8},{112,16},{120,24},{0,32},{8,40},{16,48},{24,56},{32... | collective-permute-start | bytes 294920 | tf_op jit(solution)/shard_map/ppermute | solution.py:1026
  5.5 21.7 %collective-permute-start.8 = (bf16[6,16,512]{2,1,0:T(8,128)(2,1)}, bf16[6,16,512]{2,1,0:T(8,128)(2,1)S(1)}, u32[]{:S(2)}, u32[]{:S(2)}) collective-permute-start(bf16[6,16,512]{2,1,0:T(8,128)(2,1)} %get-tuple-element.117.refs_1_), channel_id=1, source_target_pairs={{64,0},{72,8},{80,16},{88,24},{96,32},{104,40},{112,48},{120,56},{... | collective-permute-start | bytes 294920 | tf_op jit(solution)/shard_map/ppermute | solution.py:1026
  9.1 12.1 %all-to-all-start = ((bf16[4,6,16,512]{3,2,1,0:T(8,128)(2,1)}), bf16[4,6,16,512]{3,2,1,0:T(8,128)(2,1)S(1)}, u32[]{:S(2)}, u32[]{:S(2)}) async-start(bf16[4,6,16,512]{3,2,1,0:T(8,128)(2,1)} %get-tuple-element.113), calls=%async_computation | async-start | bytes 786432 | tf_op jit(solution)/shard_map/all_to_all | solution.py:1031
  21.2 19.7 %collective-permute-start.2 = (bf16[4,6,16,512]{3,2,1,0:T(8,128)(2,1)S(1)}, bf16[4,6,16,512]{3,2,1,0:T(8,128)(2,1)S(1)}, u32[]{:S(2)}, u32[]{:S(2)}) collective-permute-start(bf16[4,6,16,512]{3,2,1,0:T(8,128)(2,1)S(1)} %all-to-all-done.refs_1_.refs_3_), channel_id=1, source_target_pairs={{96,0},{104,8},{112,16},{120,24},{0,32},{8,40},{16,48},{24,56},{32... | collective-permute-start | bytes 1179656 | tf_op jit(solution)/shard_map/ppermute | solution.py:1026
  21.2 19.7 %collective-permute-start.1 = (bf16[4,6,16,512]{3,2,1,0:T(8,128)(2,1)S(1)}, bf16[4,6,16,512]{3,2,1,0:T(8,128)(2,1)S(1)}, u32[]{:S(2)}, u32[]{:S(2)}) collective-permute-start(bf16[4,6,16,512]{3,2,1,0:T(8,128)(2,1)S(1)} %all-to-all-done.refs_1_.refs_3_), channel_id=1, source_target_pairs={{64,0},{72,8},{80,16},{88,24},{96,32},{104,40},{112,48},{120,56},{... | collective-permute-start | bytes 1179656 | tf_op jit(solution)/shard_map/ppermute | solution.py:1026
  23.6 18.9 %collective-permute-start = (bf16[4,6,16,512]{3,2,1,0:T(8,128)(2,1)S(1)}, bf16[4,6,16,512]{3,2,1,0:T(8,128)(2,1)S(1)}, u32[]{:S(2)}, u32[]{:S(2)}) collective-permute-start(bf16[4,6,16,512]{3,2,1,0:T(8,128)(2,1)S(1)} %all-to-all-done.refs_1_.refs_3_), channel_id=1, source_target_pairs={{32,0},{40,8},{48,16},{56,24},{64,32},{72,40},{80,48},{88,56},{96,... | collective-permute-start | bytes 1179656 | tf_op jit(solution)/shard_map/ppermute | solution.py:1026
  26.2 17.4 %collective-permute-start.7 = (bf16[6,16,512]{2,1,0:T(8,128)(2,1)S(1)}, bf16[6,16,512]{2,1,0:T(8,128)(2,1)S(1)}, u32[]{:S(2)}, u32[]{:S(2)}) collective-permute-start(bf16[6,16,512]{2,1,0:T(8,128)(2,1)S(1)} %copy-done.43), channel_id=1, source_target_pairs={{32,0},{40,8},{48,16},{56,24},{64,32},{72,40},{80,48},{88,56},{96,... | collective-permute-start | bytes 294920 | tf_op jit(solution)/shard_map/ppermute | solution.py:1026
  27.2 20.7 %collective-permute-start.3 = (bf16[4,6,16,512]{3,2,1,0:T(8,128)(2,1)S(1)}, bf16[4,6,16,512]{3,2,1,0:T(8,128)(2,1)S(1)}, u32[]{:S(2)}, u32[]{:S(2)}) collective-permute-start(bf16[4,6,16,512]{3,2,1,0:T(8,128)(2,1)S(1)} %all-to-all-done.refs_1_.refs_3_), channel_id=1, source_target_pairs={{0,8},{8,0},{16,24},{24,16},{32,40},{40,32},{48,56},{56,48},{64,72... | collective-permute-start | bytes 1179656 | tf_op jit(solution)/shard_map/ppermute | solution.py:920
  40.8 11.4 %collective-permute-start.5 = (bf16[4,6,16,512]{3,2,1,0:T(8,128)(2,1)S(1)}, bf16[4,6,16,512]{3,2,1,0:T(8,128)(2,1)S(1)}, u32[]{:S(2)}, u32[]{:S(2)}) collective-permute-start(bf16[4,6,16,512]{3,2,1,0:T(8,128)(2,1)S(1)} %collective-permute-done.1.refs_3_.refs_5_), channel_id=1, source_target_pairs={{0,8},{8,0},{16,24},{24,16},{32,40},{40,32},{48,56},{56,48},{64,72... | collective-permute-start | bytes 1179656 | tf_op jit(solution)/shard_map/ppermute | solution.py:920
  46.0 32.7 %collective-permute-start.12 = (bf16[4,6,16,512]{3,2,1,0:T(8,128)(2,1)}, bf16[4,6,16,512]{3,2,1,0:T(8,128)(2,1)}, u32[]{:S(2)}, u32[]{:S(2)}) collective-permute-start(bf16[4,6,16,512]{3,2,1,0:T(8,128)(2,1)} %shard_map.449.refs_11_), channel_id=1, source_target_pairs={{17,0},{25,8},{0,16},{8,24},{16,1},{24,9},{1,17},{9,25},{49,32},{5... | collective-permute-start | bytes 1179656 | tf_op jit(solution)/shard_map/ppermute | solution.py:1029
  47.8 31.4 %collective-permute-start.11 = (bf16[4,6,16,512]{3,2,1,0:T(8,128)(2,1)}, bf16[4,6,16,512]{3,2,1,0:T(8,128)(2,1)S(1)}, u32[]{:S(2)}, u32[]{:S(2)}) collective-permute-start(bf16[4,6,16,512]{3,2,1,0:T(8,128)(2,1)} %shard_map.449.refs_11_), channel_id=1, source_target_pairs={{1,0},{9,8},{17,16},{25,24},{0,1},{8,9},{16,17},{24,25},{33,32},{4... | collective-permute-start | bytes 1179656 | tf_op jit(solution)/shard_map/ppermute | solution.py:1029
  50.5 28.8 %collective-permute-start.10 = (bf16[4,6,16,512]{3,2,1,0:T(8,128)(2,1)}, bf16[4,6,16,512]{3,2,1,0:T(8,128)(2,1)}, u32[]{:S(2)}, u32[]{:S(2)}) collective-permute-start(bf16[4,6,16,512]{3,2,1,0:T(8,128)(2,1)} %shard_map.449.refs_11_), channel_id=1, source_target_pairs={{16,0},{24,8},{1,16},{9,24},{17,1},{25,9},{0,17},{8,25},{48,32},{5... | collective-permute-start | bytes 1179656 | tf_op jit(solution)/shard_map/ppermute | solution.py:1029
  74.3 17.9 %all-to-all-start.2 = ((bf16[16,3,16,512]{3,2,1,0:T(8,128)(2,1)}), bf16[16,3,16,512]{3,2,1,0:T(8,128)(2,1)S(1)}, u32[]{:S(2)}, u32[]{:S(2)}) async-start(bf16[16,3,16,512]{3,2,1,0:T(8,128)(2,1)} %get-tuple-element.115.refs_0_), calls=%async_computation.2 | async-start | bytes 1572864 | tf_op jit(solution)/shard_map/all_to_all | solution.py:1076
  78.7 10.4 %collective-permute-start.16 = (bf16[4,6,16,512]{3,2,1,0:T(8,128)(2,1)}, bf16[4,6,16,512]{3,2,1,0:T(8,128)(2,1)}, u32[]{:S(2)}, u32[]{:S(2)}) collective-permute-start(bf16[4,6,16,512]{3,2,1,0:T(8,128)(2,1)} %collective-permute-done.12.refs_14_), channel_id=1, source_target_pairs={{0,8},{8,0},{16,24},{24,16},{32,40},{40,32},{48,56},{56,48},{64,72... | collective-permute-start | bytes 1179656 | tf_op jit(solution)/shard_map/ppermute | solution.py:920
  79.2 11.4 %collective-permute-start.15 = (bf16[4,6,16,512]{3,2,1,0:T(8,128)(2,1)S(1)}, bf16[4,6,16,512]{3,2,1,0:T(8,128)(2,1)}, u32[]{:S(2)}, u32[]{:S(2)}) collective-permute-start(bf16[4,6,16,512]{3,2,1,0:T(8,128)(2,1)S(1)} %collective-permute-done.11.refs_13_), channel_id=1, source_target_pairs={{0,8},{8,0},{16,24},{24,16},{32,40},{40,32},{48,56},{56,48},{64,72... | collective-permute-start | bytes 1179656 | tf_op jit(solution)/shard_map/ppermute | solution.py:920
  79.3 13.3 %collective-permute-start.14 = (bf16[4,6,16,512]{3,2,1,0:T(8,128)(2,1)}, bf16[4,6,16,512]{3,2,1,0:T(8,128)(2,1)}, u32[]{:S(2)}, u32[]{:S(2)}) collective-permute-start(bf16[4,6,16,512]{3,2,1,0:T(8,128)(2,1)} %collective-permute-done.10.refs_12_), channel_id=1, source_target_pairs={{0,8},{8,0},{16,24},{24,16},{32,40},{40,32},{48,56},{56,48},{64,72... | collective-permute-start | bytes 1179656 | tf_op jit(solution)/shard_map/ppermute | solution.py:920
  84.6 27.7 %collective-permute-start.19 = (bf16[9,16,512]{2,1,0:T(8,128)(2,1)S(1)}, bf16[9,16,512]{2,1,0:T(8,128)(2,1)S(1)}, u32[]{:S(2)}, u32[]{:S(2)}) collective-permute-start(bf16[9,16,512]{2,1,0:T(8,128)(2,1)S(1)} %copy-done.39), channel_id=1, source_target_pairs={{17,0},{25,8},{0,16},{8,24},{16,1},{24,9},{1,17},{9,25},{49,32},{5... | collective-permute-start | bytes 442376 | tf_op jit(solution)/shard_map/ppermute | solution.py:1029
  86.5 26.5 %collective-permute-start.18 = (bf16[9,16,512]{2,1,0:T(8,128)(2,1)S(1)}, bf16[9,16,512]{2,1,0:T(8,128)(2,1)S(1)}, u32[]{:S(2)}, u32[]{:S(2)}) collective-permute-start(bf16[9,16,512]{2,1,0:T(8,128)(2,1)S(1)} %copy-done.39), channel_id=1, source_target_pairs={{1,0},{9,8},{17,16},{25,24},{0,1},{8,9},{16,17},{24,25},{33,32},{4... | collective-permute-start | bytes 442376 | tf_op jit(solution)/shard_map/ppermute | solution.py:1029
  89.2 26.8 %collective-permute-start.17 = (bf16[9,16,512]{2,1,0:T(8,128)(2,1)S(1)}, bf16[9,16,512]{2,1,0:T(8,128)(2,1)S(1)}, u32[]{:S(2)}, u32[]{:S(2)}) collective-permute-start(bf16[9,16,512]{2,1,0:T(8,128)(2,1)S(1)} %copy-done.39), channel_id=1, source_target_pairs={{16,0},{24,8},{1,16},{9,24},{17,1},{25,9},{0,17},{8,25},{48,32},{5... | collective-permute-start | bytes 442376 | tf_op jit(solution)/shard_map/ppermute | solution.py:1029
  92.3 30.7 %collective-permute-start.20 = (bf16[16,3,16,512]{3,2,1,0:T(8,128)(2,1)S(1)}, bf16[16,3,16,512]{3,2,1,0:T(8,128)(2,1)}, u32[]{:S(2)}, u32[]{:S(2)}) collective-permute-start(bf16[16,3,16,512]{3,2,1,0:T(8,128)(2,1)S(1)} %all-to-all-done.2.refs_2_), channel_id=1, source_target_pairs={{0,8},{8,0},{16,24},{24,16},{32,40},{40,32},{48,56},{56,48},{64,72... | collective-permute-start | bytes 2359304 | tf_op jit(solution)/shard_map/ppermute | solution.py:920
  109.1 13.8 %collective-permute-start.23 = (bf16[16,512]{1,0:T(8,128)(2,1)}, bf16[16,512]{1,0:T(8,128)(2,1)S(1)}, u32[]{:S(2)}, u32[]{:S(2)}) collective-permute-start(bf16[16,512]{1,0:T(8,128)(2,1)} %get-tuple-element.121), channel_id=1, source_target_pairs={{0,7},{1,6},{2,1},{3,0},{4,3},{5,2},{6,5},{7,4},{8,15},{9,14},{10,... | collective-permute-start | bytes 49160 | tf_op jit(solution)/shard_map/ppermute | solution.py:890
  112.3 10.7 %collective-permute-start.21 = (bf16[96,512]{1,0:T(8,128)(2,1)}, bf16[96,512]{1,0:T(8,128)(2,1)S(1)}, u32[]{:S(2)}, u32[]{:S(2)}) collective-permute-start(bf16[96,512]{1,0:T(8,128)(2,1)} %get-tuple-element.119), channel_id=1, source_target_pairs={{0,6},{2,0},{4,2},{6,4},{1,7},{3,1},{5,3},{7,5},{8,14},{10,8},{12,... | collective-permute-start | bytes 294920 | tf_op jit(solution)/shard_map/ppermute | solution.py:888
  119.3 32.8 %all-to-all-start.1 = ((bf16[4,4,9,16,512]{4,3,2,1,0:T(8,128)(2,1)}), bf16[4,4,9,16,512]{4,3,2,1,0:T(8,128)(2,1)S(1)}, u32[]{:S(2)}, u32[]{:S(2)}) async-start(bf16[4,4,9,16,512]{4,3,2,1,0:T(8,128)(2,1)} %shard_map.451), calls=%async_computation.1 | async-start | bytes 4718592 | tf_op jit(solution)/shard_map/all_to_all | solution.py:916
  153.4 10.4 %collective-permute-start.24 = (bf16[16,9,16,512]{3,2,1,0:T(8,128)(2,1)}, bf16[16,9,16,512]{3,2,1,0:T(8,128)(2,1)}, u32[]{:S(2)}, u32[]{:S(2)}) collective-permute-start(bf16[16,9,16,512]{3,2,1,0:T(8,128)(2,1)} %shard_map.453.refs_1_), channel_id=1, source_target_pairs={{0,8},{8,0},{16,24},{24,16},{32,40},{40,32},{48,56},{56,48},{64,72... | collective-permute-start | bytes 7077896 | tf_op jit(solution)/shard_map/ppermute | solution.py:920
  190.5 14.4 %collective-permute-start.29 = (bf16[96,512]{1,0:T(8,128)(2,1)}, bf16[96,512]{1,0:T(8,128)(2,1)S(1)}, u32[]{:S(2)}, u32[]{:S(2)}) collective-permute-start(bf16[96,512]{1,0:T(8,128)(2,1)} %get-tuple-element.133), channel_id=1, source_target_pairs={{0,6},{2,0},{4,2},{6,4},{1,7},{3,1},{5,3},{7,5},{8,14},{10,8},{12,... | collective-permute-start | bytes 294920 | tf_op jit(solution)/shard_map/ppermute | solution.py:888
  191.3 13.7 %collective-permute-start.30 = (bf16[96,512]{1,0:T(8,128)(2,1)}, bf16[96,512]{1,0:T(8,128)(2,1)S(1)}, u32[]{:S(2)}, u32[]{:S(2)}) collective-permute-start(bf16[96,512]{1,0:T(8,128)(2,1)} %get-tuple-element.134), channel_id=1, source_target_pairs={{0,1},{1,0},{2,3},{3,2},{4,5},{5,4},{6,7},{7,6},{8,9},{9,8},{10,11... | collective-permute-start | bytes 294920 | tf_op jit(solution)/shard_map/ppermute | solution.py:889
  194.2 10.7 %collective-permute-start.31 = (bf16[16,512]{1,0:T(8,128)(2,1)}, bf16[16,512]{1,0:T(8,128)(2,1)S(1)}, u32[]{:S(2)}, u32[]{:S(2)}) collective-permute-start(bf16[16,512]{1,0:T(8,128)(2,1)} %get-tuple-element.135), channel_id=1, source_target_pairs={{0,7},{1,6},{2,1},{3,0},{4,3},{5,2},{6,5},{7,4},{8,15},{9,14},{10,... | collective-permute-start | bytes 49160 | tf_op jit(solution)/shard_map/ppermute | solution.py:890
  201.3 38.0 %all-to-all-start.3 = ((bf16[4,4,9,16,512]{4,3,2,1,0:T(8,128)(2,1)}), bf16[4,4,9,16,512]{4,3,2,1,0:T(8,128)(2,1)S(1)}, u32[]{:S(2)}, u32[]{:S(2)}) async-start(bf16[4,4,9,16,512]{4,3,2,1,0:T(8,128)(2,1)} %shard_map.455.refs_0_), calls=%async_computation.3 | async-start | bytes 4718592 | tf_op jit(solution)/shard_map/all_to_all | solution.py:916
  227.6 16.3 %collective-permute-start.34 = (bf16[16,512]{1,0:T(8,128)(2,1)}, bf16[16,512]{1,0:T(8,128)(2,1)S(1)}, u32[]{:S(2)}, u32[]{:S(2)}) collective-permute-start(bf16[16,512]{1,0:T(8,128)(2,1)} %get-tuple-element.146), channel_id=1, source_target_pairs={{0,3},{1,2},{2,5},{3,4},{4,7},{5,6},{6,1},{7,0},{8,11},{9,10},{10,... | collective-permute-start | bytes 49160 | tf_op jit(solution)/shard_map/ppermute | solution.py:890
  231.1 16.2 %collective-permute-start.32 = (bf16[96,512]{1,0:T(8,128)(2,1)}, bf16[96,512]{1,0:T(8,128)(2,1)S(1)}, u32[]{:S(2)}, u32[]{:S(2)}) collective-permute-start(bf16[96,512]{1,0:T(8,128)(2,1)} %get-tuple-element.144), channel_id=1, source_target_pairs={{0,2},{2,4},{4,6},{6,0},{1,3},{3,5},{5,7},{7,1},{8,10},{10,12},{12... | collective-permute-start | bytes 294920 | tf_op jit(solution)/shard_map/ppermute | solution.py:888
  232.4 16.6 %collective-permute-start.33 = (bf16[96,512]{1,0:T(8,128)(2,1)}, bf16[96,512]{1,0:T(8,128)(2,1)S(1)}, u32[]{:S(2)}, u32[]{:S(2)}) collective-permute-start(bf16[96,512]{1,0:T(8,128)(2,1)} %get-tuple-element.145), channel_id=1, source_target_pairs={{0,1},{1,0},{2,3},{3,2},{4,5},{5,4},{6,7},{7,6},{8,9},{9,8},{10,11... | collective-permute-start | bytes 294920 | tf_op jit(solution)/shard_map/ppermute | solution.py:889
  239.1 41.0 %collective-permute-start.36 = (bf16[4,4,3,16,512]{4,3,2,1,0:T(8,128)(2,1)}, bf16[4,4,3,16,512]{4,3,2,1,0:T(8,128)(2,1)S(1)}, u32[]{:S(2)}, u32[]{:S(2)}) collective-permute-start(bf16[4,4,3,16,512]{4,3,2,1,0:T(8,128)(2,1)} %get-tuple-element.153), channel_id=1, source_target_pairs={{0,8},{8,0},{16,24},{24,16},{32,40},{40,32},{48,56},{56,48},{64,72... | collective-permute-start | bytes 2359304 | tf_op jit(solution)/shard_map/ppermute | solution.py:920
  243.3 22.1 %collective-permute-start.37 = (bf16[9,16,512]{2,1,0:T(8,128)(2,1)}, bf16[9,16,512]{2,1,0:T(8,128)(2,1)S(1)}, u32[]{:S(2)}, u32[]{:S(2)}) collective-permute-start(bf16[9,16,512]{2,1,0:T(8,128)(2,1)} %get-tuple-element.154), channel_id=1, source_target_pairs={{17,0},{25,8},{0,16},{8,24},{16,1},{24,9},{1,17},{9,25},{49,32},{5... | collective-permute-start | bytes 442376 | tf_op jit(solution)/shard_map/ppermute | solution.py:1155
  243.9 21.5 %collective-permute-start.38 = (bf16[9,16,512]{2,1,0:T(8,128)(2,1)}, bf16[9,16,512]{2,1,0:T(8,128)(2,1)S(1)}, u32[]{:S(2)}, u32[]{:S(2)}) collective-permute-start(bf16[9,16,512]{2,1,0:T(8,128)(2,1)} %get-tuple-element.155), channel_id=1, source_target_pairs={{1,0},{9,8},{17,16},{25,24},{0,1},{8,9},{16,17},{24,25},{33,32},{4... | collective-permute-start | bytes 442376 | tf_op jit(solution)/shard_map/ppermute | solution.py:1155
  247.3 18.2 %collective-permute-start.39 = (bf16[9,16,512]{2,1,0:T(8,128)(2,1)}, bf16[9,16,512]{2,1,0:T(8,128)(2,1)S(1)}, u32[]{:S(2)}, u32[]{:S(2)}) collective-permute-start(bf16[9,16,512]{2,1,0:T(8,128)(2,1)} %get-tuple-element.156), channel_id=1, source_target_pairs={{16,0},{24,8},{1,16},{9,24},{17,1},{25,9},{0,17},{8,25},{48,32},{5... | collective-permute-start | bytes 442376 | tf_op jit(solution)/shard_map/ppermute | solution.py:1155
  265.3 14.8 %collective-permute-start.35 = (bf16[4,4,8,16,512]{4,3,2,1,0:T(8,128)(2,1)}, bf16[4,4,8,16,512]{4,3,2,1,0:T(8,128)(2,1)S(1)}, u32[]{:S(2)}, u32[]{:S(2)}) collective-permute-start(bf16[4,4,8,16,512]{4,3,2,1,0:T(8,128)(2,1)} %get-tuple-element.152), channel_id=1, source_target_pairs={{0,8},{8,0},{16,24},{24,16},{32,40},{40,32},{48,56},{56,48},{64,72... | collective-permute-start | bytes 6291464 | tf_op jit(solution)/shard_map/ppermute | solution.py:920
  265.6 26.0 %collective-permute-start.42 = (bf16[9,16,512]{2,1,0:T(8,128)(2,1)S(1)}, bf16[9,16,512]{2,1,0:T(8,128)(2,1)S(1)}, u32[]{:S(2)}, u32[]{:S(2)}) collective-permute-start(bf16[9,16,512]{2,1,0:T(8,128)(2,1)S(1)} %add_convert_fusion.refs_0_.refs_1_), channel_id=1, source_target_pairs={{0,6},{2,4},{4,2},{6,0},{1,7},{3,5},{5,3},{7,1},{8,14},{10,12},{12... | collective-permute-start | bytes 442376 | tf_op jit(solution)/shard_map/ppermute | solution.py:942
  267.6 24.0 %collective-permute-start.41 = (bf16[9,16,512]{2,1,0:T(8,128)(2,1)S(1)}, bf16[9,16,512]{2,1,0:T(8,128)(2,1)}, u32[]{:S(2)}, u32[]{:S(2)}) collective-permute-start(bf16[9,16,512]{2,1,0:T(8,128)(2,1)S(1)} %add_convert_fusion.refs_0_.refs_1_), channel_id=1, source_target_pairs={{0,4},{2,6},{4,0},{6,2},{1,5},{3,7},{5,1},{7,3},{8,12},{10,14},{12... | collective-permute-start | bytes 442376 | tf_op jit(solution)/shard_map/ppermute | solution.py:942
  268.1 23.5 %collective-permute-start.40 = (bf16[9,16,512]{2,1,0:T(8,128)(2,1)S(1)}, bf16[9,16,512]{2,1,0:T(8,128)(2,1)}, u32[]{:S(2)}, u32[]{:S(2)}) collective-permute-start(bf16[9,16,512]{2,1,0:T(8,128)(2,1)S(1)} %add_convert_fusion.refs_0_.refs_1_), channel_id=1, source_target_pairs={{0,2},{2,0},{4,6},{6,4},{1,3},{3,1},{5,7},{7,5},{8,10},{10,8},{12,... | collective-permute-start | bytes 442376 | tf_op jit(solution)/shard_map/ppermute | solution.py:942
  286.6 39.5 %all-to-all-start.4 = ((bf16[4,4,11,16,512]{4,3,2,1,0:T(8,128)(2,1)}), bf16[4,4,11,16,512]{4,3,2,1,0:T(8,128)(2,1)S(1)}, u32[]{:S(2)}, u32[]{:S(2)}) async-start(bf16[4,4,11,16,512]{4,3,2,1,0:T(8,128)(2,1)} %shard_map.460.refs_0_), calls=%async_computation.4 | async-start | bytes 5767168 | tf_op jit(solution)/shard_map/all_to_all | solution.py:916
  331.9 28.2 %all-to-all-start.5 = ((bf16[16,5,16,512]{3,2,1,0:T(8,128)(2,1)}), bf16[16,5,16,512]{3,2,1,0:T(8,128)(2,1)S(1)}, u32[]{:S(2)}, u32[]{:S(2)}) async-start(bf16[16,5,16,512]{3,2,1,0:T(8,128)(2,1)} %get-tuple-element.179), calls=%async_computation.5 | async-start | bytes 2621440 | tf_op jit(solution)/shard_map/all_to_all | solution.py:1190
  335.7 22.1 %collective-permute-start.45 = (bf16[11,16,512]{2,1,0:T(8,128)(2,1)S(1)}, bf16[11,16,512]{2,1,0:T(8,128)(2,1)S(1)}, u32[]{:S(2)}, u32[]{:S(2)}) collective-permute-start(bf16[11,16,512]{2,1,0:T(8,128)(2,1)S(1)} %copy-done.35), channel_id=1, source_target_pairs={{17,0},{25,8},{0,16},{8,24},{16,1},{24,9},{1,17},{9,25},{49,32},{5... | collective-permute-start | bytes 540680 | tf_op jit(solution)/shard_map/ppermute | solution.py:1191
  337.6 22.5 %collective-permute-start.46 = (bf16[11,16,512]{2,1,0:T(8,128)(2,1)S(1)}, bf16[11,16,512]{2,1,0:T(8,128)(2,1)S(1)}, u32[]{:S(2)}, u32[]{:S(2)}) collective-permute-start(bf16[11,16,512]{2,1,0:T(8,128)(2,1)S(1)} %copy-done.33), channel_id=1, source_target_pairs={{1,0},{9,8},{17,16},{25,24},{0,1},{8,9},{16,17},{24,25},{33,32},{4... | collective-permute-start | bytes 540680 | tf_op jit(solution)/shard_map/ppermute | solution.py:1191
  340.3 19.8 %collective-permute-start.47 = (bf16[11,16,512]{2,1,0:T(8,128)(2,1)S(1)}, bf16[11,16,512]{2,1,0:T(8,128)(2,1)S(1)}, u32[]{:S(2)}, u32[]{:S(2)}) collective-permute-start(bf16[11,16,512]{2,1,0:T(8,128)(2,1)S(1)} %copy-done.32), channel_id=1, source_target_pairs={{16,0},{24,8},{1,16},{9,24},{17,1},{25,9},{0,17},{8,25},{48,32},{5... | collective-permute-start | bytes 540680 | tf_op jit(solution)/shard_map/ppermute | solution.py:1191
  363.9 16.2 %collective-permute-start.50 = (bf16[15,16,512]{2,1,0:T(8,128)(2,1)}, bf16[15,16,512]{2,1,0:T(8,128)(2,1)S(1)}, u32[]{:S(2)}, u32[]{:S(2)}) collective-permute-start(bf16[15,16,512]{2,1,0:T(8,128)(2,1)} %get-tuple-element.184.refs_4_), channel_id=1, source_target_pairs={{0,6},{2,4},{4,2},{6,0},{1,7},{3,5},{5,3},{7,1},{8,14},{10,12},{12... | collective-permute-start | bytes 737288 | tf_op jit(solution)/shard_map/ppermute | solution.py:942
  365.9 14.2 %collective-permute-start.49 = (bf16[15,16,512]{2,1,0:T(8,128)(2,1)}, bf16[15,16,512]{2,1,0:T(8,128)(2,1)S(1)}, u32[]{:S(2)}, u32[]{:S(2)}) collective-permute-start(bf16[15,16,512]{2,1,0:T(8,128)(2,1)} %get-tuple-element.184.refs_4_), channel_id=1, source_target_pairs={{0,4},{2,6},{4,0},{6,2},{1,5},{3,7},{5,1},{7,3},{8,12},{10,14},{12... | collective-permute-start | bytes 737288 | tf_op jit(solution)/shard_map/ppermute | solution.py:942
  366.9 13.3 %collective-permute-start.48 = (bf16[15,16,512]{2,1,0:T(8,128)(2,1)}, bf16[15,16,512]{2,1,0:T(8,128)(2,1)S(1)}, u32[]{:S(2)}, u32[]{:S(2)}) collective-permute-start(bf16[15,16,512]{2,1,0:T(8,128)(2,1)} %get-tuple-element.184.refs_4_), channel_id=1, source_target_pairs={{0,2},{2,0},{4,6},{6,4},{1,3},{3,1},{5,7},{7,5},{8,10},{10,8},{12,... | collective-permute-start | bytes 737288 | tf_op jit(solution)/shard_map/ppermute | solution.py:942
  372.4 20.3 %all-to-all-start.6 = ((f32[64,16,128]{2,1,0:T(8,128)}), f32[64,16,128]{2,1,0:T(8,128)S(1)}, u32[]{:S(2)}, u32[]{:S(2)}) async-start(f32[64,16,128]{2,1,0:T(8,128)} %get-tuple-element.197), calls=%async_computation.6 | async-start | bytes 1048576 | tf_op jit(solution)/shard_map/all_to_all | solution.py:1194
  (74 other events, 436.9 us)

commit v3 on v2

--- a/solution.py
+++ b/solution.py
@@ -409,7 +409,7 @@
             store_diagonal(into_ref, pl.multiple_of(p * 128, 128), lane, dot_tn(attn, values))
         return carry
 
-    lax.fori_loop(0, PAIRS // 2, one_pair, 0)
+    lax.fori_loop(0, PAIRS // 2, one_pair, 0, unroll=4)
 
 
 def attend_kernel(shifted, moves, *refs):
@@ -850,32 +850,37 @@
         step_into((layer,), sums_ref[24:40, 256 * layer : 256 * layer + REL], table, new_table, 0.6, 0.0)
 
 
+def reordered_steps(pieces, at, n, order_ref, old, new):
+    wide = order_ref.shape[0]
+    grads = [four(pieces, at + b) for b in range(n)]
+    for g in range(GROUPS):
+        part = jnp.concatenate([v[:, 128 * g : 128 * g + 128] for v in grads], 1)
+        lanes = (0, slice(None), slice(wide * g, wide * g + wide))
+        step_into(lanes, reorder(part, order_ref[...]), old, new, 0.03, 0.05)
+
+
+def rest_steps(pieces, at, units_ref, old, new):
+    step_into((0,), four(pieces, at), old[0:3], new[0:3], 0.1, 0.05)
+    for b in range(4):
+        step_into((0, slice(16 * b, 16 * b + 16)), four(pieces, at + 5 + b), old[6:9], new[6:9], 0.03, 0.05)
+    reordered_steps(pieces, at + 1, 4, units_ref, old[3:6], new[3:6])
+
+
+def update_early_kernel(*refs):
+    rest_steps(refs[:4], 0, refs[4], refs[5:14], refs[14:])
+
+
 def update_kernel(*refs):
-    early, late, heads_ref, units_ref, refs = refs[:4], refs[4:8], refs[8], refs[9], refs[10:]
-    old = [refs[3 * i : 3 * i + 3] for i in range(4)]
-    new = [refs[12 + 3 * i : 15 + 3 * i] for i in range(4)]
-
-    def layer_step(heads, head_at, rest, rest_at):
-        step_into((0,), four(rest, rest_at), old[1], new[1], 0.1, 0.05)
-        for b in range(4):
-            step_into((0, slice(16 * b, 16 * b + 16)), four(rest, rest_at + 5 + b), old[3], new[3], 0.03, 0.05)
-        for n, wide, order_ref, i, pieces, at in (
-            (3, 384, heads_ref, 0, heads, head_at),
-            (4, 512, units_ref, 2, rest, rest_at + 1),
-        ):
-            grads = [four(pieces, at + b) for b in range(n)]
-            for g in range(GROUPS):
-                part = jnp.concatenate([v[:, 128 * g : 128 * g + 128] for v in grads], 1)
-                lanes = (0, slice(None), slice(wide * g, wide * g + wide))
-                step_into(lanes, reorder(part, order_ref[...]), old[i], new[i], 0.03, 0.05)
+    late, heads_ref, units_ref, old, new = refs[9:13], refs[13], refs[14], refs[15:27], refs[27:]
 
     @pl.when(pl.program_id(0) == 0)
     def _():
-        layer_step(late, 0, late, 3)
+        reordered_steps(late, 0, 3, heads_ref, old[:3], new[:3])
+        rest_steps(late, 3, units_ref, old[3:], new[3:])
 
     @pl.when(pl.program_id(0) == 1)
     def _():
-        layer_step(late, 12, early, 0)
+        reordered_steps(late, 12, 3, heads_ref, old[:3], new[:3])
 
 
 def to_neighbours(slabs, ahead):
@@ -943,17 +948,30 @@
 
 
 def update(early, late, heads, units, state):
-    whole = [pl.BlockSpec(memory_space=pltpu.VMEM)] * 10
-    parts = [pl.BlockSpec((1, *a.shape[1:]), lambda layer: (layer, 0, 0)) for a in state]
+    inside, anywhere = pl.BlockSpec(memory_space=pltpu.VMEM), pl.BlockSpec(memory_space=pl.ANY)
+    rest = state[3:]
+    second = [pl.BlockSpec((1, *a.shape[1:]), lambda _: (1, 0, 0)) for a in rest]
+    first = [pl.BlockSpec((1, *a.shape[1:]), lambda _: (0, 0, 0)) for a in rest]
+    both = [pl.BlockSpec((1, *a.shape[1:]), lambda layer: (layer, 0, 0)) for a in state[:3]]
+    done = pl.pallas_call(
+        update_early_kernel,
+        grid=(1,),
+        out_shape=[jax.ShapeDtypeStruct(a.shape, F32) for a in rest],
+        in_specs=[inside] * 5 + second,
+        out_specs=second,
+        compiler_params=pltpu.CompilerParams(vmem_limit_bytes=VMEM_BYTES),
+        cost_estimate=pl.CostEstimate(flops=4 * 10**9, bytes_accessed=4 * 10**6, transcendentals=0),
+    )(*early, units, *rest)
     return pl.pallas_call(
         update_kernel,
         grid=(LAYERS,),
         out_shape=[jax.ShapeDtypeStruct(a.shape, F32) for a in state],
-        in_specs=whole + parts,
-        out_specs=parts,
+        in_specs=[anywhere] * 9 + [inside] * 6 + both + first,
+        out_specs=both + first,
+        input_output_aliases={i: 3 + i for i in range(9)},
         compiler_params=pltpu.CompilerParams(vmem_limit_bytes=VMEM_BYTES),
         cost_estimate=pl.CostEstimate(flops=8 * 10**9, bytes_accessed=8 * 10**6, transcendentals=0),
-    )(*early, *late, heads, units, *state)
+    )(*done, *late, heads, units, *state)
 
 
 def adamw(weight, first, second, grad, rate, decay):

time: 404 us -> 405 us (level)
  no operation moved by 1% of the time
where the time goes in v3:
time: 405 us; the launch traced here: 397 us
  Pallas kernels  202 us (50%)
  starting transfers between devices  98.1 us (24%)
  waiting for transfers between devices  62.4 us (15%)
  local copies, waits for them, and re-layouts  27.8 us (7%)
  other arithmetic  4.36 us (1%)
    pallas_call x18, Pallas kernels, call(): pl.pallas_call(whole, out_shape=shapes, in_specs=specs, out_specs=[anywhe...  184 us
    ppermute x6, waiting for transfers between devices, local(): lax.ppermute(v, ('img', 'col'), from_x(4 - d))  17.3 us
    unnamed x129, local copies, waits for them, and re-layouts  16.6 us
    ppermute x6, waiting for transfers between devices, along_z(): return [value] + [lax.ppermute(value, 'img', from_z(d)) for d in (1, 2, 3)]  15.2 us
    all_to_all x3, waiting for transfers between devices, scattered_z(): lax.all_to_all(value, 'img', 0, 0, tiled=True, axis_index_groups=ALONG_Z)  14.8 us
    all_to_all x3, starting transfers between devices, scattered_z(): lax.all_to_all(value, 'img', 0, 0, tiled=True, axis_index_groups=ALONG_Z)  12.4 us
    ppermute x6, starting transfers between devices, along_x(): lax.ppermute(value, ('img', 'col'), from_x(d))  12.2 us
    ppermute x6, starting transfers between devices, local(): lax.ppermute(v, ('img', 'col'), from_x(4 - d))  11.9 us
  transfers between devices with their start and end apart: 58, of which 13 were waited for; matrix products, arithmetic and copies ran while one was open for 4% of the time, Pallas kernels for 41%

profile of v3, /device:TPU:0, one launch (start us, length us, event | category | flops | bytes accessed | tf_op | source)
XLA Modules:
  0.0 397.4 jit_solution(3629282790194323384)
XLA Ops:
  0.7 2.8 shard_map.445
  5.5 3.6 collective-permute-start.8
  9.1 4.3 %all-to-all-start = ((bf16[4,6,16,512]{3,2,1,0:T(8,128)(2,1)}), bf16[4,6,16,512]{3,2,1,0:T(8,128)(2,1)S(1)}, u32[]{:S(2)}, u32[]{:S(2)}) async-start(bf16[4,6,16,512]{3,2,1,0:T(8,128)(2,1)} %get-tuple-element.122), calls=%async_computation | async-start | bytes 786432 | tf_op jit(solution)/shard_map/all_to_all | solution.py:1049
  16.2 4.3 %shard_map.446.refs_9_.refs_0_.refs_10_ = bf16[1024,512]{1,0:T(8,128)(2,1)} custom-call(bf16[784,512]{1,0:T(8,128)(2,1)} %reshape.137.refs_0_.refs_19_.refs_15_, f32[1,512]{1,0:T(1,128)} %get-tuple-element.303.refs_1_.refs_17_, f32[1,512]{1,0:T(1,128)} %get-tuple-element.302.refs_2_, bf16[1024,784]{1,0:T(8,128)(2,1)} %constant.82.clone.refs_3_.refs_7_), custom_call_target="tpu_custom_call" | custom-call | flops 12000000000 | bytes 4000000 | tf_op jit(solution)/shard_map/pallas_call | solution.py:264
  21.2 2.5 collective-permute-start.1
  27.2 13.6 %collective-permute-done.2.refs_4_.refs_6_ = bf16[4,6,16,512]{3,2,1,0:T(8,128)(2,1)S(1)} collective-permute-done((bf16[4,6,16,512]{3,2,1,0:T(8,128)(2,1)S(1)}, bf16[4,6,16,512]{3,2,1,0:T(8,128)(2,1)S(1)}, u32[]{:S(2)}, u32[]{:S(2)}) %collective-permute-start.2) | collective-permute-done | bytes 393248 | tf_op jit(solution)/shard_map/ppermute | solution.py:1044
  47.8 2.7 collective-permute-start.11
  53.0 17.3 %shard_map.447 = (bf16[3,32,16,512]{3,2,1,0:T(8,128)(2,1)}, bf16[1024,1536]{1,0:T(8,128)(2,1)}, bf16[4,4,256,128]{3,2,1,0:T(8,128)(2,1)}, bf16[4,4,256,128]{3,2,1,0:T(8,128)(2,1)}, bf16[784,512]{1,0:T(8,128)(2,1)}) custom-call(s32[3]{0:T(128)} %pad_add_fusion.1.refs_0_.refs_2_.refs_1_.refs_5_, bf16[4,6,16,512]{3,2,1,0:T(8,128)(2,1)} %copy-done.15, ...), custom_call_target="tpu_custom_call" | custom-call | flops 54000001024 | bytes 18000000 | tf_op jit(solution)/shard_map/pallas_call | solution.py:264
  70.4 2.9 shard_map.448
  73.3 3.8 all-to-all-start.2
  85.4 2.7 collective-permute-start.18
  91.5 16.4 %shard_map.450 = (bf16[9,32,16,512]{3,2,1,0:T(8,128)(2,1)}, f32[784,512]{1,0:T(8,128)}, bf16[784,512]{1,0:T(8,128)(2,1)}, bf16[784,2048]{1,0:T(8,128)(2,1)}, bf1...) custom-call(bf16[16,3,16,512]{3,2,1,0:T(8,128)(2,1)} %get-tuple-elem, ...), custom_call_target="tpu_custom_call" | custom-call | flops 44999999488 | bytes 15000000 | tf_op jit(solution)/shard_map/pallas_call | solution.py:264
  108.0 3.2 collective-permute-start.23
  111.9 2.9 collective-permute-start.22
  115.5 2.7 shard_map.451
  118.2 3.8 all-to-all-start.1
  122.7 19.5 %shard_map.452 = (bf16[3,32,16,512]{3,2,1,0:T(8,128)(2,1)}, bf16[1024,512]{1,0:T(8,128)(2,1)}, bf16[1024,1536]{1,0:T(8,128)(2,1)}, bf16[4,4,256,128]{3,2,1,0:T(8...) custom-call(s32[25,256]{1,0:T(8,128)} %reshape.141.refs_0_.refs_11_., ...), custom_call_target="tpu_custom_call" | custom-call | flops 54000001024 | bytes 18000000 | tf_op jit(solution)/shard_map/pallas_call | solution.py:264
  142.2 8.9 %all-to-all-done.1 = bf16[4,4,9,16,512]{4,3,2,1,0:T(8,128)(2,1)S(1)} async-done(((bf16[4,4,9,16,512]{4,3,2,1,0:T(8,128)(2,1)}), bf16[4,4,9,16,512]{4,3,2,1,0:T(8,128)(2,1)S(1)}, u32[]{:S(2)}, u32[]{:S(2)}) %all-to-all-start.1) | async-done | bytes 2359328 | tf_op jit(solution)/shard_map/all_to_all | solution.py:921
  155.3 2.7 collective-permute-start.27
  159.9 3.1 collective-permute-done.27.refs_7_
  163.8 25.6 %shard_map.454 = (bf16[784,512]{1,0:T(8,128)(2,1)}, f32[784,512]{1,0:T(8,128)}, f32[4,512]{1,0:T(4,128)}, f32[1,2048]{1,0:T(1,128)}, bf16[784,512]{1,0:T(8,128)(...) custom-call(s32[3]{0:T(128)} %pad_add_fusion.1.refs_0_.refs_2_.refs_, ...), custom_call_target="tpu_custom_call" | custom-call | flops 102000001024 | bytes 34000000 | tf_op jit(solution)/shard_map/pallas_call | solution.py:264
  190.3 2.9 collective-permute-start.30
  195.7 4.6 %shard_map.455.refs_0_ = bf16[4,4,9,16,512]{4,3,2,1,0:T(8,128)(2,1)} custom-call(bf16[4,4,9,16,512]{4,3,2,1,0:T(8,128)(2,1)} %get-tuple-element.138.refs_0_, bf16[4,4,9,16,512]{4,3,2,1,0:T(8,128)(2,1)} %copy-done.4), custom_call_target="tpu_custom_call" | custom-call | flops 2359296 | bytes 7077888 | tf_op jit(solution)/shard_map/pallas_call | solution.py:935
  200.3 3.6 all-to-all-start.3
  204.6 22.0 %shard_map.457 = (bf16[1024,1536]{1,0:T(8,128)(2,1)}, f32[3,512]{1,0:T(4,128)}, f32[16,256]{1,0:T(8,128)}, bf16[1024,512]{1,0:T(8,128)(2,1)}, bf16[96,512]{1,0:T...) custom-call(bf16[4,4,9,16,512]{4,3,2,1,0:T(8,128)(2,1)} %shard_map.455.refs_0_, ...), custom_call_target="tpu_custom_call" | custom-call | flops 60000002048 | bytes 20000000 | tf_op jit(solution)/shard_map/pallas_call | solution.py:264
  226.6 3.5 collective-permute-start.34
  232.0 6.1 %shard_map.458 = (bf16[4,4,3,16,512]{4,3,2,1,0:T(8,128)(2,1)}, bf16[4,4,3,16,512]{4,3,2,1,0:T(8,128)(2,1)}) custom-call(s32[3]{0:T(128)} %pad_add_fusion.1.refs_0_.refs_2_.refs_1_.refs_5_, bf16[1024,512]{1,0:T(8,128)(2,1)} %get-tuple-element.131.refs_1_, bf16[1024,1536]{1,0:T(8,128)(2,1)} %get-tuple-element.149.refs_2_), custom_call_target="tpu_custom_call" | custom-call | flops 12000000000 | bytes 4000000 | tf_op jit(solution)/shard_map/pallas_call | solution.py:264
  239.6 2.7 shard_map.456
  242.9 3.3 collective-permute-start.38
  248.9 15.7 %shard_map.459 = (f32[784,512]{1,0:T(8,128)}, bf16[784,2048]{1,0:T(8,128)(2,1)}, bf16[4,4,8,16,512]{4,3,2,1,0:T(8,128)(2,1)}, bf16[4,4,8,16,512]{4,3,2,1,0:T(8,1...) custom-call(bf16[9,16,512]{2,1,0:T(8,128)(2,1)} %get-tuple-element.140.refs_0_, ...), custom_call_target="tpu_custom_call" | custom-call | flops 48000000000 | bytes 16000000 | tf_op jit(solution)/shard_map/pallas_call | solution.py:264
  269.0 10.4 %shard_map.461 = (f32[784,512]{1,0:T(8,128)}, bf16[512,512]{1,0:T(8,128)(2,1)}, f32[3,512]{1,0:T(4,128)}, bf16[1024,512]{1,0:T(8,128)(2,1)}) custom-call(bf16[9,16,512]{2,1,0:T(8,128)(2,1)} %copy-done.16, f32[784,512]{1,0:T(8,128)} %get-tuple-element.166.refs_1_, bf16[784,2048]{1,0:T(8,128)(2,1)} %get-tuple-element.167.refs_2_, ...), custom_call_target="tpu_custom_call" | custom-call | flops 24000000000 | bytes 8000000 | tf_op jit(solution)/shard_map/pallas_call | solution.py:264
  281.0 4.8 %shard_map.460.refs_0_ = bf16[4,4,11,16,512]{4,3,2,1,0:T(8,128)(2,1)} custom-call(bf16[4,4,8,16,512]{4,3,2,1,0:T(8,128)(2,1)} %get-tuple-element.160.refs_0_, bf16[4,4,8,16,512]{4,3,2,1,0:T(8,128)(2,1)} %copy-done.6, bf16[4,4,3,16,512]{4,3,2,1,0:T(8,128)(2,1)} %get-tuple-element.150.refs_1_.refs_2_, bf16[4,4,3,16,512]{4,3,2,1,0:T(8,128)(2,1)} %copy-done.12), custom_call_target="tpu_custom_call" | custom-call | flops 2883584 | bytes 8650752 | tf_op jit(solution)/shard_map/pallas_call | solution.py:935
  285.9 4.9 %all-to-all-start.4 = ((bf16[4,4,11,16,512]{4,3,2,1,0:T(8,128)(2,1)}), bf16[4,4,11,16,512]{4,3,2,1,0:T(8,128)(2,1)S(1)}, u32[]{:S(2)}, u32[]{:S(2)}) async-start(bf16[4,4,11,16,512]{4,3,2,1,0:T(8,128)(2,1)} %shard_map.460.refs_0_), calls=%async_computation.4 | async-start | bytes 5767168 | tf_op jit(solution)/shard_map/all_to_all | solution.py:921
  291.5 24.8 %shard_map.462 = (bf16[4,4,4,16,512]{4,3,2,1,0:T(8,128)(2,1)}, bf16[4,4,4,16,512]{4,3,2,1,0:T(8,128)(2,1)}, f32[784,512]{1,0:T(8,128)}, f32[40,512]{1,0:T(8,128)}) custom-call(bf16[4,4,11,16,512]{4,3,2,1,0:T(8,128)(2,1)} %shard_map.460.refs_0_, bf16[9,16,512]{2,1,0:T(8,128)(2,1)} %copy-done.16, bf16[9,16,512]{2,1,0:T(8,128)(2,1)} %collective-permute-done.40.refs_2_.refs_1_, ...), custom_call_target="tpu_custom_call" | custom-call | flops 77999996928 | bytes 26000000 | tf_op jit(solution)/shard_map/pallas_call | solution.py:264
  316.8 2.1 collective-permute-done.44.refs_5_
  319.5 5.9 %all-to-all-done.4.refs_3_ = bf16[4,4,11,16,512]{4,3,2,1,0:T(8,128)(2,1)S(1)} async-done(((bf16[4,4,11,16,512]{4,3,2,1,0:T(8,128)(2,1)}), bf16[4,4,11,16,512]{4,3,2,1,0:T(8,128)(2,1)S(1)}, u32[]{:S(2)}, u32[]{:S(2)}) %all-to-all-start.4) | async-done | bytes 2883616 | tf_op jit(solution)/shard_map/all_to_all | solution.py:921
  326.9 4.1 %shard_map.464 = (bf16[16,5,16,512]{3,2,1,0:T(8,128)(2,1)}, bf16[11,16,512]{2,1,0:T(8,128)(2,1)}, bf16[11,16,512]{2,1,0:T(8,128)(2,1)}, bf16[11,16,512]{2,1,0:T(8,128)(2,1)}, bf16[11,16,512]{2,1,0:T(8,128)(2,1)}) custom-call(s32[3]{0:T(128)} %pad_add_fusion.1.refs_0_.refs_2_.refs_1_.refs_5_, bf16[4,4,4,16,512]{4,3,2,1,0:T(8,128)(2,1)} %get-tuple-element.194.refs_1_, ...), custom_call_target="tpu_custom_call" | custom-call | flops 15000000512 | bytes 5000000 | tf_op jit(solution)/shard_map/pallas_call | solution.py:264
  331.1 3.8 all-to-all-start.5
  336.8 2.7 collective-permute-start.46
  342.0 15.0 %collective-permute-done.45.refs_2_ = bf16[11,16,512]{2,1,0:T(8,128)(2,1)S(1)} collective-permute-done((bf16[11,16,512]{2,1,0:T(8,128)(2,1)S(1)}, bf16[11,16,512]{2,1,0:T(8,128)(2,1)S(1)}, u32[]{:S(2)}, u32[]{:S(2)}) %collective-permute-start.45) | collective-permute-done | bytes 180256 | tf_op jit(solution)/shard_map/ppermute | solution.py:1209
  357.0 2.3 collective-permute-done.46.refs_3_
  360.5 2.6 shard_map.465
  367.4 3.2 shard_map.463
  370.6 3.1 reshape.149
  373.7 7.7 %all-to-all-start.6 = ((f32[64,16,128]{2,1,0:T(8,128)}), f32[64,16,128]{2,1,0:T(8,128)S(1)}, u32[]{:S(2)}, u32[]{:S(2)}) async-start(f32[64,16,128]{2,1,0:T(8,128)} %get-tuple-element.215), calls=%async_computation.6 | async-start | bytes 1048576 | tf_op jit(solution)/shard_map/all_to_all | solution.py:1212
  382.3 4.8 %shard_map.466 = (f32[2,16,1536]{2,1,0:T(8,128)}, f32[2,16,1536]{2,1,0:T(8,128)}, f32[2,16,1536]{2,1,0:T(8,128)}, f32[2,16,512]{2,1,0:T(8,128)}, f32[2,16,512]{2...) custom-call(f32[2,16,512]{2,1,0:T(8,128)} %get-tuple-element.185.ref, ...), custom_call_target="tpu_custom_call", output_to_operand_aliasing={{3}: (0, {}), {4}: (1, {}), {5}: (2, {}), {6}: (3, {}), {7}... | custom-call | flops 8000000000 | bytes 8000000 | tf_op jit(solution)/shard_map/pallas_call | solution.py:965
  387.1 6.9 %all-to-all-done.6.refs_0_ = f32[64,16,128]{2,1,0:T(8,128)S(1)} async-done(((f32[64,16,128]{2,1,0:T(8,128)}), f32[64,16,128]{2,1,0:T(8,128)S(1)}, u32[]{:S(2)}, u32[]{:S(2)}) %all-to-all-start.6) | async-done | bytes 524320 | tf_op jit(solution)/shard_map/all_to_all | solution.py:1212
  394.8 2.4 shard_map.467
  (261 shorter events, 70.3 us)
Async XLA Ops:
  3.5 22.6 %collective-permute-start.9 = (bf16[6,16,512]{2,1,0:T(8,128)(2,1)}, bf16[6,16,512]{2,1,0:T(8,128)(2,1)S(1)}, u32[]{:S(2)}, u32[]{:S(2)}) collective-permute-start(bf16[6,16,512]{2,1,0:T(8,128)(2,1)} %get-tuple-element.126.refs_1_), channel_id=1, source_target_pairs={{96,0},{104,8},{112,16},{120,24},{0,32},{8,40},{16,48},{24,56},{32... | collective-permute-start | bytes 294920 | tf_op jit(solution)/shard_map/ppermute | solution.py:1044
  5.5 21.7 %collective-permute-start.8 = (bf16[6,16,512]{2,1,0:T(8,128)(2,1)}, bf16[6,16,512]{2,1,0:T(8,128)(2,1)S(1)}, u32[]{:S(2)}, u32[]{:S(2)}) collective-permute-start(bf16[6,16,512]{2,1,0:T(8,128)(2,1)} %get-tuple-element.126.refs_1_), channel_id=1, source_target_pairs={{64,0},{72,8},{80,16},{88,24},{96,32},{104,40},{112,48},{120,56},{... | collective-permute-start | bytes 294920 | tf_op jit(solution)/shard_map/ppermute | solution.py:1044
  9.1 12.1 %all-to-all-start = ((bf16[4,6,16,512]{3,2,1,0:T(8,128)(2,1)}), bf16[4,6,16,512]{3,2,1,0:T(8,128)(2,1)S(1)}, u32[]{:S(2)}, u32[]{:S(2)}) async-start(bf16[4,6,16,512]{3,2,1,0:T(8,128)(2,1)} %get-tuple-element.122), calls=%async_computation | async-start | bytes 786432 | tf_op jit(solution)/shard_map/all_to_all | solution.py:1049
  21.1 19.7 %collective-permute-start.2 = (bf16[4,6,16,512]{3,2,1,0:T(8,128)(2,1)S(1)}, bf16[4,6,16,512]{3,2,1,0:T(8,128)(2,1)S(1)}, u32[]{:S(2)}, u32[]{:S(2)}) collective-permute-start(bf16[4,6,16,512]{3,2,1,0:T(8,128)(2,1)S(1)} %all-to-all-done.refs_1_.refs_3_), channel_id=1, source_target_pairs={{96,0},{104,8},{112,16},{120,24},{0,32},{8,40},{16,48},{24,56},{32... | collective-permute-start | bytes 1179656 | tf_op jit(solution)/shard_map/ppermute | solution.py:1044
  21.2 19.7 %collective-permute-start.1 = (bf16[4,6,16,512]{3,2,1,0:T(8,128)(2,1)S(1)}, bf16[4,6,16,512]{3,2,1,0:T(8,128)(2,1)S(1)}, u32[]{:S(2)}, u32[]{:S(2)}) collective-permute-start(bf16[4,6,16,512]{3,2,1,0:T(8,128)(2,1)S(1)} %all-to-all-done.refs_1_.refs_3_), channel_id=1, source_target_pairs={{64,0},{72,8},{80,16},{88,24},{96,32},{104,40},{112,48},{120,56},{... | collective-permute-start | bytes 1179656 | tf_op jit(solution)/shard_map/ppermute | solution.py:1044
  23.6 18.9 %collective-permute-start = (bf16[4,6,16,512]{3,2,1,0:T(8,128)(2,1)S(1)}, bf16[4,6,16,512]{3,2,1,0:T(8,128)(2,1)S(1)}, u32[]{:S(2)}, u32[]{:S(2)}) collective-permute-start(bf16[4,6,16,512]{3,2,1,0:T(8,128)(2,1)S(1)} %all-to-all-done.refs_1_.refs_3_), channel_id=1, source_target_pairs={{32,0},{40,8},{48,16},{56,24},{64,32},{72,40},{80,48},{88,56},{96,... | collective-permute-start | bytes 1179656 | tf_op jit(solution)/shard_map/ppermute | solution.py:1044
  26.2 17.4 %collective-permute-start.7 = (bf16[6,16,512]{2,1,0:T(8,128)(2,1)S(1)}, bf16[6,16,512]{2,1,0:T(8,128)(2,1)S(1)}, u32[]{:S(2)}, u32[]{:S(2)}) collective-permute-start(bf16[6,16,512]{2,1,0:T(8,128)(2,1)S(1)} %copy-done.43), channel_id=1, source_target_pairs={{32,0},{40,8},{48,16},{56,24},{64,32},{72,40},{80,48},{88,56},{96,... | collective-permute-start | bytes 294920 | tf_op jit(solution)/shard_map/ppermute | solution.py:1044
  27.2 20.6 %collective-permute-start.3 = (bf16[4,6,16,512]{3,2,1,0:T(8,128)(2,1)S(1)}, bf16[4,6,16,512]{3,2,1,0:T(8,128)(2,1)S(1)}, u32[]{:S(2)}, u32[]{:S(2)}) collective-permute-start(bf16[4,6,16,512]{3,2,1,0:T(8,128)(2,1)S(1)} %all-to-all-done.refs_1_.refs_3_), channel_id=1, source_target_pairs={{0,8},{8,0},{16,24},{24,16},{32,40},{40,32},{48,56},{56,48},{64,72... | collective-permute-start | bytes 1179656 | tf_op jit(solution)/shard_map/ppermute | solution.py:925
  40.8 11.3 %collective-permute-start.5 = (bf16[4,6,16,512]{3,2,1,0:T(8,128)(2,1)S(1)}, bf16[4,6,16,512]{3,2,1,0:T(8,128)(2,1)S(1)}, u32[]{:S(2)}, u32[]{:S(2)}) collective-permute-start(bf16[4,6,16,512]{3,2,1,0:T(8,128)(2,1)S(1)} %collective-permute-done.1.refs_3_.refs_5_), channel_id=1, source_target_pairs={{0,8},{8,0},{16,24},{24,16},{32,40},{40,32},{48,56},{56,48},{64,72... | collective-permute-start | bytes 1179656 | tf_op jit(solution)/shard_map/ppermute | solution.py:925
  46.0 31.7 %collective-permute-start.12 = (bf16[4,6,16,512]{3,2,1,0:T(8,128)(2,1)}, bf16[4,6,16,512]{3,2,1,0:T(8,128)(2,1)}, u32[]{:S(2)}, u32[]{:S(2)}) collective-permute-start(bf16[4,6,16,512]{3,2,1,0:T(8,128)(2,1)} %shard_map.449.refs_11_), channel_id=1, source_target_pairs={{17,0},{25,8},{0,16},{8,24},{16,1},{24,9},{1,17},{9,25},{49,32},{5... | collective-permute-start | bytes 1179656 | tf_op jit(solution)/shard_map/ppermute | solution.py:1047
  47.8 30.3 %collective-permute-start.11 = (bf16[4,6,16,512]{3,2,1,0:T(8,128)(2,1)}, bf16[4,6,16,512]{3,2,1,0:T(8,128)(2,1)S(1)}, u32[]{:S(2)}, u32[]{:S(2)}) collective-permute-start(bf16[4,6,16,512]{3,2,1,0:T(8,128)(2,1)} %shard_map.449.refs_11_), channel_id=1, source_target_pairs={{1,0},{9,8},{17,16},{25,24},{0,1},{8,9},{16,17},{24,25},{33,32},{4... | collective-permute-start | bytes 1179656 | tf_op jit(solution)/shard_map/ppermute | solution.py:1047
  50.5 27.8 %collective-permute-start.10 = (bf16[4,6,16,512]{3,2,1,0:T(8,128)(2,1)}, bf16[4,6,16,512]{3,2,1,0:T(8,128)(2,1)}, u32[]{:S(2)}, u32[]{:S(2)}) collective-permute-start(bf16[4,6,16,512]{3,2,1,0:T(8,128)(2,1)} %shard_map.449.refs_11_), channel_id=1, source_target_pairs={{16,0},{24,8},{1,16},{9,24},{17,1},{25,9},{0,17},{8,25},{48,32},{5... | collective-permute-start | bytes 1179656 | tf_op jit(solution)/shard_map/ppermute | solution.py:1047
  73.3 17.8 %all-to-all-start.2 = ((bf16[16,3,16,512]{3,2,1,0:T(8,128)(2,1)}), bf16[16,3,16,512]{3,2,1,0:T(8,128)(2,1)S(1)}, u32[]{:S(2)}, u32[]{:S(2)}) async-start(bf16[16,3,16,512]{3,2,1,0:T(8,128)(2,1)} %get-tuple-element.124.refs_0_), calls=%async_computation.2 | async-start | bytes 1572864 | tf_op jit(solution)/shard_map/all_to_all | solution.py:1094
  77.7 10.4 %collective-permute-start.16 = (bf16[4,6,16,512]{3,2,1,0:T(8,128)(2,1)}, bf16[4,6,16,512]{3,2,1,0:T(8,128)(2,1)}, u32[]{:S(2)}, u32[]{:S(2)}) collective-permute-start(bf16[4,6,16,512]{3,2,1,0:T(8,128)(2,1)} %collective-permute-done.12.refs_14_), channel_id=1, source_target_pairs={{0,8},{8,0},{16,24},{24,16},{32,40},{40,32},{48,56},{56,48},{64,72... | collective-permute-start | bytes 1179656 | tf_op jit(solution)/shard_map/ppermute | solution.py:925
  78.2 11.4 %collective-permute-start.15 = (bf16[4,6,16,512]{3,2,1,0:T(8,128)(2,1)S(1)}, bf16[4,6,16,512]{3,2,1,0:T(8,128)(2,1)}, u32[]{:S(2)}, u32[]{:S(2)}) collective-permute-start(bf16[4,6,16,512]{3,2,1,0:T(8,128)(2,1)S(1)} %collective-permute-done.11.refs_13_), channel_id=1, source_target_pairs={{0,8},{8,0},{16,24},{24,16},{32,40},{40,32},{48,56},{56,48},{64,72... | collective-permute-start | bytes 1179656 | tf_op jit(solution)/shard_map/ppermute | solution.py:925
  78.3 13.2 %collective-permute-start.14 = (bf16[4,6,16,512]{3,2,1,0:T(8,128)(2,1)}, bf16[4,6,16,512]{3,2,1,0:T(8,128)(2,1)}, u32[]{:S(2)}, u32[]{:S(2)}) collective-permute-start(bf16[4,6,16,512]{3,2,1,0:T(8,128)(2,1)} %collective-permute-done.10.refs_12_), channel_id=1, source_target_pairs={{0,8},{8,0},{16,24},{24,16},{32,40},{40,32},{48,56},{56,48},{64,72... | collective-permute-start | bytes 1179656 | tf_op jit(solution)/shard_map/ppermute | solution.py:925
  83.5 27.7 %collective-permute-start.19 = (bf16[9,16,512]{2,1,0:T(8,128)(2,1)S(1)}, bf16[9,16,512]{2,1,0:T(8,128)(2,1)S(1)}, u32[]{:S(2)}, u32[]{:S(2)}) collective-permute-start(bf16[9,16,512]{2,1,0:T(8,128)(2,1)S(1)} %copy-done.39), channel_id=1, source_target_pairs={{17,0},{25,8},{0,16},{8,24},{16,1},{24,9},{1,17},{9,25},{49,32},{5... | collective-permute-start | bytes 442376 | tf_op jit(solution)/shard_map/ppermute | solution.py:1047
  85.4 26.5 %collective-permute-start.18 = (bf16[9,16,512]{2,1,0:T(8,128)(2,1)S(1)}, bf16[9,16,512]{2,1,0:T(8,128)(2,1)S(1)}, u32[]{:S(2)}, u32[]{:S(2)}) collective-permute-start(bf16[9,16,512]{2,1,0:T(8,128)(2,1)S(1)} %copy-done.39), channel_id=1, source_target_pairs={{1,0},{9,8},{17,16},{25,24},{0,1},{8,9},{16,17},{24,25},{33,32},{4... | collective-permute-start | bytes 442376 | tf_op jit(solution)/shard_map/ppermute | solution.py:1047
  88.1 26.7 %collective-permute-start.17 = (bf16[9,16,512]{2,1,0:T(8,128)(2,1)S(1)}, bf16[9,16,512]{2,1,0:T(8,128)(2,1)S(1)}, u32[]{:S(2)}, u32[]{:S(2)}) collective-permute-start(bf16[9,16,512]{2,1,0:T(8,128)(2,1)S(1)} %copy-done.39), channel_id=1, source_target_pairs={{16,0},{24,8},{1,16},{9,24},{17,1},{25,9},{0,17},{8,25},{48,32},{5... | collective-permute-start | bytes 442376 | tf_op jit(solution)/shard_map/ppermute | solution.py:1047
  91.1 30.9 %collective-permute-start.20 = (bf16[16,3,16,512]{3,2,1,0:T(8,128)(2,1)S(1)}, bf16[16,3,16,512]{3,2,1,0:T(8,128)(2,1)}, u32[]{:S(2)}, u32[]{:S(2)}) collective-permute-start(bf16[16,3,16,512]{3,2,1,0:T(8,128)(2,1)S(1)} %all-to-all-done.2.refs_2_), channel_id=1, source_target_pairs={{0,8},{8,0},{16,24},{24,16},{32,40},{40,32},{48,56},{56,48},{64,72... | collective-permute-start | bytes 2359304 | tf_op jit(solution)/shard_map/ppermute | solution.py:925
  108.0 14.0 %collective-permute-start.23 = (bf16[16,512]{1,0:T(8,128)(2,1)}, bf16[16,512]{1,0:T(8,128)(2,1)S(1)}, u32[]{:S(2)}, u32[]{:S(2)}) collective-permute-start(bf16[16,512]{1,0:T(8,128)(2,1)} %get-tuple-element.130), channel_id=1, source_target_pairs={{0,7},{1,6},{2,1},{3,0},{4,3},{5,2},{6,5},{7,4},{8,15},{9,14},{10,... | collective-permute-start | bytes 49160 | tf_op jit(solution)/shard_map/ppermute | solution.py:895
  111.2 10.8 %collective-permute-start.21 = (bf16[96,512]{1,0:T(8,128)(2,1)}, bf16[96,512]{1,0:T(8,128)(2,1)S(1)}, u32[]{:S(2)}, u32[]{:S(2)}) collective-permute-start(bf16[96,512]{1,0:T(8,128)(2,1)} %get-tuple-element.128), channel_id=1, source_target_pairs={{0,6},{2,0},{4,2},{6,4},{1,7},{3,1},{5,3},{7,5},{8,14},{10,8},{12,... | collective-permute-start | bytes 294920 | tf_op jit(solution)/shard_map/ppermute | solution.py:893
  118.2 33.0 %all-to-all-start.1 = ((bf16[4,4,9,16,512]{4,3,2,1,0:T(8,128)(2,1)}), bf16[4,4,9,16,512]{4,3,2,1,0:T(8,128)(2,1)S(1)}, u32[]{:S(2)}, u32[]{:S(2)}) async-start(bf16[4,4,9,16,512]{4,3,2,1,0:T(8,128)(2,1)} %shard_map.451), calls=%async_computation.1 | async-start | bytes 4718592 | tf_op jit(solution)/shard_map/all_to_all | solution.py:921
  152.5 10.6 %collective-permute-start.24 = (bf16[16,9,16,512]{3,2,1,0:T(8,128)(2,1)}, bf16[16,9,16,512]{3,2,1,0:T(8,128)(2,1)}, u32[]{:S(2)}, u32[]{:S(2)}) collective-permute-start(bf16[16,9,16,512]{3,2,1,0:T(8,128)(2,1)} %shard_map.453.refs_1_), channel_id=1, source_target_pairs={{0,8},{8,0},{16,24},{24,16},{32,40},{40,32},{48,56},{56,48},{64,72... | collective-permute-start | bytes 7077896 | tf_op jit(solution)/shard_map/ppermute | solution.py:925
  189.5 14.4 %collective-permute-start.29 = (bf16[96,512]{1,0:T(8,128)(2,1)}, bf16[96,512]{1,0:T(8,128)(2,1)S(1)}, u32[]{:S(2)}, u32[]{:S(2)}) collective-permute-start(bf16[96,512]{1,0:T(8,128)(2,1)} %get-tuple-element.142), channel_id=1, source_target_pairs={{0,6},{2,0},{4,2},{6,4},{1,7},{3,1},{5,3},{7,5},{8,14},{10,8},{12,... | collective-permute-start | bytes 294920 | tf_op jit(solution)/shard_map/ppermute | solution.py:893
  190.3 13.6 %collective-permute-start.30 = (bf16[96,512]{1,0:T(8,128)(2,1)}, bf16[96,512]{1,0:T(8,128)(2,1)S(1)}, u32[]{:S(2)}, u32[]{:S(2)}) collective-permute-start(bf16[96,512]{1,0:T(8,128)(2,1)} %get-tuple-element.143), channel_id=1, source_target_pairs={{0,1},{1,0},{2,3},{3,2},{4,5},{5,4},{6,7},{7,6},{8,9},{9,8},{10,11... | collective-permute-start | bytes 294920 | tf_op jit(solution)/shard_map/ppermute | solution.py:894
  193.2 10.7 %collective-permute-start.31 = (bf16[16,512]{1,0:T(8,128)(2,1)}, bf16[16,512]{1,0:T(8,128)(2,1)S(1)}, u32[]{:S(2)}, u32[]{:S(2)}) collective-permute-start(bf16[16,512]{1,0:T(8,128)(2,1)} %get-tuple-element.144), channel_id=1, source_target_pairs={{0,7},{1,6},{2,1},{3,0},{4,3},{5,2},{6,5},{7,4},{8,15},{9,14},{10,... | collective-permute-start | bytes 49160 | tf_op jit(solution)/shard_map/ppermute | solution.py:895
  200.3 38.0 %all-to-all-start.3 = ((bf16[4,4,9,16,512]{4,3,2,1,0:T(8,128)(2,1)}), bf16[4,4,9,16,512]{4,3,2,1,0:T(8,128)(2,1)S(1)}, u32[]{:S(2)}, u32[]{:S(2)}) async-start(bf16[4,4,9,16,512]{4,3,2,1,0:T(8,128)(2,1)} %shard_map.455.refs_0_), calls=%async_computation.3 | async-start | bytes 4718592 | tf_op jit(solution)/shard_map/all_to_all | solution.py:921
  226.6 16.3 %collective-permute-start.34 = (bf16[16,512]{1,0:T(8,128)(2,1)}, bf16[16,512]{1,0:T(8,128)(2,1)S(1)}, u32[]{:S(2)}, u32[]{:S(2)}) collective-permute-start(bf16[16,512]{1,0:T(8,128)(2,1)} %get-tuple-element.155), channel_id=1, source_target_pairs={{0,3},{1,2},{2,5},{3,4},{4,7},{5,6},{6,1},{7,0},{8,11},{9,10},{10,... | collective-permute-start | bytes 49160 | tf_op jit(solution)/shard_map/ppermute | solution.py:895
  230.1 16.2 %collective-permute-start.32 = (bf16[96,512]{1,0:T(8,128)(2,1)}, bf16[96,512]{1,0:T(8,128)(2,1)S(1)}, u32[]{:S(2)}, u32[]{:S(2)}) collective-permute-start(bf16[96,512]{1,0:T(8,128)(2,1)} %get-tuple-element.153), channel_id=1, source_target_pairs={{0,2},{2,4},{4,6},{6,0},{1,3},{3,5},{5,7},{7,1},{8,10},{10,12},{12... | collective-permute-start | bytes 294920 | tf_op jit(solution)/shard_map/ppermute | solution.py:893
  231.4 16.9 %collective-permute-start.33 = (bf16[96,512]{1,0:T(8,128)(2,1)}, bf16[96,512]{1,0:T(8,128)(2,1)S(1)}, u32[]{:S(2)}, u32[]{:S(2)}) collective-permute-start(bf16[96,512]{1,0:T(8,128)(2,1)} %get-tuple-element.154), channel_id=1, source_target_pairs={{0,1},{1,0},{2,3},{3,2},{4,5},{5,4},{6,7},{7,6},{8,9},{9,8},{10,11... | collective-permute-start | bytes 294920 | tf_op jit(solution)/shard_map/ppermute | solution.py:894
  238.1 41.2 %collective-permute-start.36 = (bf16[4,4,3,16,512]{4,3,2,1,0:T(8,128)(2,1)}, bf16[4,4,3,16,512]{4,3,2,1,0:T(8,128)(2,1)S(1)}, u32[]{:S(2)}, u32[]{:S(2)}) collective-permute-start(bf16[4,4,3,16,512]{4,3,2,1,0:T(8,128)(2,1)} %get-tuple-element.162), channel_id=1, source_target_pairs={{0,8},{8,0},{16,24},{24,16},{32,40},{40,32},{48,56},{56,48},{64,72... | collective-permute-start | bytes 2359304 | tf_op jit(solution)/shard_map/ppermute | solution.py:925
  242.3 22.3 %collective-permute-start.37 = (bf16[9,16,512]{2,1,0:T(8,128)(2,1)}, bf16[9,16,512]{2,1,0:T(8,128)(2,1)S(1)}, u32[]{:S(2)}, u32[]{:S(2)}) collective-permute-start(bf16[9,16,512]{2,1,0:T(8,128)(2,1)} %get-tuple-element.163), channel_id=1, source_target_pairs={{17,0},{25,8},{0,16},{8,24},{16,1},{24,9},{1,17},{9,25},{49,32},{5... | collective-permute-start | bytes 442376 | tf_op jit(solution)/shard_map/ppermute | solution.py:1173
  242.9 21.8 %collective-permute-start.38 = (bf16[9,16,512]{2,1,0:T(8,128)(2,1)}, bf16[9,16,512]{2,1,0:T(8,128)(2,1)S(1)}, u32[]{:S(2)}, u32[]{:S(2)}) collective-permute-start(bf16[9,16,512]{2,1,0:T(8,128)(2,1)} %get-tuple-element.164), channel_id=1, source_target_pairs={{1,0},{9,8},{17,16},{25,24},{0,1},{8,9},{16,17},{24,25},{33,32},{4... | collective-permute-start | bytes 442376 | tf_op jit(solution)/shard_map/ppermute | solution.py:1173
  246.3 18.4 %collective-permute-start.39 = (bf16[9,16,512]{2,1,0:T(8,128)(2,1)}, bf16[9,16,512]{2,1,0:T(8,128)(2,1)S(1)}, u32[]{:S(2)}, u32[]{:S(2)}) collective-permute-start(bf16[9,16,512]{2,1,0:T(8,128)(2,1)} %get-tuple-element.165), channel_id=1, source_target_pairs={{16,0},{24,8},{1,16},{9,24},{17,1},{25,9},{0,17},{8,25},{48,32},{5... | collective-permute-start | bytes 442376 | tf_op jit(solution)/shard_map/ppermute | solution.py:1173
  264.6 14.8 %collective-permute-start.35 = (bf16[4,4,8,16,512]{4,3,2,1,0:T(8,128)(2,1)}, bf16[4,4,8,16,512]{4,3,2,1,0:T(8,128)(2,1)S(1)}, u32[]{:S(2)}, u32[]{:S(2)}) collective-permute-start(bf16[4,4,8,16,512]{4,3,2,1,0:T(8,128)(2,1)} %get-tuple-element.161), channel_id=1, source_target_pairs={{0,8},{8,0},{16,24},{24,16},{32,40},{40,32},{48,56},{56,48},{64,72... | collective-permute-start | bytes 6291464 | tf_op jit(solution)/shard_map/ppermute | solution.py:925
  264.8 26.0 %collective-permute-start.42 = (bf16[9,16,512]{2,1,0:T(8,128)(2,1)S(1)}, bf16[9,16,512]{2,1,0:T(8,128)(2,1)S(1)}, u32[]{:S(2)}, u32[]{:S(2)}) collective-permute-start(bf16[9,16,512]{2,1,0:T(8,128)(2,1)S(1)} %add_convert_fusion.refs_0_.refs_1_), channel_id=1, source_target_pairs={{0,6},{2,4},{4,2},{6,0},{1,7},{3,5},{5,3},{7,1},{8,14},{10,12},{12... | collective-permute-start | bytes 442376 | tf_op jit(solution)/shard_map/ppermute | solution.py:947
  266.8 24.0 %collective-permute-start.41 = (bf16[9,16,512]{2,1,0:T(8,128)(2,1)S(1)}, bf16[9,16,512]{2,1,0:T(8,128)(2,1)}, u32[]{:S(2)}, u32[]{:S(2)}) collective-permute-start(bf16[9,16,512]{2,1,0:T(8,128)(2,1)S(1)} %add_convert_fusion.refs_0_.refs_1_), channel_id=1, source_target_pairs={{0,4},{2,6},{4,0},{6,2},{1,5},{3,7},{5,1},{7,3},{8,12},{10,14},{12... | collective-permute-start | bytes 442376 | tf_op jit(solution)/shard_map/ppermute | solution.py:947
  267.3 23.5 %collective-permute-start.40 = (bf16[9,16,512]{2,1,0:T(8,128)(2,1)S(1)}, bf16[9,16,512]{2,1,0:T(8,128)(2,1)}, u32[]{:S(2)}, u32[]{:S(2)}) collective-permute-start(bf16[9,16,512]{2,1,0:T(8,128)(2,1)S(1)} %add_convert_fusion.refs_0_.refs_1_), channel_id=1, source_target_pairs={{0,2},{2,0},{4,6},{6,4},{1,3},{3,1},{5,7},{7,5},{8,10},{10,8},{12,... | collective-permute-start | bytes 442376 | tf_op jit(solution)/shard_map/ppermute | solution.py:947
  285.9 39.5 %all-to-all-start.4 = ((bf16[4,4,11,16,512]{4,3,2,1,0:T(8,128)(2,1)}), bf16[4,4,11,16,512]{4,3,2,1,0:T(8,128)(2,1)S(1)}, u32[]{:S(2)}, u32[]{:S(2)}) async-start(bf16[4,4,11,16,512]{4,3,2,1,0:T(8,128)(2,1)} %shard_map.460.refs_0_), calls=%async_computation.4 | async-start | bytes 5767168 | tf_op jit(solution)/shard_map/all_to_all | solution.py:921
  331.1 28.2 %all-to-all-start.5 = ((bf16[16,5,16,512]{3,2,1,0:T(8,128)(2,1)}), bf16[16,5,16,512]{3,2,1,0:T(8,128)(2,1)S(1)}, u32[]{:S(2)}, u32[]{:S(2)}) async-start(bf16[16,5,16,512]{3,2,1,0:T(8,128)(2,1)} %get-tuple-element.197), calls=%async_computation.5 | async-start | bytes 2621440 | tf_op jit(solution)/shard_map/all_to_all | solution.py:1208
  334.9 22.1 %collective-permute-start.45 = (bf16[11,16,512]{2,1,0:T(8,128)(2,1)S(1)}, bf16[11,16,512]{2,1,0:T(8,128)(2,1)S(1)}, u32[]{:S(2)}, u32[]{:S(2)}) collective-permute-start(bf16[11,16,512]{2,1,0:T(8,128)(2,1)S(1)} %copy-done.35), channel_id=1, source_target_pairs={{17,0},{25,8},{0,16},{8,24},{16,1},{24,9},{1,17},{9,25},{49,32},{5... | collective-permute-start | bytes 540680 | tf_op jit(solution)/shard_map/ppermute | solution.py:1209
  336.8 22.5 %collective-permute-start.46 = (bf16[11,16,512]{2,1,0:T(8,128)(2,1)S(1)}, bf16[11,16,512]{2,1,0:T(8,128)(2,1)S(1)}, u32[]{:S(2)}, u32[]{:S(2)}) collective-permute-start(bf16[11,16,512]{2,1,0:T(8,128)(2,1)S(1)} %copy-done.33), channel_id=1, source_target_pairs={{1,0},{9,8},{17,16},{25,24},{0,1},{8,9},{16,17},{24,25},{33,32},{4... | collective-permute-start | bytes 540680 | tf_op jit(solution)/shard_map/ppermute | solution.py:1209
  339.5 19.8 %collective-permute-start.47 = (bf16[11,16,512]{2,1,0:T(8,128)(2,1)S(1)}, bf16[11,16,512]{2,1,0:T(8,128)(2,1)S(1)}, u32[]{:S(2)}, u32[]{:S(2)}) collective-permute-start(bf16[11,16,512]{2,1,0:T(8,128)(2,1)S(1)} %copy-done.32), channel_id=1, source_target_pairs={{16,0},{24,8},{1,16},{9,24},{17,1},{25,9},{0,17},{8,25},{48,32},{5... | collective-permute-start | bytes 540680 | tf_op jit(solution)/shard_map/ppermute | solution.py:1209
  363.1 18.3 %collective-permute-start.50 = (bf16[15,16,512]{2,1,0:T(8,128)(2,1)}, bf16[15,16,512]{2,1,0:T(8,128)(2,1)S(1)}, u32[]{:S(2)}, u32[]{:S(2)}) collective-permute-start(bf16[15,16,512]{2,1,0:T(8,128)(2,1)} %get-tuple-element.202.refs_9_), channel_id=1, source_target_pairs={{0,6},{2,4},{4,2},{6,0},{1,7},{3,5},{5,3},{7,1},{8,14},{10,12},{12... | collective-permute-start | bytes 737288 | tf_op jit(solution)/shard_map/ppermute | solution.py:947
  365.0 16.4 %collective-permute-start.49 = (bf16[15,16,512]{2,1,0:T(8,128)(2,1)}, bf16[15,16,512]{2,1,0:T(8,128)(2,1)S(1)}, u32[]{:S(2)}, u32[]{:S(2)}) collective-permute-start(bf16[15,16,512]{2,1,0:T(8,128)(2,1)} %get-tuple-element.202.refs_9_), channel_id=1, source_target_pairs={{0,4},{2,6},{4,0},{6,2},{1,5},{3,7},{5,1},{7,3},{8,12},{10,14},{12... | collective-permute-start | bytes 737288 | tf_op jit(solution)/shard_map/ppermute | solution.py:947
  366.1 15.4 %collective-permute-start.48 = (bf16[15,16,512]{2,1,0:T(8,128)(2,1)}, bf16[15,16,512]{2,1,0:T(8,128)(2,1)S(1)}, u32[]{:S(2)}, u32[]{:S(2)}) collective-permute-start(bf16[15,16,512]{2,1,0:T(8,128)(2,1)} %get-tuple-element.202.refs_9_), channel_id=1, source_target_pairs={{0,2},{2,0},{4,6},{6,4},{1,3},{3,1},{5,7},{7,5},{8,10},{10,8},{12,... | collective-permute-start | bytes 737288 | tf_op jit(solution)/shard_map/ppermute | solution.py:947
  373.7 20.3 %all-to-all-start.6 = ((f32[64,16,128]{2,1,0:T(8,128)}), f32[64,16,128]{2,1,0:T(8,128)S(1)}, u32[]{:S(2)}, u32[]{:S(2)}) async-start(f32[64,16,128]{2,1,0:T(8,128)} %get-tuple-element.215), calls=%async_computation.6 | async-start | bytes 1048576 | tf_op jit(solution)/shard_map/all_to_all | solution.py:1212
  (74 other events, 442.3 us)
